TPU v7x, 32 devices: a whole 2x2x4 slice. The times are simulated.
32 devices in a mesh: row: 4 (over z), col: 8 (over y, x, core).
Axes of the slice: x: 2, y: 2, z: 4, core: 2. Of those that a mesh axis runs over, the one named last changes fastest.
Arguments:
- queries: bfloat16 [4, 1024, 512], P('row', 'col'), may hold values from -6 to 6
- keys: bfloat16 [8, 512, 512], P('col', 'row'), may hold values from -6 to 6
- values: bfloat16 [8, 512, 512], P('col', 'row'), may hold values from -6 to 6
- outputs: bfloat16 [4, 1024, 512], P('row', 'col'), may hold values from -2 to 2
- grad_out: bfloat16 [4, 1024, 512], P('row', 'col'), may hold values from -48 to 48
- lse: float32 [4, 8, 1024], P('row'), may hold values from 7 to 9.5
- tile_slot: int32 [4, 8, 24], P('row', 'col'), may hold values from 0 to 31, as said below
- tile_live: int32 [4, 8], P('row', 'col'), may hold values from 1 to 24, as said below
- tile_bits: int32 [4, 8, 24, 8, 128], P('row', 'col'), may hold values from 0 to 65535, as said below
Outputs:
- grad_queries: bfloat16 [4, 1024, 512], P('row', 'col')
- grad_keys: bfloat16 [8, 512, 512], P('col', 'row')
- grad_values: bfloat16 [8, 512, 512], P('col', 'row')
Inputs may be any that keep to these rules, and one draw needn't show every extreme that they name: `tile_slot`: the 24 entries of one pair of blocks are distinct slots. `tile_live`: some pair of blocks has all 24 entries live. `tile_bits`: each word holds 16 edge bits in its low bits.
All inputs are finite; a program needn't handle non-finite values.
Results may differ from a plain program's by a relative error of at most 0.02.
Values may be sent and summed in bfloat16 or wider, within the bound.
No kernel may reach another device: no remote copies, remote signals or barrier semaphores. Data moves between devices by JAX's collectives and lax.ppermute only.
A program may use at most 64 MiB of HBM per device.

v0:
```python
import functools

import jax
import jax.numpy as jnp
from jax import lax
from jax.experimental import pallas as pl
from jax.experimental.pallas import tpu as pltpu
from jax.sharding import Mesh
from jax.sharding import PartitionSpec as P


F32 = jnp.float32
BF16 = jnp.bfloat16
I32 = jnp.int32
LANES = 128
PAD = 16
QUARTERS = 4
LOG2E = 1.4426950408889634
NT = (((1,), (1,)), ((), ()))
NN = (((1,), (0,)), ((), ()))
LARGE = pltpu.CompilerParams(vmem_limit_bytes=58 * 1024 * 1024)
MEDIUM = pltpu.CompilerParams(vmem_limit_bytes=28 * 1024 * 1024)
SMALL = pltpu.CompilerParams(vmem_limit_bytes=12 * 1024 * 1024)
VMEM = pl.BlockSpec(memory_space=pltpu.VMEM)
SMEM = pl.BlockSpec(memory_space=pltpu.SMEM)
HBM = pl.BlockSpec(memory_space=pl.ANY)


def lanes_of(quarter):
    return pl.ds(pl.multiple_of(quarter * LANES, LANES), LANES)


def pack_kernel(
    heads, place_ref, q_hbm, g_hbm, o_hbm, k_hbm, v_hbm, bits_hbm, slot_ref, live_ref, *refs
):
    qg_refs, refs = refs[:QUARTERS], refs[QUARTERS:]
    kv_refs, refs = refs[:QUARTERS], refs[QUARTERS:]
    packed_ref, q_ref, g_ref, o_ref, k_ref, v_ref, bits_ref, delta_ref, sems = refs
    arrays = (
        (q_hbm, q_ref), (g_hbm, g_ref), (o_hbm, o_ref),
        (k_hbm, k_ref), (v_hbm, v_ref), (bits_hbm, bits_ref),
    )
    copies = [pltpu.make_async_copy(a, b, sems.at[i]) for i, (a, b) in enumerate(arrays)]
    for copy in copies:
        copy.start()
    rows, width = q_ref.shape[1:]
    krows = k_ref.shape[1]
    head_dim = width // heads
    local = heads // QUARTERS
    capacity = bits_ref.shape[2]
    quarter = place_ref[0] % 2 * 2 + place_ref[2]
    feature = lax.broadcasted_iota(I32, (QUARTERS * PAD, width), 1)
    line = lax.broadcasted_iota(I32, (QUARTERS * PAD, width), 0)
    wanted = jnp.where(line % PAD < local, line // PAD * local + line % PAD, -1)
    pick = (feature // head_dim == wanted).astype(F32)
    for copy in copies:
        copy.wait()
    product = g_ref[0].astype(F32) * o_ref[0].astype(F32)
    delta = lax.dot_general(
        pick, product, NT, precision=lax.Precision.HIGHEST, preferred_element_type=F32
    ).astype(BF16)
    for index in range(QUARTERS):
        delta_ref[index] = delta[index * PAD : (index + 1) * PAD]
    for step in range(QUARTERS):
        target = quarter ^ step
        lanes = lanes_of(target)
        qg_refs[step][:rows] = q_ref[0, :, lanes]
        qg_refs[step][rows : 2 * rows] = g_ref[0, :, lanes]
        if rows < LANES:
            qg_refs[step][2 * rows :] = jnp.zeros((PAD, LANES), BF16)
        qg_refs[step][2 * rows :, :rows] = delta_ref[target]
        kv_refs[step][:krows] = k_ref[0, :, lanes]
        kv_refs[step][krows:] = v_ref[0, :, lanes]
    for entry in range(capacity):
        words = bits_ref[0, 0, entry]
        span = slice(entry % 2 * 4, entry % 2 * 4 + 4)
        packed_ref[entry // 2, span] = words[:4] | lax.shift_left(words[4:], I32(16))
    packed_ref[capacity // 2] = jnp.zeros((8, LANES), I32)
    packed_ref[capacity // 2, 0:1, 0:capacity] = slot_ref[0]
    packed_ref[capacity // 2, 1:2, 0:1] = live_ref[...]


def join_kernel(place_ref, *refs):
    out = refs[-1]
    quarter = place_ref[0] % 2 * 2 + place_ref[2]
    for step in range(QUARTERS):
        out[quarter ^ step] = refs[step][...]


def pair_kernel(sizes, place_ref, *refs):
    head_dim, tile, capacity, chips, key_sources = sizes
    qg_refs, refs = refs[:chips], refs[chips:]
    kv_refs, refs = refs[:key_sources], refs[key_sources:]
    bits_refs, refs = refs[:QUARTERS], refs[QUARTERS:]
    lse_refs, refs = refs[:2], refs[2:]
    dq_refs, refs = refs[:chips], refs[chips:]
    dkv_refs, refs = refs[:key_sources], refs[key_sources:]
    (q2_scr, g2_scr, k_scr, v_scr, k2t_scr, lse_scr, delta_scr, dqt_scr, dk_scr, dv_scr, dq_scr,
     info, sems) = refs
    rows = (qg_refs[0].shape[1] - PAD) // 2
    krows = kv_refs[0].shape[0] // 2
    query_tiles = q2_scr.shape[1]
    key_tiles = k_scr.shape[1]
    scaling = float(head_dim) ** -0.5
    row, chip, core = place_ref[0], place_ref[1], place_ref[2]
    side = row % 2
    quarter = side * 2 + core
    line = row * 2 + core

    copies = [
        pltpu.make_async_copy(ref.at[capacity // 2], info.at[i], sems.at[i])
        for i, ref in enumerate(bits_refs)
    ]
    for copy in copies:
        copy.start()

    for step, ref in enumerate(lse_refs):
        every = ref[0] * LOG2E
        own = every[:2]
        for index in range(1, QUARTERS):
            own = jnp.where(quarter == index, every[2 * index : 2 * index + 2], own)
        for u in range(query_tiles):
            lse_scr[side ^ step, u] = own[:, u * tile : (u + 1) * tile]
    low = lax.broadcasted_iota(I32, (rows, LANES), 1) < head_dim
    none = jnp.zeros((rows, LANES), BF16)
    for step in range(chips):
        for index in range(QUARTERS):
            source = (chip ^ step) * 2 + index % 2
            start = source * rows
            u = start // tile
            inner = pl.multiple_of(start % tile, rows)
            block = index // 2
            for scr, part in ((q2_scr, 0), (g2_scr, 1)):
                piece = qg_refs[step][index, part * rows : (part + 1) * rows]
                scr[block, u, 0, pl.ds(inner, rows)] = jnp.where(low, piece, none)
                scr[block, u, 1, pl.ds(inner, rows)] = jnp.where(low, none, piece)
            delta = qg_refs[step][index, 2 * rows :, :rows].astype(F32)
            if rows == tile:
                delta_scr[block, u] = delta
            else:
                for part in range(tile // rows):
                    @pl.when(source % (tile // rows) == part)
                    def _(part=part, delta=delta, u=u, block=block):
                        delta_scr[block, u, :, part * rows : (part + 1) * rows] = delta
    for step in range(key_sources):
        source = line ^ step
        start = source // 2 * krows
        inner = pl.multiple_of(start % tile, krows)
        k_scr[source % 2, start // tile, pl.ds(inner, krows)] = kv_refs[step][:krows]
        v_scr[source % 2, start // tile, pl.ds(inner, krows)] = kv_refs[step][krows:]
    low_row = lax.broadcasted_iota(I32, (LANES, tile), 0) < head_dim
    none_t = jnp.zeros((LANES, tile), BF16)
    for block in range(2):
        for w in range(key_tiles):
            flipped = k_scr[block, w].T
            k2t_scr[block, w] = jnp.concatenate(
                [jnp.where(low_row, flipped, none_t), jnp.where(low_row, none_t, flipped)], axis=1
            )
    dqt_scr[...] = jnp.zeros_like(dqt_scr)
    dk_scr[...] = jnp.zeros_like(dk_scr)
    dv_scr[...] = jnp.zeros_like(dv_scr)
    place_in = lax.broadcasted_iota(I32, (2, 4, 16, tile), 2)
    upper = lax.broadcasted_iota(I32, (2, 4, 16, tile), 0)
    bit = lax.shift_left(I32(1), place_in + 16 * upper).reshape(tile, tile)
    for copy in copies:
        copy.wait()

    for step in range(QUARTERS):
        qb = side ^ (step // 2)
        kb = core ^ (step % 2)
        live = info[step, 1, 0]
        bits_ref = bits_refs[step]

        def two_tiles(index, _, step=step, qb=qb, kb=kb, live=live, bits_ref=bits_ref):
            both = bits_ref[index]
            second = jnp.where(index * 2 + 1 < live, I32(-1), I32(0))
            work = []
            for part in range(2):
                slot = info[step, 0, index * 2 + part]
                u = slot // key_tiles
                w = slot % key_tiles
                words = both[part * 4 : part * 4 + 4]
                if part:
                    words = words & second
                words = jnp.broadcast_to(words[:, None, :], (4, 16, tile)).reshape(64, tile)
                edge = (jnp.concatenate([words, words], axis=0) & bit) != 0
                q2 = q2_scr[qb, u].reshape(2 * tile, LANES)
                g2 = g2_scr[qb, u].reshape(2 * tile, LANES)
                scores = lax.dot_general(k_scr[kb, w], q2, NT, preferred_element_type=F32)
                grad_prob = lax.dot_general(v_scr[kb, w], g2, NT, preferred_element_type=F32)
                work.append((u, w, edge, q2, g2, scores, grad_prob))
            done = []
            for u, w, edge, q2, g2, scores, grad_prob in work:
                lse_tile = lse_scr[qb, u]
                delta_tile = delta_scr[qb, u]
                probs, grads = [], []
                for h in range(2):
                    s = scores[:, h * tile : (h + 1) * tile]
                    gp = grad_prob[:, h * tile : (h + 1) * tile]
                    p = jnp.exp2(s * (scaling * LOG2E) - lse_tile[h : h + 1])
                    p = jnp.where(edge, p, 0.0)
                    ds = p * (gp - delta_tile[h : h + 1])
                    probs.append(p.astype(BF16))
                    grads.append(ds.astype(BF16))
                done.append((
                    lax.dot_general(
                        jnp.concatenate(probs, axis=1), g2, NN, preferred_element_type=F32
                    ),
                    lax.dot_general(
                        jnp.concatenate(grads, axis=1), q2, NN, preferred_element_type=F32
                    ),
                    lax.dot_general(
                        k2t_scr[kb, w], jnp.concatenate(grads, axis=0), NN,
                        preferred_element_type=F32,
                    ),
                ))
            for (u, w, *_), (dv, dk, dqt) in zip(work, done):
                dv_scr[kb, w] += dv
                dk_scr[kb, w] += dk
                dqt_scr[qb, u] += dqt
            return 0

        lax.fori_loop(0, (live + 1) // 2, two_tiles, 0)

    for step in range(key_sources):
        target = line ^ step
        start = target // 2 * krows
        inner = pl.multiple_of(start % tile, krows)
        dk = dk_scr[target % 2, start // tile, pl.ds(inner, krows)] * scaling
        dv = dv_scr[target % 2, start // tile, pl.ds(inner, krows)]
        dkv_refs[step][:krows] = dk.astype(BF16)
        dkv_refs[step][krows:] = dv.astype(BF16)
    for block in range(2):
        for u in range(query_tiles):
            dq_scr[block, u * tile : (u + 1) * tile] = (dqt_scr[block, u] * scaling).astype(BF16).T
    for step in range(chips):
        for index in range(QUARTERS):
            start = pl.multiple_of(((chip ^ step) * 2 + index % 2) * rows, rows)
            dq_refs[step][index] = dq_scr[index // 2, pl.ds(start, rows)]


def query_sum_kernel(chips, place_ref, *refs):
    parts, outs = refs[:chips], refs[chips:]
    quarter = place_ref[0] % 2 * 2 + place_ref[2]
    for step in range(QUARTERS):
        target = quarter ^ step
        total = parts[0][target].astype(F32)
        for part in parts[1:]:
            total += part[target].astype(F32)
        outs[step][...] = total.astype(BF16)


def finish_kernel(key_sources, place_ref, *refs):
    dq_refs, refs = refs[:QUARTERS], refs[QUARTERS:]
    dkv_refs, refs = refs[:key_sources], refs[key_sources:]
    dq_out, dk_out, dv_out = refs
    krows = dkv_refs[0].shape[0] // 2
    quarter = place_ref[0] % 2 * 2 + place_ref[2]
    for step in range(QUARTERS):
        lanes = lanes_of(quarter ^ step)
        dq_out[0, :, lanes] = dq_refs[step][...]
        total = dkv_refs[step][...].astype(F32)
        for other in range(step + QUARTERS, key_sources, QUARTERS):
            total += dkv_refs[other][...].astype(F32)
        total = total.astype(BF16)
        dk_out[0, :, lanes] = total[:krows]
        dv_out[0, :, lanes] = total[krows:]


def send(block, axes, count, step):
    return lax.ppermute(block, axes, [(place, place ^ step) for place in range(count)])


def body(sizes, queries, keys, values, outputs, grad_out, lse, tile_slot, tile_live, tile_bits):
    row_count, chips, cores = sizes
    heads = lse.shape[1]
    width = queries.shape[2]
    head_dim = width // heads
    tile = tile_bits.shape[4]
    capacity = tile_slot.shape[2]
    rows = queries.shape[1]
    krows = keys.shape[1]
    key_sources = row_count * cores
    query_tiles = lse.shape[2] // tile
    key_tiles = row_count * krows // tile
    line = ("row", "core")
    place = jnp.stack([lax.axis_index(name) for name in ("row", "chip", "core")]).astype(I32)

    qg_shape = jax.ShapeDtypeStruct((2 * rows + PAD, LANES), BF16)
    kv_shape = jax.ShapeDtypeStruct((2 * krows, LANES), BF16)
    packed_shape = jax.ShapeDtypeStruct((capacity // 2 + 1, 8, LANES), I32)
    packed = pl.pallas_call(
        functools.partial(pack_kernel, heads),
        out_shape=(qg_shape,) * QUARTERS + (kv_shape,) * QUARTERS + (packed_shape,),
        in_specs=[SMEM] + [HBM] * 6 + [VMEM] * 2,
        out_specs=(VMEM,) * (2 * QUARTERS + 1),
        scratch_shapes=[
            pltpu.VMEM(queries.shape, BF16),
            pltpu.VMEM(queries.shape, BF16),
            pltpu.VMEM(queries.shape, BF16),
            pltpu.VMEM(keys.shape, BF16),
            pltpu.VMEM(keys.shape, BF16),
            pltpu.VMEM(tile_bits.shape, I32),
            pltpu.VMEM((QUARTERS, PAD, rows), BF16),
            pltpu.SemaphoreType.DMA((6,)),
        ],
        compiler_params=LARGE,
        name="pack",
    )(place, queries, grad_out, outputs, keys, values, tile_bits, tile_slot, tile_live)
    qg_own, kv_own, bits_own = packed[:QUARTERS], packed[QUARTERS : 2 * QUARTERS], packed[-1]

    qg_group = [qg_own[0]] + [
        send(qg_own[step], line, key_sources, step) for step in range(1, QUARTERS)
    ]
    bits = [bits_own] + [send(bits_own, line, key_sources, step) for step in range(1, QUARTERS)]
    lse_other = send(lse, "row", row_count, 1)
    joined = pl.pallas_call(
        join_kernel,
        out_shape=jax.ShapeDtypeStruct((QUARTERS,) + qg_shape.shape, BF16),
        in_specs=[SMEM] + [VMEM] * QUARTERS,
        out_specs=VMEM,
        compiler_params=SMALL,
        name="join",
    )(place, *qg_group)
    qg = [joined] + [send(joined, "chip", chips, step) for step in range(1, chips)]
    kv = [kv_own[0]] + [
        send(kv_own[step % QUARTERS], line, key_sources, step) for step in range(1, key_sources)
    ]

    dq_shape = jax.ShapeDtypeStruct((QUARTERS, rows, LANES), BF16)
    parts = pl.pallas_call(
        functools.partial(pair_kernel, (head_dim, tile, capacity, chips, key_sources)),
        out_shape=(dq_shape,) * chips + (kv_shape,) * key_sources,
        in_specs=[SMEM] + [VMEM] * (chips + key_sources + QUARTERS + 2),
        out_specs=(VMEM,) * (chips + key_sources),
        scratch_shapes=[
            pltpu.VMEM((2, query_tiles, 2, tile, LANES), BF16),
            pltpu.VMEM((2, query_tiles, 2, tile, LANES), BF16),
            pltpu.VMEM((2, key_tiles, tile, LANES), BF16),
            pltpu.VMEM((2, key_tiles, tile, LANES), BF16),
            pltpu.VMEM((2, key_tiles, LANES, 2 * tile), BF16),
            pltpu.VMEM((2, query_tiles, 2, tile), F32),
            pltpu.VMEM((2, query_tiles, PAD, tile), F32),
            pltpu.VMEM((2, query_tiles, LANES, tile), F32),
            pltpu.VMEM((2, key_tiles, tile, LANES), F32),
            pltpu.VMEM((2, key_tiles, tile, LANES), F32),
            pltpu.VMEM((2, query_tiles * tile, LANES), BF16),
            pltpu.SMEM((QUARTERS, 8, LANES), I32),
            pltpu.SemaphoreType.DMA((QUARTERS,)),
        ],
        compiler_params=MEDIUM,
        name="pair",
    )(place, *qg, *kv, *bits, lse, lse_other)

    dq_parts, dkv_parts = parts[:chips], parts[chips:]
    dq_parts = [dq_parts[0]] + [
        send(dq_parts[step], "chip", chips, step) for step in range(1, chips)
    ]
    dkv = [dkv_parts[0]] + [
        send(dkv_parts[step], line, key_sources, step) for step in range(1, key_sources)
    ]
    dq = pl.pallas_call(
        functools.partial(query_sum_kernel, chips),
        out_shape=(jax.ShapeDtypeStruct((rows, LANES), BF16),) * QUARTERS,
        in_specs=[SMEM] + [VMEM] * chips,
        out_specs=(VMEM,) * QUARTERS,
        compiler_params=SMALL,
        name="query_sum",
    )(place, *dq_parts)
    dq = [dq[0]] + [send(dq[step], line, key_sources, step) for step in range(1, QUARTERS)]
    return pl.pallas_call(
        functools.partial(finish_kernel, key_sources),
        out_shape=(
            jax.ShapeDtypeStruct((1, rows, width), BF16),
            jax.ShapeDtypeStruct((1, krows, width), BF16),
            jax.ShapeDtypeStruct((1, krows, width), BF16),
        ),
        in_specs=[SMEM] + [VMEM] * (QUARTERS + key_sources),
        out_specs=(VMEM, VMEM, VMEM),
        compiler_params=SMALL,
        name="finish",
    )(place, *dq, *dkv)


def solution(mesh):
    row_count, columns = mesh.devices.shape
    cores = 2
    chips = columns // cores
    fine = Mesh(mesh.devices.reshape(row_count, chips, cores), ("row", "chip", "core"))
    col = ("chip", "core")
    in_specs = (
        P("row", col, None),
        P(col, "row", None),
        P(col, "row", None),
        P("row", col, None),
        P("row", col, None),
        P("row", None, None),
        P("row", col, None),
        P("row", col),
        P("row", col, None, None, None),
    )
    out_specs = (P("row", col, None), P(col, "row", None), P(col, "row", None))
    return jax.shard_map(
        functools.partial(body, (row_count, chips, cores)),
        mesh=fine, in_specs=in_specs, out_specs=out_specs, check_vma=False,
    )
```

profile of v0, /device:TPU:0, one launch (start us, length us, event | category | flops | bytes accessed | tf_op | source)
XLA Modules:
  0.0 77.9 jit_solution(16167251171200422111)
XLA Ops:
  1.3 0.6 pad_add_fusion.place_ref
  1.9 3.2 %pack.1 = (bf16[272,128]{1,0:T(8,128)(2,1)}, bf16[272,128]{1,0:T(8,128)(2,1)}, bf16[272,128]{1,0:T(8,128)(2,1)}, bf16[272,128]{1,0:T(8,128)(2,1)}, bf16[256,128]...) custom-call(s32[3]{0:T(128)} %pad_add_fusion.place_ref, ...), custom_call_target="tpu_custom_call" | custom-call | tf_op jit(solution)/shard_map/pack/pallas_call | solution.py:292
  5.1 0.5 collective-permute-start
  5.6 2.7 %collective-permute-start.1 = (bf16[272,128]{1,0:T(8,128)(2,1)}, bf16[272,128]{1,0:T(8,128)(2,1)S(1)}, u32[]{:S(2)}, u32[]{:S(2)}) collective-permute-start(bf16[272,128]{1,0:T(8,128)(2,1)} %get-tuple-element.30), channel_id=1, source_target_pairs={{0,8},{1,9},{8,0},{9,1},{16,24},{17,25},{24,16},{25,17},{2,10},{3,... | collective-permute-start | bytes 208904 | tf_op jit(solution)/shard_map/ppermute | solution.py:271
  8.2 0.1 collective-permute-start.2
  8.3 1.7 %collective-permute-start.15 = (s32[13,8,128]{2,1,0:T(8,128)}, s32[13,8,128]{2,1,0:T(8,128)S(1)}, u32[]{:S(2)}, u32[]{:S(2)}) collective-permute-start(s32[13,8,128]{2,1,0:T(8,128)} %get-tuple-element.36.refs_12_), channel_id=1, source_target_pairs={{0,9},{1,8},{8,1},{9,0},{16,25},{17,24},{24,17},{25,16},{2,11},{3,... | collective-permute-start | bytes 159752 | tf_op jit(solution)/shard_map/ppermute | solution.py:271
  10.0 0.1 collective-permute-start.16
  10.1 0.0 collective-permute-done.refs_1_
  10.1 1.9 %collective-permute-start.14 = (s32[13,8,128]{2,1,0:T(8,128)}, s32[13,8,128]{2,1,0:T(8,128)S(1)}, u32[]{:S(2)}, u32[]{:S(2)}) collective-permute-start(s32[13,8,128]{2,1,0:T(8,128)} %get-tuple-element.36.refs_12_), channel_id=1, source_target_pairs={{0,8},{1,9},{8,0},{9,1},{16,24},{17,25},{24,16},{25,17},{2,10},{3,... | collective-permute-start | bytes 159752 | tf_op jit(solution)/shard_map/ppermute | solution.py:271
  12.0 0.0 collective-permute-done.1.refs_2_
  12.0 0.6 collective-permute-done.2.refs_3_
  12.7 0.9 %copy-done = bf16[272,128]{1,0:T(8,128)(2,1)S(1)} copy-done((bf16[272,128]{1,0:T(8,128)(2,1)S(1)}, bf16[272,128]{1,0:T(8,128)(2,1)}, u32[]{:S(2)}) %copy-start) | copy-done | bytes 69656
  13.6 0.6 join.1.refs_0_
  14.2 2.5 %collective-permute-start.5 = (bf16[4,272,128]{2,1,0:T(8,128)(2,1)S(1)}, bf16[4,272,128]{2,1,0:T(8,128)(2,1)S(1)}, u32[]{:S(2)}, u32[]{:S(2)}) collective-permute-start(bf16[4,272,128]{2,1,0:T(8,128)(2,1)S(1)} %join.1.refs_0_), channel_id=1, source_target_pairs={{0,6},{2,4},{4,2},{6,0},{1,7},{3,5},{5,3},{7,1},{8,14},{10,12},{12... | collective-permute-start | bytes 835592 | tf_op jit(solution)/shard_map/ppermute | solution.py:271
  16.7 0.5 collective-permute-start.4
  17.2 0.0 collective-permute-done.16.refs_17_
  17.2 0.5 collective-permute-start.3
  17.7 0.0 collective-permute-done.15.refs_15_
  17.7 2.6 %collective-permute-start.9 = (bf16[256,128]{1,0:T(8,128)(2,1)S(1)}, bf16[256,128]{1,0:T(8,128)(2,1)S(1)}, u32[]{:S(2)}, u32[]{:S(2)}) collective-permute-start(bf16[256,128]{1,0:T(8,128)(2,1)S(1)} %copy-done.1), channel_id=1, source_target_pairs={{0,16},{1,17},{8,24},{9,25},{16,0},{17,1},{24,8},{25,9},{2,18},{3,... | collective-permute-start | bytes 196616 | tf_op jit(solution)/shard_map/ppermute | solution.py:271
  20.3 0.0 collective-permute-done.14.refs_14_
  20.3 0.0 collective-permute-start.13
  20.3 1.2 %collective-permute-done.13.refs_13_ = s32[13,8,128]{2,1,0:T(8,128)S(1)} collective-permute-done((s32[13,8,128]{2,1,0:T(8,128)S(1)}, s32[13,8,128]{2,1,0:T(8,128)S(1)}, u32[]{:S(2)}, u32[]{:S(2)}) %collective-permute-start.13) | collective-permute-done | bytes 53280 | tf_op jit(solution)/shard_map/ppermute | solution.py:271
  21.6 0.1 collective-permute-start.10
  21.7 2.6 %collective-permute-done.9.refs_8_ = bf16[256,128]{1,0:T(8,128)(2,1)S(1)} collective-permute-done((bf16[256,128]{1,0:T(8,128)(2,1)S(1)}, bf16[256,128]{1,0:T(8,128)(2,1)S(1)}, u32[]{:S(2)}, u32[]{:S(2)}) %collective-permute-start.9) | collective-permute-done | bytes 65568 | tf_op jit(solution)/shard_map/ppermute | solution.py:271
  24.3 0.0 collective-permute-start.6
  24.3 3.6 %collective-permute-done.10.refs_9_ = bf16[256,128]{1,0:T(8,128)(2,1)S(1)} collective-permute-done((bf16[256,128]{1,0:T(8,128)(2,1)S(1)}, bf16[256,128]{1,0:T(8,128)(2,1)S(1)}, u32[]{:S(2)}, u32[]{:S(2)}) %collective-permute-start.10) | collective-permute-done | bytes 65568 | tf_op jit(solution)/shard_map/ppermute | solution.py:271
  27.9 1.9 %collective-permute-start.11 = (bf16[256,128]{1,0:T(8,128)(2,1)S(1)}, bf16[256,128]{1,0:T(8,128)(2,1)S(1)}, u32[]{:S(2)}, u32[]{:S(2)}) collective-permute-start(bf16[256,128]{1,0:T(8,128)(2,1)S(1)} %copy-done.6), channel_id=1, source_target_pairs={{0,24},{1,25},{8,16},{9,17},{16,8},{17,9},{24,0},{25,1},{2,26},{3,... | collective-permute-start | bytes 196616 | tf_op jit(solution)/shard_map/ppermute | solution.py:271
  29.8 0.0 collective-permute-done.6.refs_5_
  29.8 0.0 collective-permute-start.7
  29.8 4.9 %collective-permute-done.11.refs_10_ = bf16[256,128]{1,0:T(8,128)(2,1)S(1)} collective-permute-done((bf16[256,128]{1,0:T(8,128)(2,1)S(1)}, bf16[256,128]{1,0:T(8,128)(2,1)S(1)}, u32[]{:S(2)}, u32[]{:S(2)}) %collective-permute-start.11) | collective-permute-done | bytes 65568 | tf_op jit(solution)/shard_map/ppermute | solution.py:271
  34.7 0.0 collective-permute-start.12
  34.7 0.4 collective-permute-done.7.refs_6_
  35.1 0.0 collective-permute-start.8
  35.1 5.2 %collective-permute-done.12.refs_11_ = bf16[256,128]{1,0:T(8,128)(2,1)S(1)} collective-permute-done((bf16[256,128]{1,0:T(8,128)(2,1)S(1)}, bf16[256,128]{1,0:T(8,128)(2,1)S(1)}, u32[]{:S(2)}, u32[]{:S(2)}) %collective-permute-start.12) | collective-permute-done | bytes 65568 | tf_op jit(solution)/shard_map/ppermute | solution.py:271
  40.2 0.0 collective-permute-done.8.refs_7_
  40.2 0.0 collective-permute-done.5.refs_3_
  40.2 0.0 collective-permute-done.4.refs_2_
  40.2 0.0 collective-permute-done.3.refs_1_
  40.3 7.9 %pair.1 = (bf16[4,128,128]{2,1,0:T(8,128)(2,1)S(1)}, bf16[4,128,128]{2,1,0:T(8,128)(2,1)S(1)}, bf16[4,128,128]{2,1,0:T(8,128)(2,1)S(1)}, bf16[4,128,128]{2,1,0:T...) custom-call(s32[3]{0:T(128)S(1)} %copy-done.4, ...), custom_call_target="tpu_custom_call" | custom-call | tf_op jit(solution)/shard_map/pair/pallas_call | solution.py:331
  48.2 0.3 collective-permute-start.17
  48.5 5.1 %collective-permute-start.18 = (bf16[4,128,128]{2,1,0:T(8,128)(2,1)S(1)}, bf16[4,128,128]{2,1,0:T(8,128)(2,1)S(1)}, u32[]{:S(2)}, u32[]{:S(2)}) collective-permute-start(bf16[4,128,128]{2,1,0:T(8,128)(2,1)S(1)} %get-tuple-element.39), channel_id=1, source_target_pairs={{0,4},{2,6},{4,0},{6,2},{1,5},{3,7},{5,1},{7,3},{8,12},{10,14},{12... | collective-permute-start | bytes 393224 | tf_op jit(solution)/shard_map/ppermute | solution.py:271
  53.5 1.4 %collective-permute-start.19 = (bf16[4,128,128]{2,1,0:T(8,128)(2,1)S(1)}, bf16[4,128,128]{2,1,0:T(8,128)(2,1)S(1)}, u32[]{:S(2)}, u32[]{:S(2)}) collective-permute-start(bf16[4,128,128]{2,1,0:T(8,128)(2,1)S(1)} %get-tuple-element.40), channel_id=1, source_target_pairs={{0,6},{2,4},{4,2},{6,0},{1,7},{3,5},{5,3},{7,1},{8,14},{10,12},{12... | collective-permute-start | bytes 393224 | tf_op jit(solution)/shard_map/ppermute | solution.py:271
  54.9 0.0 collective-permute-start.23
  54.9 0.8 %collective-permute-start.24 = (bf16[256,128]{1,0:T(8,128)(2,1)S(1)}, bf16[256,128]{1,0:T(8,128)(2,1)S(1)}, u32[]{:S(2)}, u32[]{:S(2)}) collective-permute-start(bf16[256,128]{1,0:T(8,128)(2,1)S(1)} %get-tuple-element.47), channel_id=1, source_target_pairs={{0,8},{1,9},{8,0},{9,1},{16,24},{17,25},{24,16},{25,17},{2,10},{3,... | collective-permute-start | bytes 196616 | tf_op jit(solution)/shard_map/ppermute | solution.py:271
  55.7 0.5 collective-permute-done.23.refs_5_
  56.2 0.6 collective-permute-start.25
  56.8 3.0 %collective-permute-done.24.refs_6_ = bf16[256,128]{1,0:T(8,128)(2,1)S(1)} collective-permute-done((bf16[256,128]{1,0:T(8,128)(2,1)S(1)}, bf16[256,128]{1,0:T(8,128)(2,1)S(1)}, u32[]{:S(2)}, u32[]{:S(2)}) %collective-permute-start.24) | collective-permute-done | bytes 65568 | tf_op jit(solution)/shard_map/ppermute | solution.py:271
  59.7 4.1 %collective-permute-start.26 = (bf16[256,128]{1,0:T(8,128)(2,1)S(1)}, bf16[256,128]{1,0:T(8,128)(2,1)S(1)}, u32[]{:S(2)}, u32[]{:S(2)}) collective-permute-start(bf16[256,128]{1,0:T(8,128)(2,1)S(1)} %get-tuple-element.49), channel_id=1, source_target_pairs={{0,16},{1,17},{8,24},{9,25},{16,0},{17,1},{24,8},{25,9},{2,18},{3,... | collective-permute-start | bytes 196616 | tf_op jit(solution)/shard_map/ppermute | solution.py:271
  63.8 0.0 collective-permute-done.17.refs_1_
  63.8 0.0 collective-permute-start.27
  63.8 2.5 %collective-permute-start.28 = (bf16[256,128]{1,0:T(8,128)(2,1)S(1)}, bf16[256,128]{1,0:T(8,128)(2,1)S(1)}, u32[]{:S(2)}, u32[]{:S(2)}) collective-permute-start(bf16[256,128]{1,0:T(8,128)(2,1)S(1)} %get-tuple-element.51), channel_id=1, source_target_pairs={{0,24},{1,25},{8,16},{9,17},{16,8},{17,9},{24,0},{25,1},{2,26},{3,... | collective-permute-start | bytes 196616 | tf_op jit(solution)/shard_map/ppermute | solution.py:271
  66.3 0.0 collective-permute-done.19.refs_3_
  66.3 1.1 %collective-permute-start.29 = (bf16[256,128]{1,0:T(8,128)(2,1)S(1)}, bf16[256,128]{1,0:T(8,128)(2,1)S(1)}, u32[]{:S(2)}, u32[]{:S(2)}) collective-permute-start(bf16[256,128]{1,0:T(8,128)(2,1)S(1)} %get-tuple-element.52), channel_id=1, source_target_pairs={{0,25},{1,24},{8,17},{9,16},{16,9},{17,8},{24,1},{25,0},{2,27},{3,... | collective-permute-start | bytes 196616 | tf_op jit(solution)/shard_map/ppermute | solution.py:271
  67.4 0.6 query_sum.1
  68.0 0.5 collective-permute-start.20
  68.5 0.0 collective-permute-done.26.refs_8_
  68.5 3.5 %collective-permute-start.21 = (bf16[128,128]{1,0:T(8,128)(2,1)S(1)}, bf16[128,128]{1,0:T(8,128)(2,1)S(1)}, u32[]{:S(2)}, u32[]{:S(2)}) collective-permute-start(bf16[128,128]{1,0:T(8,128)(2,1)S(1)} %get-tuple-element.43), channel_id=1, source_target_pairs={{0,8},{1,9},{8,0},{9,1},{16,24},{17,25},{24,16},{25,17},{2,10},{3,... | collective-permute-start | bytes 98312 | tf_op jit(solution)/shard_map/ppermute | solution.py:271
  72.1 1.1 %collective-permute-done.27.refs_9_ = bf16[256,128]{1,0:T(8,128)(2,1)S(1)} collective-permute-done((bf16[256,128]{1,0:T(8,128)(2,1)S(1)}, bf16[256,128]{1,0:T(8,128)(2,1)S(1)}, u32[]{:S(2)}, u32[]{:S(2)}) %collective-permute-start.27) | collective-permute-done | bytes 65568 | tf_op jit(solution)/shard_map/ppermute | solution.py:271
  73.2 0.0 collective-permute-done.28.refs_10_
  73.2 0.0 collective-permute-done.29.refs_11_
  73.2 0.0 collective-permute-done.20.refs_1_
  73.2 0.7 collective-permute-done.21.refs_2_
  74.0 2.6 %collective-permute-done.22.refs_3_ = bf16[128,128]{1,0:T(8,128)(2,1)S(1)} collective-permute-done((bf16[128,128]{1,0:T(8,128)(2,1)S(1)}, bf16[128,128]{1,0:T(8,128)(2,1)S(1)}, u32[]{:S(2)}, u32[]{:S(2)}) %collective-permute-start.22) | collective-permute-done | bytes 32800 | tf_op jit(solution)/shard_map/ppermute | solution.py:271
  76.6 1.3 %finish.1 = (bf16[1,128,512]{2,1,0:T(8,128)(2,1)}, bf16[1,128,512]{2,1,0:T(8,128)(2,1)}, bf16[1,128,512]{2,1,0:T(8,128)(2,1)}) custom-call(s32[3]{0:T(128)S(1)} %copy-done.4, bf16[128,128]{1,0:T(8,128)(2,1)S(1)} %get-tuple-element.41.refs_0_, bf16[128,128]{1,0:T(8,128)(2,1)S(1)} %collective-permute-done.20.refs_1_, ...), custom_call_target="tpu_custom_call" | custom-call | tf_op jit(solution)/shard_map/finish/pallas_call | solution.py:371
  (18 shorter events, 0.0 us)
Async XLA Ops:
  1.9 8.1 %copy-start.3 = (f32[1,8,1024]{2,1,0:T(8,128)S(1)}, f32[1,8,1024]{2,1,0:T(8,128)}, u32[]{:S(2)}) copy-start(f32[1,8,1024]{2,1,0:T(8,128)} %refs_16_.1) | copy-start | bytes 98308
  5.1 5.0 %collective-permute-start = (bf16[272,128]{1,0:T(8,128)(2,1)}, bf16[272,128]{1,0:T(8,128)(2,1)S(1)}, u32[]{:S(2)}, u32[]{:S(2)}) collective-permute-start(bf16[272,128]{1,0:T(8,128)(2,1)} %get-tuple-element.29), channel_id=1, source_target_pairs={{0,1},{1,0},{8,9},{9,8},{16,17},{17,16},{24,25},{25,24},{2,3},{3,2... | collective-permute-start | bytes 208904 | tf_op jit(solution)/shard_map/ppermute | solution.py:271
  5.6 6.4 %collective-permute-start.1 = (bf16[272,128]{1,0:T(8,128)(2,1)}, bf16[272,128]{1,0:T(8,128)(2,1)S(1)}, u32[]{:S(2)}, u32[]{:S(2)}) collective-permute-start(bf16[272,128]{1,0:T(8,128)(2,1)} %get-tuple-element.30), channel_id=1, source_target_pairs={{0,8},{1,9},{8,0},{9,1},{16,24},{17,25},{24,16},{25,17},{2,10},{3,... | collective-permute-start | bytes 208904 | tf_op jit(solution)/shard_map/ppermute | solution.py:271
  8.2 4.4 %collective-permute-start.2 = (bf16[272,128]{1,0:T(8,128)(2,1)}, bf16[272,128]{1,0:T(8,128)(2,1)S(1)}, u32[]{:S(2)}, u32[]{:S(2)}) collective-permute-start(bf16[272,128]{1,0:T(8,128)(2,1)} %get-tuple-element.31), channel_id=1, source_target_pairs={{0,9},{1,8},{8,1},{9,0},{16,25},{17,24},{24,17},{25,16},{2,11},{3,... | collective-permute-start | bytes 208904 | tf_op jit(solution)/shard_map/ppermute | solution.py:271
  8.3 4.4 %copy-start.4 = (s32[3]{0:T(128)S(1)}, s32[3]{0:T(128)}, u32[]{:S(2)}) copy-start(s32[3]{0:T(128)} %pad_add_fusion.place_ref) | copy-start | bytes 40
  8.3 9.4 %collective-permute-start.15 = (s32[13,8,128]{2,1,0:T(8,128)}, s32[13,8,128]{2,1,0:T(8,128)S(1)}, u32[]{:S(2)}, u32[]{:S(2)}) collective-permute-start(s32[13,8,128]{2,1,0:T(8,128)} %get-tuple-element.36.refs_12_), channel_id=1, source_target_pairs={{0,9},{1,8},{8,1},{9,0},{16,25},{17,24},{24,17},{25,16},{2,11},{3,... | collective-permute-start | bytes 159752 | tf_op jit(solution)/shard_map/ppermute | solution.py:271
  10.0 7.2 %collective-permute-start.16 = (f32[1,8,1024]{2,1,0:T(8,128)S(1)}, f32[1,8,1024]{2,1,0:T(8,128)S(1)}, u32[]{:S(2)}, u32[]{:S(2)}) collective-permute-start(f32[1,8,1024]{2,1,0:T(8,128)S(1)} %copy-done.3), channel_id=1, source_target_pairs={{0,8},{8,0},{16,24},{24,16},{1,9},{9,1},{17,25},{25,17},{2,10},{10... | collective-permute-start | bytes 98312 | tf_op jit(solution)/shard_map/ppermute | solution.py:271
  10.1 10.2 %collective-permute-start.14 = (s32[13,8,128]{2,1,0:T(8,128)}, s32[13,8,128]{2,1,0:T(8,128)S(1)}, u32[]{:S(2)}, u32[]{:S(2)}) collective-permute-start(s32[13,8,128]{2,1,0:T(8,128)} %get-tuple-element.36.refs_12_), channel_id=1, source_target_pairs={{0,8},{1,9},{8,0},{9,1},{16,24},{17,25},{24,16},{25,17},{2,10},{3,... | collective-permute-start | bytes 159752 | tf_op jit(solution)/shard_map/ppermute | solution.py:271
  12.7 0.9 %copy-start = (bf16[272,128]{1,0:T(8,128)(2,1)S(1)}, bf16[272,128]{1,0:T(8,128)(2,1)}, u32[]{:S(2)}) copy-start(bf16[272,128]{1,0:T(8,128)(2,1)} %get-tuple-element.28.refs_0_) | copy-start | bytes 208900
  13.6 4.2 %copy-start.1 = (bf16[256,128]{1,0:T(8,128)(2,1)S(1)}, bf16[256,128]{1,0:T(8,128)(2,1)}, u32[]{:S(2)}) copy-start(bf16[256,128]{1,0:T(8,128)(2,1)} %get-tuple-element.32.refs_4_) | copy-start | bytes 196612
  13.6 6.8 %copy-start.2 = (s32[13,8,128]{2,1,0:T(8,128)S(1)}, s32[13,8,128]{2,1,0:T(8,128)}, u32[]{:S(2)}) copy-start(s32[13,8,128]{2,1,0:T(8,128)} %get-tuple-element.36.refs_12_) | copy-start | bytes 159748
  13.6 8.0 %copy-start.7 = (bf16[256,128]{1,0:T(8,128)(2,1)S(1)}, bf16[256,128]{1,0:T(8,128)(2,1)}, u32[]{:S(2)}) copy-start(bf16[256,128]{1,0:T(8,128)(2,1)} %get-tuple-element.33) | copy-start | bytes 196612
  13.6 14.4 %copy-start.6 = (bf16[256,128]{1,0:T(8,128)(2,1)S(1)}, bf16[256,128]{1,0:T(8,128)(2,1)}, u32[]{:S(2)}) copy-start(bf16[256,128]{1,0:T(8,128)(2,1)} %get-tuple-element.34) | copy-start | bytes 196612
  13.6 21.1 %copy-start.5 = (bf16[256,128]{1,0:T(8,128)(2,1)S(1)}, bf16[256,128]{1,0:T(8,128)(2,1)}, u32[]{:S(2)}) copy-start(bf16[256,128]{1,0:T(8,128)(2,1)} %get-tuple-element.35) | copy-start | bytes 196612
  14.2 26.1 %collective-permute-start.5 = (bf16[4,272,128]{2,1,0:T(8,128)(2,1)S(1)}, bf16[4,272,128]{2,1,0:T(8,128)(2,1)S(1)}, u32[]{:S(2)}, u32[]{:S(2)}) collective-permute-start(bf16[4,272,128]{2,1,0:T(8,128)(2,1)S(1)} %join.1.refs_0_), channel_id=1, source_target_pairs={{0,6},{2,4},{4,2},{6,0},{1,7},{3,5},{5,3},{7,1},{8,14},{10,12},{12... | collective-permute-start | bytes 835592 | tf_op jit(solution)/shard_map/ppermute | solution.py:271
  16.7 23.6 %collective-permute-start.4 = (bf16[4,272,128]{2,1,0:T(8,128)(2,1)S(1)}, bf16[4,272,128]{2,1,0:T(8,128)(2,1)S(1)}, u32[]{:S(2)}, u32[]{:S(2)}) collective-permute-start(bf16[4,272,128]{2,1,0:T(8,128)(2,1)S(1)} %join.1.refs_0_), channel_id=1, source_target_pairs={{0,4},{2,6},{4,0},{6,2},{1,5},{3,7},{5,1},{7,3},{8,12},{10,14},{12... | collective-permute-start | bytes 835592 | tf_op jit(solution)/shard_map/ppermute | solution.py:271
  17.2 23.1 %collective-permute-start.3 = (bf16[4,272,128]{2,1,0:T(8,128)(2,1)S(1)}, bf16[4,272,128]{2,1,0:T(8,128)(2,1)S(1)}, u32[]{:S(2)}, u32[]{:S(2)}) collective-permute-start(bf16[4,272,128]{2,1,0:T(8,128)(2,1)S(1)} %join.1.refs_0_), channel_id=1, source_target_pairs={{0,2},{2,0},{4,6},{6,4},{1,3},{3,1},{5,7},{7,5},{8,10},{10,8},{12,... | collective-permute-start | bytes 835592 | tf_op jit(solution)/shard_map/ppermute | solution.py:271
  17.7 6.6 %collective-permute-start.9 = (bf16[256,128]{1,0:T(8,128)(2,1)S(1)}, bf16[256,128]{1,0:T(8,128)(2,1)S(1)}, u32[]{:S(2)}, u32[]{:S(2)}) collective-permute-start(bf16[256,128]{1,0:T(8,128)(2,1)S(1)} %copy-done.1), channel_id=1, source_target_pairs={{0,16},{1,17},{8,24},{9,25},{16,0},{17,1},{24,8},{25,9},{2,18},{3,... | collective-permute-start | bytes 196616 | tf_op jit(solution)/shard_map/ppermute | solution.py:271
  20.3 1.2 %collective-permute-start.13 = (s32[13,8,128]{2,1,0:T(8,128)S(1)}, s32[13,8,128]{2,1,0:T(8,128)S(1)}, u32[]{:S(2)}, u32[]{:S(2)}) collective-permute-start(s32[13,8,128]{2,1,0:T(8,128)S(1)} %copy-done.2), channel_id=1, source_target_pairs={{0,1},{1,0},{8,9},{9,8},{16,17},{17,16},{24,25},{25,24},{2,3},{3,2... | collective-permute-start | bytes 159752 | tf_op jit(solution)/shard_map/ppermute | solution.py:271
  21.6 6.4 %collective-permute-start.10 = (bf16[256,128]{1,0:T(8,128)(2,1)S(1)}, bf16[256,128]{1,0:T(8,128)(2,1)S(1)}, u32[]{:S(2)}, u32[]{:S(2)}) collective-permute-start(bf16[256,128]{1,0:T(8,128)(2,1)S(1)} %copy-done.7), channel_id=1, source_target_pairs={{0,17},{1,16},{8,25},{9,24},{16,1},{17,0},{24,9},{25,8},{2,19},{3,... | collective-permute-start | bytes 196616 | tf_op jit(solution)/shard_map/ppermute | solution.py:271
  24.3 5.5 %collective-permute-start.6 = (bf16[256,128]{1,0:T(8,128)(2,1)S(1)}, bf16[256,128]{1,0:T(8,128)(2,1)S(1)}, u32[]{:S(2)}, u32[]{:S(2)}) collective-permute-start(bf16[256,128]{1,0:T(8,128)(2,1)S(1)} %copy-done.7), channel_id=1, source_target_pairs={{0,1},{1,0},{8,9},{9,8},{16,17},{17,16},{24,25},{25,24},{2,3},{3,2... | collective-permute-start | bytes 196616 | tf_op jit(solution)/shard_map/ppermute | solution.py:271
  27.9 6.8 %collective-permute-start.11 = (bf16[256,128]{1,0:T(8,128)(2,1)S(1)}, bf16[256,128]{1,0:T(8,128)(2,1)S(1)}, u32[]{:S(2)}, u32[]{:S(2)}) collective-permute-start(bf16[256,128]{1,0:T(8,128)(2,1)S(1)} %copy-done.6), channel_id=1, source_target_pairs={{0,24},{1,25},{8,16},{9,17},{16,8},{17,9},{24,0},{25,1},{2,26},{3,... | collective-permute-start | bytes 196616 | tf_op jit(solution)/shard_map/ppermute | solution.py:271
  29.8 5.3 %collective-permute-start.7 = (bf16[256,128]{1,0:T(8,128)(2,1)S(1)}, bf16[256,128]{1,0:T(8,128)(2,1)S(1)}, u32[]{:S(2)}, u32[]{:S(2)}) collective-permute-start(bf16[256,128]{1,0:T(8,128)(2,1)S(1)} %copy-done.6), channel_id=1, source_target_pairs={{0,8},{1,9},{8,0},{9,1},{16,24},{17,25},{24,16},{25,17},{2,10},{3,... | collective-permute-start | bytes 196616 | tf_op jit(solution)/shard_map/ppermute | solution.py:271
  34.7 5.5 %collective-permute-start.12 = (bf16[256,128]{1,0:T(8,128)(2,1)S(1)}, bf16[256,128]{1,0:T(8,128)(2,1)S(1)}, u32[]{:S(2)}, u32[]{:S(2)}) collective-permute-start(bf16[256,128]{1,0:T(8,128)(2,1)S(1)} %copy-done.5), channel_id=1, source_target_pairs={{0,25},{1,24},{8,17},{9,16},{16,9},{17,8},{24,1},{25,0},{2,27},{3,... | collective-permute-start | bytes 196616 | tf_op jit(solution)/shard_map/ppermute | solution.py:271
  35.1 5.2 %collective-permute-start.8 = (bf16[256,128]{1,0:T(8,128)(2,1)S(1)}, bf16[256,128]{1,0:T(8,128)(2,1)S(1)}, u32[]{:S(2)}, u32[]{:S(2)}) collective-permute-start(bf16[256,128]{1,0:T(8,128)(2,1)S(1)} %copy-done.5), channel_id=1, source_target_pairs={{0,9},{1,8},{8,1},{9,0},{16,25},{17,24},{24,17},{25,16},{2,11},{3,... | collective-permute-start | bytes 196616 | tf_op jit(solution)/shard_map/ppermute | solution.py:271
  48.2 15.7 %collective-permute-start.17 = (bf16[4,128,128]{2,1,0:T(8,128)(2,1)S(1)}, bf16[4,128,128]{2,1,0:T(8,128)(2,1)S(1)}, u32[]{:S(2)}, u32[]{:S(2)}) collective-permute-start(bf16[4,128,128]{2,1,0:T(8,128)(2,1)S(1)} %get-tuple-element.38), channel_id=1, source_target_pairs={{0,2},{2,0},{4,6},{6,4},{1,3},{3,1},{5,7},{7,5},{8,10},{10,8},{12,... | collective-permute-start | bytes 393224 | tf_op jit(solution)/shard_map/ppermute | solution.py:271
  48.5 15.3 %collective-permute-start.18 = (bf16[4,128,128]{2,1,0:T(8,128)(2,1)S(1)}, bf16[4,128,128]{2,1,0:T(8,128)(2,1)S(1)}, u32[]{:S(2)}, u32[]{:S(2)}) collective-permute-start(bf16[4,128,128]{2,1,0:T(8,128)(2,1)S(1)} %get-tuple-element.39), channel_id=1, source_target_pairs={{0,4},{2,6},{4,0},{6,2},{1,5},{3,7},{5,1},{7,3},{8,12},{10,14},{12... | collective-permute-start | bytes 393224 | tf_op jit(solution)/shard_map/ppermute | solution.py:271
  53.5 12.8 %collective-permute-start.19 = (bf16[4,128,128]{2,1,0:T(8,128)(2,1)S(1)}, bf16[4,128,128]{2,1,0:T(8,128)(2,1)S(1)}, u32[]{:S(2)}, u32[]{:S(2)}) collective-permute-start(bf16[4,128,128]{2,1,0:T(8,128)(2,1)S(1)} %get-tuple-element.40), channel_id=1, source_target_pairs={{0,6},{2,4},{4,2},{6,0},{1,7},{3,5},{5,3},{7,1},{8,14},{10,12},{12... | collective-permute-start | bytes 393224 | tf_op jit(solution)/shard_map/ppermute | solution.py:271
  54.9 1.3 %collective-permute-start.23 = (bf16[256,128]{1,0:T(8,128)(2,1)S(1)}, bf16[256,128]{1,0:T(8,128)(2,1)S(1)}, u32[]{:S(2)}, u32[]{:S(2)}) collective-permute-start(bf16[256,128]{1,0:T(8,128)(2,1)S(1)} %get-tuple-element.46), channel_id=1, source_target_pairs={{0,1},{1,0},{8,9},{9,8},{16,17},{17,16},{24,25},{25,24},{2,3},{3,2... | collective-permute-start | bytes 196616 | tf_op jit(solution)/shard_map/ppermute | solution.py:271
  54.9 4.8 %collective-permute-start.24 = (bf16[256,128]{1,0:T(8,128)(2,1)S(1)}, bf16[256,128]{1,0:T(8,128)(2,1)S(1)}, u32[]{:S(2)}, u32[]{:S(2)}) collective-permute-start(bf16[256,128]{1,0:T(8,128)(2,1)S(1)} %get-tuple-element.47), channel_id=1, source_target_pairs={{0,8},{1,9},{8,0},{9,1},{16,24},{17,25},{24,16},{25,17},{2,10},{3,... | collective-permute-start | bytes 196616 | tf_op jit(solution)/shard_map/ppermute | solution.py:271
  56.2 11.8 %collective-permute-start.25 = (bf16[256,128]{1,0:T(8,128)(2,1)S(1)}, bf16[256,128]{1,0:T(8,128)(2,1)S(1)}, u32[]{:S(2)}, u32[]{:S(2)}) collective-permute-start(bf16[256,128]{1,0:T(8,128)(2,1)S(1)} %get-tuple-element.48), channel_id=1, source_target_pairs={{0,9},{1,8},{8,1},{9,0},{16,25},{17,24},{24,17},{25,16},{2,11},{3,... | collective-permute-start | bytes 196616 | tf_op jit(solution)/shard_map/ppermute | solution.py:271
  59.7 8.8 %collective-permute-start.26 = (bf16[256,128]{1,0:T(8,128)(2,1)S(1)}, bf16[256,128]{1,0:T(8,128)(2,1)S(1)}, u32[]{:S(2)}, u32[]{:S(2)}) collective-permute-start(bf16[256,128]{1,0:T(8,128)(2,1)S(1)} %get-tuple-element.49), channel_id=1, source_target_pairs={{0,16},{1,17},{8,24},{9,25},{16,0},{17,1},{24,8},{25,9},{2,18},{3,... | collective-permute-start | bytes 196616 | tf_op jit(solution)/shard_map/ppermute | solution.py:271
  63.8 9.4 %collective-permute-start.27 = (bf16[256,128]{1,0:T(8,128)(2,1)S(1)}, bf16[256,128]{1,0:T(8,128)(2,1)S(1)}, u32[]{:S(2)}, u32[]{:S(2)}) collective-permute-start(bf16[256,128]{1,0:T(8,128)(2,1)S(1)} %get-tuple-element.50), channel_id=1, source_target_pairs={{0,17},{1,16},{8,25},{9,24},{16,1},{17,0},{24,9},{25,8},{2,19},{3,... | collective-permute-start | bytes 196616 | tf_op jit(solution)/shard_map/ppermute | solution.py:271
  63.8 9.4 %collective-permute-start.28 = (bf16[256,128]{1,0:T(8,128)(2,1)S(1)}, bf16[256,128]{1,0:T(8,128)(2,1)S(1)}, u32[]{:S(2)}, u32[]{:S(2)}) collective-permute-start(bf16[256,128]{1,0:T(8,128)(2,1)S(1)} %get-tuple-element.51), channel_id=1, source_target_pairs={{0,24},{1,25},{8,16},{9,17},{16,8},{17,9},{24,0},{25,1},{2,26},{3,... | collective-permute-start | bytes 196616 | tf_op jit(solution)/shard_map/ppermute | solution.py:271
  66.3 6.9 %collective-permute-start.29 = (bf16[256,128]{1,0:T(8,128)(2,1)S(1)}, bf16[256,128]{1,0:T(8,128)(2,1)S(1)}, u32[]{:S(2)}, u32[]{:S(2)}) collective-permute-start(bf16[256,128]{1,0:T(8,128)(2,1)S(1)} %get-tuple-element.52), channel_id=1, source_target_pairs={{0,25},{1,24},{8,17},{9,16},{16,9},{17,8},{24,1},{25,0},{2,27},{3,... | collective-permute-start | bytes 196616 | tf_op jit(solution)/shard_map/ppermute | solution.py:271
  68.0 5.2 %collective-permute-start.20 = (bf16[128,128]{1,0:T(8,128)(2,1)S(1)}, bf16[128,128]{1,0:T(8,128)(2,1)S(1)}, u32[]{:S(2)}, u32[]{:S(2)}) collective-permute-start(bf16[128,128]{1,0:T(8,128)(2,1)S(1)} %get-tuple-element.42), channel_id=1, source_target_pairs={{0,1},{1,0},{8,9},{9,8},{16,17},{17,16},{24,25},{25,24},{2,3},{3,2... | collective-permute-start | bytes 98312 | tf_op jit(solution)/shard_map/ppermute | solution.py:271
  68.5 5.4 %collective-permute-start.21 = (bf16[128,128]{1,0:T(8,128)(2,1)S(1)}, bf16[128,128]{1,0:T(8,128)(2,1)S(1)}, u32[]{:S(2)}, u32[]{:S(2)}) collective-permute-start(bf16[128,128]{1,0:T(8,128)(2,1)S(1)} %get-tuple-element.43), channel_id=1, source_target_pairs={{0,8},{1,9},{8,0},{9,1},{16,24},{17,25},{24,16},{25,17},{2,10},{3,... | collective-permute-start | bytes 98312 | tf_op jit(solution)/shard_map/ppermute | solution.py:271
  73.2 3.3 %collective-permute-start.22 = (bf16[128,128]{1,0:T(8,128)(2,1)S(1)}, bf16[128,128]{1,0:T(8,128)(2,1)S(1)}, u32[]{:S(2)}, u32[]{:S(2)}) collective-permute-start(bf16[128,128]{1,0:T(8,128)(2,1)S(1)} %get-tuple-element.44), channel_id=1, source_target_pairs={{0,9},{1,8},{8,1},{9,0},{16,25},{17,24},{24,17},{25,16},{2,11},{3,... | collective-permute-start | bytes 98312 | tf_op jit(solution)/shard_map/ppermute | solution.py:271
where the time goes:
time: 77.8 us; the launch traced here: 77.9 us
  starting transfers between devices  34.9 us (45%)
  waiting for transfers between devices  26.5 us (34%)
  Pallas kernels  13.6 us (17%)
  between operations  1.4 us (2%)
  local copies, waits for them, and re-layouts  0.91 us (1%)
    ppermute x30, starting transfers between devices, send(): lax.ppermute(block, axes, [(place, place ^ step) for place in range(count)])  34.9 us
    ppermute x30, waiting for transfers between devices, send(): lax.ppermute(block, axes, [(place, place ^ step) for place in range(count)])  26.5 us
    pallas_call x1, Pallas kernels, body(): pl.pallas_call(functools.partial(pair_kernel, (head_dim, tile, capacity,...  7.91 us
    pallas_call x1, Pallas kernels, body(): pl.pallas_call(functools.partial(pack_kernel, heads), out_shape=(qg_shape...  3.16 us
  transfers between devices with their start and end apart: 30, of which 12 were waited for; matrix products, arithmetic and copies ran while one was open for 0% of the time, Pallas kernels for 2%

commit v1 on v0

v1 whole, which is shorter than its diff:
```python
import functools

import jax
import jax.numpy as jnp
from jax import lax
from jax.experimental import pallas as pl
from jax.experimental.pallas import tpu as pltpu
from jax.sharding import Mesh
from jax.sharding import PartitionSpec as P


F32 = jnp.float32
BF16 = jnp.bfloat16
I32 = jnp.int32
LANES = 128
PAD = 16
QUARTERS = 4
LOG2E = 1.4426950408889634
NT = (((1,), (1,)), ((), ()))
NN = (((1,), (0,)), ((), ()))
MEDIUM = pltpu.CompilerParams(vmem_limit_bytes=28 * 1024 * 1024)
SMALL = pltpu.CompilerParams(vmem_limit_bytes=12 * 1024 * 1024)
VMEM = pl.BlockSpec(memory_space=pltpu.VMEM)
HBM = pl.BlockSpec(memory_space=pltpu.HBM)


def lanes_of(quarter):
    return pl.ds(pl.multiple_of(quarter * LANES, LANES), LANES)


def my_place():
    row, chip, core = (lax.axis_index(name) for name in ("row", "chip", "core"))
    return row, chip, core, row % 2 * 2 + core


def pack_kernel(
    heads, q_hbm, g_hbm, o_hbm, k_hbm, v_hbm, bits_hbm, slot_ref, live_ref,
    qg_own, qg_pair0, qg_pair1, kv_own, sib_ref, packed_ref,
    q_ref, g_ref, o_ref, k_ref, v_ref, bits_ref, delta_ref, sems,
):
    arrays = (
        (q_hbm, q_ref), (g_hbm, g_ref), (o_hbm, o_ref),
        (k_hbm, k_ref), (v_hbm, v_ref), (bits_hbm, bits_ref),
    )
    copies = [pltpu.make_async_copy(a, b, sems.at[i]) for i, (a, b) in enumerate(arrays)]
    for copy in copies:
        copy.start()
    rows, width = q_ref.shape[1:]
    krows = k_ref.shape[1]
    head_dim = width // heads
    local = heads // QUARTERS
    capacity = bits_ref.shape[2]
    quarter = my_place()[3]
    feature = lax.broadcasted_iota(I32, (QUARTERS * PAD, width), 1)
    line = lax.broadcasted_iota(I32, (QUARTERS * PAD, width), 0)
    wanted = jnp.where(line % PAD < local, line // PAD * local + line % PAD, -1)
    pick = (feature // head_dim == wanted).astype(F32)
    packed_ref[capacity // 2] = jnp.zeros((8, LANES), I32)
    packed_ref[capacity // 2, 0:1, 0:capacity] = slot_ref[0]
    packed_ref[capacity // 2, 1:2, 0:1] = live_ref[...]
    for copy in copies:
        copy.wait()
    product = g_ref[0].astype(F32) * o_ref[0].astype(F32)
    delta = lax.dot_general(
        pick, product, NT, precision=lax.Precision.HIGHEST, preferred_element_type=F32
    ).astype(BF16)
    for index in range(QUARTERS):
        delta_ref[index] = delta[index * PAD : (index + 1) * PAD]
    base = 4 * krows
    for step, (ref, start) in enumerate(
        ((qg_own, 0), (sib_ref, base), (qg_pair0, 0), (qg_pair1, 0))
    ):
        lanes = lanes_of(quarter ^ step)
        ref[start : start + rows] = q_ref[0, :, lanes]
        ref[start + rows : start + 2 * rows] = g_ref[0, :, lanes]
        if rows < LANES:
            ref[start + 2 * rows : start + 2 * rows + PAD] = jnp.zeros((PAD, LANES), BF16)
        ref[start + 2 * rows : start + 2 * rows + PAD, :rows] = delta_ref[quarter ^ step]
    for side in range(2):
        for ref, step in ((kv_own, 2 * side), (sib_ref, 2 * side + 1)):
            lanes = lanes_of(quarter ^ step)
            start = side * 2 * krows
            ref[start : start + krows] = k_ref[0, :, lanes]
            ref[start + krows : start + 2 * krows] = v_ref[0, :, lanes]
    for entry in range(capacity):
        words = bits_ref[0, 0, entry]
        span = slice(entry % 2 * 4, entry % 2 * 4 + 4)
        packed_ref[entry // 2, span] = words[:4] | lax.shift_left(words[4:], I32(16))


def join_kernel(
    krows, qg_own, qg_pair0, qg_pair1, kv_own, sib_ref, bits_own, bits_sib,
    qg_out, kv_same, kv_pair, bits_out,
):
    row, chip, core, quarter = my_place()
    qg_out[quarter] = qg_own[...]
    qg_out[quarter ^ 1] = sib_ref[4 * krows :]
    qg_out[quarter ^ 2] = qg_pair0[...]
    qg_out[quarter ^ 3] = qg_pair1[...]
    for side, ref in enumerate((kv_same, kv_pair)):
        span = slice(side * 2 * krows, (side + 1) * 2 * krows)
        ref[core] = kv_own[span]
        ref[1 - core] = sib_ref[span]
    bits_out[core] = bits_own[...]
    bits_out[1 - core] = bits_sib[...]


def pair_kernel(sizes, *refs):
    head_dim, tile, capacity, chips, row_count = sizes
    qg_refs, refs = refs[:chips], refs[chips:]
    kv_refs, refs = refs[:row_count], refs[row_count:]
    bits_refs, refs = refs[:2], refs[2:]
    lse_refs, refs = refs[:2], refs[2:]
    dq_refs, refs = refs[:chips], refs[chips:]
    dkv_refs, refs = refs[:row_count], refs[row_count:]
    (q2_scr, g2_scr, q2t_scr, g2t_scr, k_scr, v_scr, k2t_scr, lse_scr, delta_scr,
     dqt_scr, dk_scr, dv_scr, dq_scr, info, sems) = refs
    rows = (qg_refs[0].shape[1] - PAD) // 2
    krows = kv_refs[0].shape[1] // 2
    query_tiles = q2_scr.shape[1]
    key_tiles = k_scr.shape[1]
    scaling = float(head_dim) ** -0.5
    row, chip, core, quarter = my_place()
    side = row % 2

    copies = [
        pltpu.make_async_copy(
            bits_refs[i // 2].at[i % 2, capacity // 2], info.at[i], sems.at[i]
        )
        for i in range(QUARTERS)
    ]
    for copy in copies:
        copy.start()

    for step, ref in enumerate(lse_refs):
        every = ref[0] * LOG2E
        own = every[:2]
        for index in range(1, QUARTERS):
            own = jnp.where(quarter == index, every[2 * index : 2 * index + 2], own)
        for u in range(query_tiles):
            lse_scr[side ^ step, u] = own[:, u * tile : (u + 1) * tile]
    low = lax.broadcasted_iota(I32, (rows, LANES), 1) < head_dim
    none = jnp.zeros((rows, LANES), BF16)
    for step in range(chips):
        for index in range(QUARTERS):
            source = (chip ^ step) * 2 + index % 2
            start = source * rows
            u = start // tile
            inner = pl.multiple_of(start % tile, rows)
            block = index // 2
            for scr, part in ((q2_scr, 0), (g2_scr, 1)):
                piece = qg_refs[step][index, part * rows : (part + 1) * rows]
                scr[block, u, 0, pl.ds(inner, rows)] = jnp.where(low, piece, none)
                scr[block, u, 1, pl.ds(inner, rows)] = jnp.where(low, none, piece)
            delta = qg_refs[step][index, 2 * rows :, :rows].astype(F32)
            if rows == tile:
                delta_scr[block, u] = delta
            else:
                for part in range(tile // rows):
                    @pl.when(source % (tile // rows) == part)
                    def _(part=part, delta=delta, u=u, block=block):
                        delta_scr[block, u, :, part * rows : (part + 1) * rows] = delta
    for step in range(row_count):
        start = (row ^ step) * krows
        inner = pl.multiple_of(start % tile, krows)
        for block in range(2):
            k_scr[block, start // tile, pl.ds(inner, krows)] = kv_refs[step][block, :krows]
            v_scr[block, start // tile, pl.ds(inner, krows)] = kv_refs[step][block, krows:]
    low_row = lax.broadcasted_iota(I32, (LANES, tile), 0) < head_dim
    none_t = jnp.zeros((LANES, tile), BF16)
    for block in range(2):
        for w in range(key_tiles):
            flipped = k_scr[block, w].T
            k2t_scr[block, w] = jnp.concatenate(
                [jnp.where(low_row, flipped, none_t), jnp.where(low_row, none_t, flipped)], axis=1
            )
    for block in range(2):
        for u in range(query_tiles):
            for part in range(2):
                lanes = slice(part * tile, (part + 1) * tile)
                q2t_scr[block, u, :, lanes] = q2_scr[block, u, part].T
                g2t_scr[block, u, :, lanes] = g2_scr[block, u, part].T
    dqt_scr[...] = jnp.zeros_like(dqt_scr)
    dk_scr[...] = jnp.zeros_like(dk_scr)
    dv_scr[...] = jnp.zeros_like(dv_scr)
    place_in = lax.broadcasted_iota(I32, (2, 4, 16, tile), 2)
    upper = lax.broadcasted_iota(I32, (2, 4, 16, tile), 0)
    bit = lax.shift_left(I32(1), place_in + 16 * upper).reshape(tile, tile)
    for copy in copies:
        copy.wait()

    for step in range(QUARTERS):
        qb = side ^ (step // 2)
        kb = step % 2
        live = info[step, 1, 0]

        def two_tiles(index, _, step=step, qb=qb, kb=kb, live=live):
            both = bits_refs[step // 2][kb, index]
            second = jnp.where(index * 2 + 1 < live, I32(-1), I32(0))
            work = []
            for part in range(2):
                slot = info[step, 0, index * 2 + part]
                u = slot // key_tiles
                w = slot % key_tiles
                words = both[part * 4 : part * 4 + 4]
                if part:
                    words = words & second
                words = jnp.broadcast_to(words[:, None, :], (4, 16, tile)).reshape(64, tile)
                edge = (jnp.concatenate([words, words], axis=0) & bit) != 0
                q2 = q2_scr[qb, u].reshape(2 * tile, LANES)
                g2 = g2_scr[qb, u].reshape(2 * tile, LANES)
                scores = lax.dot_general(
                    k_scr[kb, w], q2t_scr[qb, u], NN, preferred_element_type=F32
                )
                grad_prob = lax.dot_general(
                    v_scr[kb, w], g2t_scr[qb, u], NN, preferred_element_type=F32
                )
                work.append((u, w, edge, q2, g2, scores, grad_prob))
            done = []
            for u, w, edge, q2, g2, scores, grad_prob in work:
                lse_tile = lse_scr[qb, u]
                delta_tile = delta_scr[qb, u]
                probs, grads = [], []
                for h in range(2):
                    s = scores[:, h * tile : (h + 1) * tile]
                    gp = grad_prob[:, h * tile : (h + 1) * tile]
                    p = jnp.exp2(s * (scaling * LOG2E) - lse_tile[h : h + 1])
                    p = jnp.where(edge, p, 0.0)
                    ds = p * (gp - delta_tile[h : h + 1])
                    probs.append(p.astype(BF16))
                    grads.append(ds.astype(BF16))
                done.append((
                    lax.dot_general(
                        jnp.concatenate(probs, axis=1), g2, NN, preferred_element_type=F32
                    ),
                    lax.dot_general(
                        jnp.concatenate(grads, axis=1), q2, NN, preferred_element_type=F32
                    ),
                    lax.dot_general(
                        k2t_scr[kb, w], jnp.concatenate(grads, axis=0), NN,
                        preferred_element_type=F32,
                    ),
                ))
            for (u, w, *_), (dv, dk, dqt) in zip(work, done):
                dv_scr[kb, w] += dv
                dk_scr[kb, w] += dk
                dqt_scr[qb, u] += dqt
            return 0

        lax.fori_loop(0, (live + 1) // 2, two_tiles, 0)

    for step in range(row_count):
        start = (row ^ step) * krows
        inner = pl.multiple_of(start % tile, krows)
        for block in range(2):
            dk = dk_scr[block, start // tile, pl.ds(inner, krows)] * scaling
            dv = dv_scr[block, start // tile, pl.ds(inner, krows)]
            dkv_refs[step][block, :krows] = dk.astype(BF16)
            dkv_refs[step][block, krows:] = dv.astype(BF16)
    for block in range(2):
        for u in range(query_tiles):
            dq_scr[block, u * tile : (u + 1) * tile] = (dqt_scr[block, u] * scaling).astype(BF16).T
    for step in range(chips):
        for index in range(QUARTERS):
            start = pl.multiple_of(((chip ^ step) * 2 + index % 2) * rows, rows)
            dq_refs[step][index] = dq_scr[index // 2, pl.ds(start, rows)]


def query_sum_kernel(chips, *refs):
    parts, (same_ref, pair_ref) = refs[:chips], refs[chips:]
    side = my_place()[0] % 2
    for step, ref in enumerate((same_ref, pair_ref)):
        for core in range(2):
            index = (side ^ step) * 2 + core
            total = parts[0][index].astype(F32)
            for part in parts[1:]:
                total += part[index].astype(F32)
            ref[core] = total.astype(BF16)


def key_sum_kernel(row_count, *refs):
    (dq_same, dq_pair), dkv_refs, (own_ref, sib_ref) = refs[:2], refs[2:-2], refs[-2:]
    krows2 = dkv_refs[0].shape[1]
    core = my_place()[2]
    for ref, block in ((own_ref, core), (sib_ref, 1 - core)):
        for side, dq in enumerate((dq_same, dq_pair)):
            total = dkv_refs[side][block].astype(F32)
            for other in range(side + 2, row_count, 2):
                total += dkv_refs[other][block].astype(F32)
            ref[side, :krows2] = total.astype(BF16)
            ref[side, krows2:] = dq[block]


def finish_kernel(krows, own_ref, sib_ref, dq_out, dk_out, dv_out):
    quarter = my_place()[3]
    for core, ref in enumerate((own_ref, sib_ref)):
        for side in range(2):
            lanes = lanes_of(quarter ^ (2 * side + core))
            dk_out[0, :, lanes] = ref[side, :krows]
            dv_out[0, :, lanes] = ref[side, krows : 2 * krows]
            dq_out[0, :, lanes] = ref[side, 2 * krows :]


def send(block, axes, count, step):
    return lax.ppermute(block, axes, [(place, place ^ step) for place in range(count)])


def body(sizes, queries, keys, values, outputs, grad_out, lse, tile_slot, tile_live, tile_bits):
    row_count, chips, cores = sizes
    heads = lse.shape[1]
    width = queries.shape[2]
    head_dim = width // heads
    tile = tile_bits.shape[4]
    capacity = tile_slot.shape[2]
    rows = queries.shape[1]
    krows = keys.shape[1]
    query_tiles = lse.shape[2] // tile
    key_tiles = row_count * krows // tile
    line = ("row", "core")
    places = row_count * cores

    def shape(*dims, dtype=BF16):
        return jax.ShapeDtypeStruct(dims, dtype)

    qg_shape = shape(2 * rows + PAD, LANES)
    kv_shape = shape(2, 2 * krows, LANES)
    qg_own, qg_pair0, qg_pair1, kv_own, to_sibling, bits_own = pl.pallas_call(
        functools.partial(pack_kernel, heads),
        out_shape=(
            qg_shape, qg_shape, qg_shape, shape(4 * krows, LANES),
            shape(4 * krows + 2 * rows + PAD, LANES),
            shape(capacity // 2 + 1, 8, LANES, dtype=I32),
        ),
        in_specs=[HBM] * 6 + [VMEM] * 2,
        out_specs=(VMEM,) * 6,
        scratch_shapes=[
            pltpu.VMEM(queries.shape, BF16),
            pltpu.VMEM(queries.shape, BF16),
            pltpu.VMEM(queries.shape, BF16),
            pltpu.VMEM(keys.shape, BF16),
            pltpu.VMEM(keys.shape, BF16),
            pltpu.VMEM(tile_bits.shape, I32),
            pltpu.VMEM((QUARTERS, PAD, rows), BF16),
            pltpu.SemaphoreType.DMA((6,)),
        ],
        compiler_params=SMALL,
        name="pack",
    )(queries, grad_out, outputs, keys, values, tile_bits, tile_slot, tile_live)

    qg_pair0 = send(qg_pair0, line, places, 2)
    qg_pair1 = send(qg_pair1, line, places, 3)
    from_sibling = send(to_sibling, "core", cores, 1)
    bits_sibling = send(bits_own, "core", cores, 1)
    lse_other = send(lse, "row", row_count, 1)
    qg, kv_same, kv_pair, bits = pl.pallas_call(
        functools.partial(join_kernel, krows),
        out_shape=(
            shape(QUARTERS, 2 * rows + PAD, LANES), kv_shape, kv_shape,
            shape(2, capacity // 2 + 1, 8, LANES, dtype=I32),
        ),
        in_specs=[VMEM] * 7,
        out_specs=(VMEM,) * 4,
        compiler_params=SMALL,
        name="join",
    )(qg_own, qg_pair0, qg_pair1, kv_own, from_sibling, bits_own, bits_sibling)
    kv_out = (kv_same, kv_pair)
    kv = [kv_same] + [
        send(kv_out[step % 2], "row", row_count, step) for step in range(1, row_count)
    ]
    bits_other = send(bits, "row", row_count, 1)
    qg = [qg] + [send(qg, "chip", chips, step) for step in range(1, chips)]

    parts = pl.pallas_call(
        functools.partial(pair_kernel, (head_dim, tile, capacity, chips, row_count)),
        out_shape=(shape(QUARTERS, rows, LANES),) * chips + (kv_shape,) * row_count,
        in_specs=[VMEM] * (chips + row_count + 4),
        out_specs=(VMEM,) * (chips + row_count),
        scratch_shapes=[
            pltpu.VMEM((2, query_tiles, 2, tile, LANES), BF16),
            pltpu.VMEM((2, query_tiles, 2, tile, LANES), BF16),
            pltpu.VMEM((2, query_tiles, LANES, 2 * tile), BF16),
            pltpu.VMEM((2, query_tiles, LANES, 2 * tile), BF16),
            pltpu.VMEM((2, key_tiles, tile, LANES), BF16),
            pltpu.VMEM((2, key_tiles, tile, LANES), BF16),
            pltpu.VMEM((2, key_tiles, LANES, 2 * tile), BF16),
            pltpu.VMEM((2, query_tiles, 2, tile), F32),
            pltpu.VMEM((2, query_tiles, PAD, tile), F32),
            pltpu.VMEM((2, query_tiles, LANES, tile), F32),
            pltpu.VMEM((2, key_tiles, tile, LANES), F32),
            pltpu.VMEM((2, key_tiles, tile, LANES), F32),
            pltpu.VMEM((2, query_tiles * tile, LANES), BF16),
            pltpu.SMEM((QUARTERS, 8, LANES), I32),
            pltpu.SemaphoreType.DMA((QUARTERS,)),
        ],
        compiler_params=MEDIUM,
        name="pair",
    )(*qg, *kv, bits, bits_other, lse, lse_other)

    dq, dkv = parts[:chips], parts[chips:]
    dq = [dq[0]] + [send(dq[step], "chip", chips, step) for step in range(1, chips)]
    dkv = [dkv[0]] + [send(dkv[step], "row", row_count, step) for step in range(1, row_count)]
    dq_same, dq_pair = pl.pallas_call(
        functools.partial(query_sum_kernel, chips),
        out_shape=(shape(2, rows, LANES),) * 2,
        in_specs=[VMEM] * chips,
        out_specs=(VMEM,) * 2,
        compiler_params=SMALL,
        name="query_sum",
    )(*dq)
    dq_pair = send(dq_pair, "row", row_count, 1)
    own, to_sibling = pl.pallas_call(
        functools.partial(key_sum_kernel, row_count),
        out_shape=(shape(2, 2 * krows + rows, LANES),) * 2,
        in_specs=[VMEM] * (2 + row_count),
        out_specs=(VMEM,) * 2,
        compiler_params=SMALL,
        name="key_sum",
    )(dq_same, dq_pair, *dkv)
    from_sibling = send(to_sibling, "core", cores, 1)
    return pl.pallas_call(
        functools.partial(finish_kernel, krows),
        out_shape=(shape(1, rows, width), shape(1, krows, width), shape(1, krows, width)),
        in_specs=[VMEM] * 2,
        out_specs=(VMEM,) * 3,
        compiler_params=SMALL,
        name="finish",
    )(own, from_sibling)


def solution(mesh):
    row_count, columns = mesh.devices.shape
    cores = 2
    chips = columns // cores
    fine = Mesh(mesh.devices.reshape(row_count, chips, cores), ("row", "chip", "core"))
    col = ("chip", "core")
    in_specs = (
        P("row", col, None),
        P(col, "row", None),
        P(col, "row", None),
        P("row", col, None),
        P("row", col, None),
        P("row", None, None),
        P("row", col, None),
        P("row", col),
        P("row", col, None, None, None),
    )
    out_specs = (P("row", col, None), P(col, "row", None), P(col, "row", None))
    return jax.shard_map(
        functools.partial(body, (row_count, chips, cores)),
        mesh=fine, in_specs=in_specs, out_specs=out_specs, check_vma=False,
    )
```

time: 77.8 us -> 66.3 us (0.85); the launches traced: 77.9 us -> 65.5 us
  starting transfers between devices: 34.9 us -> 26.6 us
  waiting for transfers between devices: 26.5 us -> 21.2 us
  local copies, waits for them, and re-layouts: 0.91 us -> 5.41 us
  Pallas kernels: 13.6 us -> 10.9 us
    ppermute x30 -> x20, starting transfers between devices: 34.9 us -> 26.6 us  [send(): lax.ppermute(block, axes, [(place, place ^ step) for place in range(count)])]
    ppermute x30 -> x20, waiting for transfers between devices: 26.5 us -> 21.2 us  [send(): lax.ppermute(block, axes, [(place, place ^ step) for place in range(count)])]
    unnamed x16, local copies, waits for them, and re-layouts: 0.91 us -> 5.41 us
    pallas_call x1, Pallas kernels: 3.16 us -> 1.46 us  [body(): pl.pallas_call(functools.partial(pack_kernel, heads), out_shape=(qg_shape...]
    pallas_call x3 -> x4, Pallas kernels: 2.52 us -> 1 us  [the longest x1 0.81 us: body(): pl.pallas_call(functools.partial(finish_kernel, krows), out_shape=(shape(...]
  transfers between devices with their start and end apart: 30 -> 20, of which waited for: 12 -> 12; matrix products, arithmetic and copies ran while one was open for 0% -> 0% of each run, Pallas kernels for 2% -> 0%
where the time goes in v1:
time: 66.3 us; the launch traced here: 65.5 us
  starting transfers between devices  26.6 us (40%)
  waiting for transfers between devices  21.2 us (32%)
  Pallas kernels  10.9 us (16%)
  local copies, waits for them, and re-layouts  5.41 us (8%)
  between operations  1.38 us (2%)
    ppermute x20, starting transfers between devices, send(): lax.ppermute(block, axes, [(place, place ^ step) for place in range(count)])  26.6 us
    ppermute x20, waiting for transfers between devices, send(): lax.ppermute(block, axes, [(place, place ^ step) for place in range(count)])  21.2 us
    pallas_call x1, Pallas kernels, body(): pl.pallas_call(functools.partial(pair_kernel, (head_dim, tile, capacity,...  8.43 us
    unnamed x16, local copies, waits for them, and re-layouts  5.41 us
    pallas_call x1, Pallas kernels, body(): pl.pallas_call(functools.partial(pack_kernel, heads), out_shape=(qg_shape...  1.46 us
  transfers between devices with their start and end apart: 20, of which 12 were waited for; matrix products, arithmetic and copies ran while one was open for 0% of the time, Pallas kernels for 0%

profile of v1, /device:TPU:0, one launch (start us, length us, event | category | flops | bytes accessed | tf_op | source)
XLA Modules:
  0.0 65.5 jit_solution(1388010405782275137)
XLA Ops:
  0.6 0.0 copy-start.7
  1.3 0.0 copy-done.7
  1.3 0.0 copy-start
  1.3 0.9 %copy-done = bf16[1,128,512]{2,1,0:T(8,128)(2,1)S(1)} copy-done((bf16[1,128,512]{2,1,0:T(8,128)(2,1)S(1)}, bf16[1,128,512]{2,1,0:T(8,128)(2,1)}, u32[]{:S(2)}) %copy-start) | copy-done | bytes 131096
  2.2 0.0 copy-start.1
  2.2 0.9 %copy-done.1 = bf16[1,128,512]{2,1,0:T(8,128)(2,1)S(1)} copy-done((bf16[1,128,512]{2,1,0:T(8,128)(2,1)S(1)}, bf16[1,128,512]{2,1,0:T(8,128)(2,1)}, u32[]{:S(2)}) %copy-start.1) | copy-done | bytes 131096
  3.1 0.0 copy-start.2
  3.1 0.9 %copy-done.2 = bf16[1,128,512]{2,1,0:T(8,128)(2,1)S(1)} copy-done((bf16[1,128,512]{2,1,0:T(8,128)(2,1)S(1)}, bf16[1,128,512]{2,1,0:T(8,128)(2,1)}, u32[]{:S(2)}) %copy-start.2) | copy-done | bytes 131096
  4.0 0.0 copy-start.3
  4.0 0.9 %copy-done.3 = bf16[1,128,512]{2,1,0:T(8,128)(2,1)S(1)} copy-done((bf16[1,128,512]{2,1,0:T(8,128)(2,1)S(1)}, bf16[1,128,512]{2,1,0:T(8,128)(2,1)}, u32[]{:S(2)}) %copy-start.3) | copy-done | bytes 131096
  4.9 0.0 copy-start.4
  4.9 0.9 %copy-done.4 = bf16[1,128,512]{2,1,0:T(8,128)(2,1)S(1)} copy-done((bf16[1,128,512]{2,1,0:T(8,128)(2,1)S(1)}, bf16[1,128,512]{2,1,0:T(8,128)(2,1)}, u32[]{:S(2)}) %copy-start.4) | copy-done | bytes 131096
  5.8 0.0 copy-start.5
  5.8 0.9 %copy-done.5 = s32[1,1,24,8,128]{4,3,2,1,0:T(8,128)S(1)} copy-done((s32[1,1,24,8,128]{4,3,2,1,0:T(8,128)S(1)}, s32[1,1,24,8,128]{4,3,2,1,0:T(8,128)}, u32[]{:S(2)}) %copy-start.5) | copy-done | bytes 98328
  6.7 1.5 %pack.1 = (bf16[272,128]{1,0:T(8,128)(2,1)S(1)}, bf16[272,128]{1,0:T(8,128)(2,1)S(1)}, bf16[272,128]{1,0:T(8,128)(2,1)S(1)}, bf16[512,128]{1,0:T(8,128)(2,1)S(1)...) custom-call(bf16[1,128,512]{2,1,0:T(8,128)(2,1)S(1)} %copy-done, bf16[1,128,512]{2,1,0:T(8,128)(2,1)S(1)} %copy-done.1, ...), custom_call_target="tpu_custom_call" | custom-call | tf_op jit(solution)/shard_map/pack/pallas_call | solution.py:327
  8.2 0.5 collective-permute-start.2
  8.7 2.6 %collective-permute-start = (bf16[272,128]{1,0:T(8,128)(2,1)S(1)}, bf16[272,128]{1,0:T(8,128)(2,1)S(1)}, u32[]{:S(2)}, u32[]{:S(2)}) collective-permute-start(bf16[272,128]{1,0:T(8,128)(2,1)S(1)} %get-tuple-element.26), channel_id=1, source_target_pairs={{0,8},{1,9},{8,0},{9,1},{16,24},{17,25},{24,16},{25,17},{2,10},{3,... | collective-permute-start | bytes 208904 | tf_op jit(solution)/shard_map/ppermute | solution.py:305
  11.4 0.1 collective-permute-start.1
  11.4 0.1 collective-permute-start.3
  11.6 1.1 %collective-permute-done.3.bits_sib = s32[13,8,128]{2,1,0:T(8,128)S(1)} collective-permute-done((s32[13,8,128]{2,1,0:T(8,128)S(1)}, s32[13,8,128]{2,1,0:T(8,128)S(1)}, u32[]{:S(2)}, u32[]{:S(2)}) %collective-permute-start.3) | collective-permute-done | bytes 53280 | tf_op jit(solution)/shard_map/ppermute | solution.py:305
  12.7 1.5 %collective-permute-done.qg_pair0 = bf16[272,128]{1,0:T(8,128)(2,1)S(1)} collective-permute-done((bf16[272,128]{1,0:T(8,128)(2,1)S(1)}, bf16[272,128]{1,0:T(8,128)(2,1)S(1)}, u32[]{:S(2)}, u32[]{:S(2)}) %collective-permute-start) | collective-permute-done | bytes 69664 | tf_op jit(solution)/shard_map/ppermute | solution.py:305
  14.1 1.4 %collective-permute-done.1.qg_pair1 = bf16[272,128]{1,0:T(8,128)(2,1)S(1)} collective-permute-done((bf16[272,128]{1,0:T(8,128)(2,1)S(1)}, bf16[272,128]{1,0:T(8,128)(2,1)S(1)}, u32[]{:S(2)}, u32[]{:S(2)}) %collective-permute-start.1) | collective-permute-done | bytes 69664 | tf_op jit(solution)/shard_map/ppermute | solution.py:305
  15.5 0.0 collective-permute-done.2.sib_ref
  15.5 0.0 copy-start.6
  15.5 0.1 join.1
  15.6 2.5 %collective-permute-start.6 = (bf16[4,272,128]{2,1,0:T(8,128)(2,1)S(1)}, bf16[4,272,128]{2,1,0:T(8,128)(2,1)S(1)}, u32[]{:S(2)}, u32[]{:S(2)}) collective-permute-start(bf16[4,272,128]{2,1,0:T(8,128)(2,1)S(1)} %get-tuple-element.31.refs_0_), channel_id=1, source_target_pairs={{0,6},{2,4},{4,2},{6,0},{1,7},{3,5},{5,3},{7,1},{8,14},{10,12},{12... | collective-permute-start | bytes 835592 | tf_op jit(solution)/shard_map/ppermute | solution.py:305
  18.1 0.5 collective-permute-start.5
  18.6 0.5 collective-permute-start.4
  19.1 0.0 copy-done.6
  19.1 1.4 %collective-permute-start.11 = (f32[1,8,1024]{2,1,0:T(8,128)S(1)}, f32[1,8,1024]{2,1,0:T(8,128)S(1)}, u32[]{:S(2)}, u32[]{:S(2)}) collective-permute-start(f32[1,8,1024]{2,1,0:T(8,128)S(1)} %copy-done.6), channel_id=1, source_target_pairs={{0,8},{8,0},{16,24},{24,16},{1,9},{9,1},{17,25},{25,17},{2,10},{10... | collective-permute-start | bytes 98312 | tf_op jit(solution)/shard_map/ppermute | solution.py:305
  20.6 2.6 %collective-permute-start.8 = (bf16[2,256,128]{2,1,0:T(8,128)(2,1)S(1)}, bf16[2,256,128]{2,1,0:T(8,128)(2,1)S(1)}, u32[]{:S(2)}, u32[]{:S(2)}) collective-permute-start(bf16[2,256,128]{2,1,0:T(8,128)(2,1)S(1)} %get-tuple-element.32.refs_4_), channel_id=1, source_target_pairs={{0,16},{8,24},{16,0},{24,8},{1,17},{9,25},{17,1},{25,9},{2,18},{10... | collective-permute-start | bytes 393224 | tf_op jit(solution)/shard_map/ppermute | solution.py:305
  23.1 0.0 collective-permute-done.11.refs_11_
  23.1 1.3 %collective-permute-start.10 = (s32[2,13,8,128]{3,2,1,0:T(8,128)S(1)}, s32[2,13,8,128]{3,2,1,0:T(8,128)S(1)}, u32[]{:S(2)}, u32[]{:S(2)}) collective-permute-start(s32[2,13,8,128]{3,2,1,0:T(8,128)S(1)} %get-tuple-element.34.refs_8_), channel_id=1, source_target_pairs={{0,8},{8,0},{16,24},{24,16},{1,9},{9,1},{17,25},{25,17},{2,10},{10... | collective-permute-start | bytes 319496 | tf_op jit(solution)/shard_map/ppermute | solution.py:305
  24.5 5.3 %collective-permute-done.10.refs_9_ = s32[2,13,8,128]{3,2,1,0:T(8,128)S(1)} collective-permute-done((s32[2,13,8,128]{3,2,1,0:T(8,128)S(1)}, s32[2,13,8,128]{3,2,1,0:T(8,128)S(1)}, u32[]{:S(2)}, u32[]{:S(2)}) %collective-permute-start.10) | collective-permute-done | bytes 106528 | tf_op jit(solution)/shard_map/ppermute | solution.py:305
  29.8 2.7 %collective-permute-start.9 = (bf16[2,256,128]{2,1,0:T(8,128)(2,1)S(1)}, bf16[2,256,128]{2,1,0:T(8,128)(2,1)S(1)}, u32[]{:S(2)}, u32[]{:S(2)}) collective-permute-start(bf16[2,256,128]{2,1,0:T(8,128)(2,1)S(1)} %get-tuple-element.33), channel_id=1, source_target_pairs={{0,24},{8,16},{16,8},{24,0},{1,25},{9,17},{17,9},{25,1},{2,26},{10... | collective-permute-start | bytes 393224 | tf_op jit(solution)/shard_map/ppermute | solution.py:305
  32.5 0.0 collective-permute-done.8.refs_6_
  32.5 0.0 collective-permute-start.7
  32.5 4.1 %collective-permute-done.9.refs_7_ = bf16[2,256,128]{2,1,0:T(8,128)(2,1)S(1)} collective-permute-done((bf16[2,256,128]{2,1,0:T(8,128)(2,1)S(1)}, bf16[2,256,128]{2,1,0:T(8,128)(2,1)S(1)}, u32[]{:S(2)}, u32[]{:S(2)}) %collective-permute-start.9) | collective-permute-done | bytes 131104 | tf_op jit(solution)/shard_map/ppermute | solution.py:305
  36.6 1.3 %collective-permute-done.7.refs_5_ = bf16[2,256,128]{2,1,0:T(8,128)(2,1)S(1)} collective-permute-done((bf16[2,256,128]{2,1,0:T(8,128)(2,1)S(1)}, bf16[2,256,128]{2,1,0:T(8,128)(2,1)S(1)}, u32[]{:S(2)}, u32[]{:S(2)}) %collective-permute-start.7) | collective-permute-done | bytes 131104 | tf_op jit(solution)/shard_map/ppermute | solution.py:305
  38.0 0.0 collective-permute-done.6.refs_3_
  38.0 0.0 collective-permute-done.5.refs_2_
  38.0 0.0 collective-permute-done.4.refs_1_
  38.0 8.4 %pair.1 = (bf16[4,128,128]{2,1,0:T(8,128)(2,1)S(1)}, bf16[4,128,128]{2,1,0:T(8,128)(2,1)S(1)}, bf16[4,128,128]{2,1,0:T(8,128)(2,1)S(1)}, bf16[4,128,128]{2,1,0:T...) custom-call(bf16[4,272,128]{2,1,0:T(8,128)(2,1)S(1)} %get-tuple-elem, ...), custom_call_target="tpu_custom_call" | custom-call | tf_op jit(solution)/shard_map/pair/pallas_call | solution.py:373
  46.4 2.4 %collective-permute-start.12 = (bf16[4,128,128]{2,1,0:T(8,128)(2,1)S(1)}, bf16[4,128,128]{2,1,0:T(8,128)(2,1)S(1)}, u32[]{:S(2)}, u32[]{:S(2)}) collective-permute-start(bf16[4,128,128]{2,1,0:T(8,128)(2,1)S(1)} %get-tuple-element.36), channel_id=1, source_target_pairs={{0,2},{2,0},{4,6},{6,4},{1,3},{3,1},{5,7},{7,5},{8,10},{10,8},{12,... | collective-permute-start | bytes 393224 | tf_op jit(solution)/shard_map/ppermute | solution.py:305
  48.8 2.5 %collective-permute-start.13 = (bf16[4,128,128]{2,1,0:T(8,128)(2,1)S(1)}, bf16[4,128,128]{2,1,0:T(8,128)(2,1)S(1)}, u32[]{:S(2)}, u32[]{:S(2)}) collective-permute-start(bf16[4,128,128]{2,1,0:T(8,128)(2,1)S(1)} %get-tuple-element.37), channel_id=1, source_target_pairs={{0,4},{2,6},{4,0},{6,2},{1,5},{3,7},{5,1},{7,3},{8,12},{10,14},{12... | collective-permute-start | bytes 393224 | tf_op jit(solution)/shard_map/ppermute | solution.py:305
  51.3 1.4 %collective-permute-start.14 = (bf16[4,128,128]{2,1,0:T(8,128)(2,1)S(1)}, bf16[4,128,128]{2,1,0:T(8,128)(2,1)S(1)}, u32[]{:S(2)}, u32[]{:S(2)}) collective-permute-start(bf16[4,128,128]{2,1,0:T(8,128)(2,1)S(1)} %get-tuple-element.38), channel_id=1, source_target_pairs={{0,6},{2,4},{4,2},{6,0},{1,7},{3,5},{5,3},{7,1},{8,14},{10,12},{12... | collective-permute-start | bytes 393224 | tf_op jit(solution)/shard_map/ppermute | solution.py:305
  52.7 0.9 %collective-permute-start.16 = (bf16[2,256,128]{2,1,0:T(8,128)(2,1)S(1)}, bf16[2,256,128]{2,1,0:T(8,128)(2,1)S(1)}, u32[]{:S(2)}, u32[]{:S(2)}) collective-permute-start(bf16[2,256,128]{2,1,0:T(8,128)(2,1)S(1)} %get-tuple-element.42), channel_id=1, source_target_pairs={{0,8},{8,0},{16,24},{24,16},{1,9},{9,1},{17,25},{25,17},{2,10},{10... | collective-permute-start | bytes 393224 | tf_op jit(solution)/shard_map/ppermute | solution.py:305
  53.5 2.6 %collective-permute-start.17 = (bf16[2,256,128]{2,1,0:T(8,128)(2,1)S(1)}, bf16[2,256,128]{2,1,0:T(8,128)(2,1)S(1)}, u32[]{:S(2)}, u32[]{:S(2)}) collective-permute-start(bf16[2,256,128]{2,1,0:T(8,128)(2,1)S(1)} %get-tuple-element.43), channel_id=1, source_target_pairs={{0,16},{8,24},{16,0},{24,8},{1,17},{9,25},{17,1},{25,9},{2,18},{10... | collective-permute-start | bytes 393224 | tf_op jit(solution)/shard_map/ppermute | solution.py:305
  56.1 0.0 collective-permute-done.12.refs_1_
  56.1 0.9 %collective-permute-start.18 = (bf16[2,256,128]{2,1,0:T(8,128)(2,1)S(1)}, bf16[2,256,128]{2,1,0:T(8,128)(2,1)S(1)}, u32[]{:S(2)}, u32[]{:S(2)}) collective-permute-start(bf16[2,256,128]{2,1,0:T(8,128)(2,1)S(1)} %get-tuple-element.44), channel_id=1, source_target_pairs={{0,24},{8,16},{16,8},{24,0},{1,25},{9,17},{17,9},{25,1},{2,26},{10... | collective-permute-start | bytes 393224 | tf_op jit(solution)/shard_map/ppermute | solution.py:305
  57.1 0.0 collective-permute-done.13.refs_2_
  57.1 0.1 collective-permute-done.14.refs_3_
  57.1 0.1 query_sum.1
  57.2 0.9 %collective-permute-start.15 = (bf16[2,128,128]{2,1,0:T(8,128)(2,1)S(1)}, bf16[2,128,128]{2,1,0:T(8,128)(2,1)S(1)}, u32[]{:S(2)}, u32[]{:S(2)}) collective-permute-start(bf16[2,128,128]{2,1,0:T(8,128)(2,1)S(1)} %get-tuple-element.40), channel_id=1, source_target_pairs={{0,8},{8,0},{16,24},{24,16},{1,9},{9,1},{17,25},{25,17},{2,10},{10... | collective-permute-start | bytes 196616 | tf_op jit(solution)/shard_map/ppermute | solution.py:305
  58.2 1.0 %collective-permute-done.16.refs_3_ = bf16[2,256,128]{2,1,0:T(8,128)(2,1)S(1)} collective-permute-done((bf16[2,256,128]{2,1,0:T(8,128)(2,1)S(1)}, bf16[2,256,128]{2,1,0:T(8,128)(2,1)S(1)}, u32[]{:S(2)}, u32[]{:S(2)}) %collective-permute-start.16) | collective-permute-done | bytes 131104 | tf_op jit(solution)/shard_map/ppermute | solution.py:305
  59.2 1.9 %collective-permute-done.17.refs_4_ = bf16[2,256,128]{2,1,0:T(8,128)(2,1)S(1)} collective-permute-done((bf16[2,256,128]{2,1,0:T(8,128)(2,1)S(1)}, bf16[2,256,128]{2,1,0:T(8,128)(2,1)S(1)}, u32[]{:S(2)}, u32[]{:S(2)}) %collective-permute-start.17) | collective-permute-done | bytes 131104 | tf_op jit(solution)/shard_map/ppermute | solution.py:305
  61.1 2.0 %collective-permute-done.18.refs_5_ = bf16[2,256,128]{2,1,0:T(8,128)(2,1)S(1)} collective-permute-done((bf16[2,256,128]{2,1,0:T(8,128)(2,1)S(1)}, bf16[2,256,128]{2,1,0:T(8,128)(2,1)S(1)}, u32[]{:S(2)}, u32[]{:S(2)}) %collective-permute-start.18) | collective-permute-done | bytes 131104 | tf_op jit(solution)/shard_map/ppermute | solution.py:305
  63.0 0.1 collective-permute-done.15.refs_1_
  63.2 0.1 key_sum.1
  63.2 0.1 collective-permute-start.19
  63.3 1.4 %collective-permute-done.19.sib_ref = bf16[2,384,128]{2,1,0:T(8,128)(2,1)S(1)} collective-permute-done((bf16[2,384,128]{2,1,0:T(8,128)(2,1)S(1)}, bf16[2,384,128]{2,1,0:T(8,128)(2,1)S(1)}, u32[]{:S(2)}, u32[]{:S(2)}) %collective-permute-start.19) | collective-permute-done | bytes 196640 | tf_op jit(solution)/shard_map/ppermute | solution.py:305
  64.7 0.8 %finish.1 = (bf16[1,128,512]{2,1,0:T(8,128)(2,1)}, bf16[1,128,512]{2,1,0:T(8,128)(2,1)}, bf16[1,128,512]{2,1,0:T(8,128)(2,1)}) custom-call(bf16[2,384,128]{2,1,0:T(8,128)(2,1)S(1)} %get-tuple-element.45.own_ref, bf16[2,384,128]{2,1,0:T(8,128)(2,1)S(1)} %collective-permute-done.19.sib_ref), custom_call_target="tpu_custom_call" | custom-call | tf_op jit(solution)/shard_map/finish/pallas_call | solution.py:420
Async XLA Ops:
  0.6 0.7 %copy-start.7 = (s32[1,1,24]{2,1,0:T(1,128)S(1)}, s32[1,1,24]{2,1,0:T(1,128)}, u32[]{:S(2)}) copy-start(s32[1,1,24]{2,1,0:T(1,128)} %slot_ref.1) | copy-start | bytes 292
  1.3 0.9 %copy-start = (bf16[1,128,512]{2,1,0:T(8,128)(2,1)S(1)}, bf16[1,128,512]{2,1,0:T(8,128)(2,1)}, u32[]{:S(2)}) copy-start(bf16[1,128,512]{2,1,0:T(8,128)(2,1)} %q_hbm.1) | copy-start | bytes 393220
  2.2 0.9 %copy-start.1 = (bf16[1,128,512]{2,1,0:T(8,128)(2,1)S(1)}, bf16[1,128,512]{2,1,0:T(8,128)(2,1)}, u32[]{:S(2)}) copy-start(bf16[1,128,512]{2,1,0:T(8,128)(2,1)} %g_hbm.1) | copy-start | bytes 393220
  3.1 0.9 %copy-start.2 = (bf16[1,128,512]{2,1,0:T(8,128)(2,1)S(1)}, bf16[1,128,512]{2,1,0:T(8,128)(2,1)}, u32[]{:S(2)}) copy-start(bf16[1,128,512]{2,1,0:T(8,128)(2,1)} %o_hbm.1) | copy-start | bytes 393220
  4.0 0.9 %copy-start.3 = (bf16[1,128,512]{2,1,0:T(8,128)(2,1)S(1)}, bf16[1,128,512]{2,1,0:T(8,128)(2,1)}, u32[]{:S(2)}) copy-start(bf16[1,128,512]{2,1,0:T(8,128)(2,1)} %k_hbm.1) | copy-start | bytes 393220
  4.9 0.9 %copy-start.4 = (bf16[1,128,512]{2,1,0:T(8,128)(2,1)S(1)}, bf16[1,128,512]{2,1,0:T(8,128)(2,1)}, u32[]{:S(2)}) copy-start(bf16[1,128,512]{2,1,0:T(8,128)(2,1)} %v_hbm.1) | copy-start | bytes 393220
  5.8 0.9 %copy-start.5 = (s32[1,1,24,8,128]{4,3,2,1,0:T(8,128)S(1)}, s32[1,1,24,8,128]{4,3,2,1,0:T(8,128)}, u32[]{:S(2)}) copy-start(s32[1,1,24,8,128]{4,3,2,1,0:T(8,128)} %bits_hbm.1) | copy-start | bytes 294916
  8.2 7.3 %collective-permute-start.2 = (bf16[784,128]{1,0:T(8,128)(2,1)S(1)}, bf16[784,128]{1,0:T(8,128)(2,1)S(1)}, u32[]{:S(2)}, u32[]{:S(2)}) collective-permute-start(bf16[784,128]{1,0:T(8,128)(2,1)S(1)} %get-tuple-element.29), channel_id=1, source_target_pairs={{0,1},{1,0},{2,3},{3,2},{4,5},{5,4},{6,7},{7,6},{8,9},{9,8},{10,11... | collective-permute-start | bytes 602120 | tf_op jit(solution)/shard_map/ppermute | solution.py:305
  8.7 5.4 %collective-permute-start = (bf16[272,128]{1,0:T(8,128)(2,1)S(1)}, bf16[272,128]{1,0:T(8,128)(2,1)S(1)}, u32[]{:S(2)}, u32[]{:S(2)}) collective-permute-start(bf16[272,128]{1,0:T(8,128)(2,1)S(1)} %get-tuple-element.26), channel_id=1, source_target_pairs={{0,8},{1,9},{8,0},{9,1},{16,24},{17,25},{24,16},{25,17},{2,10},{3,... | collective-permute-start | bytes 208904 | tf_op jit(solution)/shard_map/ppermute | solution.py:305
  11.4 4.1 %collective-permute-start.1 = (bf16[272,128]{1,0:T(8,128)(2,1)S(1)}, bf16[272,128]{1,0:T(8,128)(2,1)S(1)}, u32[]{:S(2)}, u32[]{:S(2)}) collective-permute-start(bf16[272,128]{1,0:T(8,128)(2,1)S(1)} %get-tuple-element.27), channel_id=1, source_target_pairs={{0,9},{1,8},{8,1},{9,0},{16,25},{17,24},{24,17},{25,16},{2,11},{3,... | collective-permute-start | bytes 208904 | tf_op jit(solution)/shard_map/ppermute | solution.py:305
  11.4 1.2 %collective-permute-start.3 = (s32[13,8,128]{2,1,0:T(8,128)S(1)}, s32[13,8,128]{2,1,0:T(8,128)S(1)}, u32[]{:S(2)}, u32[]{:S(2)}) collective-permute-start(s32[13,8,128]{2,1,0:T(8,128)S(1)} %get-tuple-element.30.bits_own), channel_id=1, source_target_pairs={{0,1},{1,0},{2,3},{3,2},{4,5},{5,4},{6,7},{7,6},{8,9},{9,8},{10,11... | collective-permute-start | bytes 159752 | tf_op jit(solution)/shard_map/ppermute | solution.py:305
  15.5 3.6 %copy-start.6 = (f32[1,8,1024]{2,1,0:T(8,128)S(1)}, f32[1,8,1024]{2,1,0:T(8,128)}, u32[]{:S(2)}) copy-start(f32[1,8,1024]{2,1,0:T(8,128)} %refs_10_.1) | copy-start | bytes 98308
  15.6 22.4 %collective-permute-start.6 = (bf16[4,272,128]{2,1,0:T(8,128)(2,1)S(1)}, bf16[4,272,128]{2,1,0:T(8,128)(2,1)S(1)}, u32[]{:S(2)}, u32[]{:S(2)}) collective-permute-start(bf16[4,272,128]{2,1,0:T(8,128)(2,1)S(1)} %get-tuple-element.31.refs_0_), channel_id=1, source_target_pairs={{0,6},{2,4},{4,2},{6,0},{1,7},{3,5},{5,3},{7,1},{8,14},{10,12},{12... | collective-permute-start | bytes 835592 | tf_op jit(solution)/shard_map/ppermute | solution.py:305
  18.1 19.9 %collective-permute-start.5 = (bf16[4,272,128]{2,1,0:T(8,128)(2,1)S(1)}, bf16[4,272,128]{2,1,0:T(8,128)(2,1)S(1)}, u32[]{:S(2)}, u32[]{:S(2)}) collective-permute-start(bf16[4,272,128]{2,1,0:T(8,128)(2,1)S(1)} %get-tuple-element.31.refs_0_), channel_id=1, source_target_pairs={{0,4},{2,6},{4,0},{6,2},{1,5},{3,7},{5,1},{7,3},{8,12},{10,14},{12... | collective-permute-start | bytes 835592 | tf_op jit(solution)/shard_map/ppermute | solution.py:305
  18.6 19.4 %collective-permute-start.4 = (bf16[4,272,128]{2,1,0:T(8,128)(2,1)S(1)}, bf16[4,272,128]{2,1,0:T(8,128)(2,1)S(1)}, u32[]{:S(2)}, u32[]{:S(2)}) collective-permute-start(bf16[4,272,128]{2,1,0:T(8,128)(2,1)S(1)} %get-tuple-element.31.refs_0_), channel_id=1, source_target_pairs={{0,2},{2,0},{4,6},{6,4},{1,3},{3,1},{5,7},{7,5},{8,10},{10,8},{12,... | collective-permute-start | bytes 835592 | tf_op jit(solution)/shard_map/ppermute | solution.py:305
  19.1 4.0 %collective-permute-start.11 = (f32[1,8,1024]{2,1,0:T(8,128)S(1)}, f32[1,8,1024]{2,1,0:T(8,128)S(1)}, u32[]{:S(2)}, u32[]{:S(2)}) collective-permute-start(f32[1,8,1024]{2,1,0:T(8,128)S(1)} %copy-done.6), channel_id=1, source_target_pairs={{0,8},{8,0},{16,24},{24,16},{1,9},{9,1},{17,25},{25,17},{2,10},{10... | collective-permute-start | bytes 98312 | tf_op jit(solution)/shard_map/ppermute | solution.py:305
  20.6 11.9 %collective-permute-start.8 = (bf16[2,256,128]{2,1,0:T(8,128)(2,1)S(1)}, bf16[2,256,128]{2,1,0:T(8,128)(2,1)S(1)}, u32[]{:S(2)}, u32[]{:S(2)}) collective-permute-start(bf16[2,256,128]{2,1,0:T(8,128)(2,1)S(1)} %get-tuple-element.32.refs_4_), channel_id=1, source_target_pairs={{0,16},{8,24},{16,0},{24,8},{1,17},{9,25},{17,1},{25,9},{2,18},{10... | collective-permute-start | bytes 393224 | tf_op jit(solution)/shard_map/ppermute | solution.py:305
  23.1 6.6 %collective-permute-start.10 = (s32[2,13,8,128]{3,2,1,0:T(8,128)S(1)}, s32[2,13,8,128]{3,2,1,0:T(8,128)S(1)}, u32[]{:S(2)}, u32[]{:S(2)}) collective-permute-start(s32[2,13,8,128]{3,2,1,0:T(8,128)S(1)} %get-tuple-element.34.refs_8_), channel_id=1, source_target_pairs={{0,8},{8,0},{16,24},{24,16},{1,9},{9,1},{17,25},{25,17},{2,10},{10... | collective-permute-start | bytes 319496 | tf_op jit(solution)/shard_map/ppermute | solution.py:305
  29.8 6.8 %collective-permute-start.9 = (bf16[2,256,128]{2,1,0:T(8,128)(2,1)S(1)}, bf16[2,256,128]{2,1,0:T(8,128)(2,1)S(1)}, u32[]{:S(2)}, u32[]{:S(2)}) collective-permute-start(bf16[2,256,128]{2,1,0:T(8,128)(2,1)S(1)} %get-tuple-element.33), channel_id=1, source_target_pairs={{0,24},{8,16},{16,8},{24,0},{1,25},{9,17},{17,9},{25,1},{2,26},{10... | collective-permute-start | bytes 393224 | tf_op jit(solution)/shard_map/ppermute | solution.py:305
  32.5 5.5 %collective-permute-start.7 = (bf16[2,256,128]{2,1,0:T(8,128)(2,1)S(1)}, bf16[2,256,128]{2,1,0:T(8,128)(2,1)S(1)}, u32[]{:S(2)}, u32[]{:S(2)}) collective-permute-start(bf16[2,256,128]{2,1,0:T(8,128)(2,1)S(1)} %get-tuple-element.33), channel_id=1, source_target_pairs={{0,8},{8,0},{16,24},{24,16},{1,9},{9,1},{17,25},{25,17},{2,10},{10... | collective-permute-start | bytes 393224 | tf_op jit(solution)/shard_map/ppermute | solution.py:305
  46.4 9.7 %collective-permute-start.12 = (bf16[4,128,128]{2,1,0:T(8,128)(2,1)S(1)}, bf16[4,128,128]{2,1,0:T(8,128)(2,1)S(1)}, u32[]{:S(2)}, u32[]{:S(2)}) collective-permute-start(bf16[4,128,128]{2,1,0:T(8,128)(2,1)S(1)} %get-tuple-element.36), channel_id=1, source_target_pairs={{0,2},{2,0},{4,6},{6,4},{1,3},{3,1},{5,7},{7,5},{8,10},{10,8},{12,... | collective-permute-start | bytes 393224 | tf_op jit(solution)/shard_map/ppermute | solution.py:305
  48.8 8.3 %collective-permute-start.13 = (bf16[4,128,128]{2,1,0:T(8,128)(2,1)S(1)}, bf16[4,128,128]{2,1,0:T(8,128)(2,1)S(1)}, u32[]{:S(2)}, u32[]{:S(2)}) collective-permute-start(bf16[4,128,128]{2,1,0:T(8,128)(2,1)S(1)} %get-tuple-element.37), channel_id=1, source_target_pairs={{0,4},{2,6},{4,0},{6,2},{1,5},{3,7},{5,1},{7,3},{8,12},{10,14},{12... | collective-permute-start | bytes 393224 | tf_op jit(solution)/shard_map/ppermute | solution.py:305
  51.3 5.9 %collective-permute-start.14 = (bf16[4,128,128]{2,1,0:T(8,128)(2,1)S(1)}, bf16[4,128,128]{2,1,0:T(8,128)(2,1)S(1)}, u32[]{:S(2)}, u32[]{:S(2)}) collective-permute-start(bf16[4,128,128]{2,1,0:T(8,128)(2,1)S(1)} %get-tuple-element.38), channel_id=1, source_target_pairs={{0,6},{2,4},{4,2},{6,0},{1,7},{3,5},{5,3},{7,1},{8,14},{10,12},{12... | collective-permute-start | bytes 393224 | tf_op jit(solution)/shard_map/ppermute | solution.py:305
  52.7 6.5 %collective-permute-start.16 = (bf16[2,256,128]{2,1,0:T(8,128)(2,1)S(1)}, bf16[2,256,128]{2,1,0:T(8,128)(2,1)S(1)}, u32[]{:S(2)}, u32[]{:S(2)}) collective-permute-start(bf16[2,256,128]{2,1,0:T(8,128)(2,1)S(1)} %get-tuple-element.42), channel_id=1, source_target_pairs={{0,8},{8,0},{16,24},{24,16},{1,9},{9,1},{17,25},{25,17},{2,10},{10... | collective-permute-start | bytes 393224 | tf_op jit(solution)/shard_map/ppermute | solution.py:305
  53.5 7.5 %collective-permute-start.17 = (bf16[2,256,128]{2,1,0:T(8,128)(2,1)S(1)}, bf16[2,256,128]{2,1,0:T(8,128)(2,1)S(1)}, u32[]{:S(2)}, u32[]{:S(2)}) collective-permute-start(bf16[2,256,128]{2,1,0:T(8,128)(2,1)S(1)} %get-tuple-element.43), channel_id=1, source_target_pairs={{0,16},{8,24},{16,0},{24,8},{1,17},{9,25},{17,1},{25,9},{2,18},{10... | collective-permute-start | bytes 393224 | tf_op jit(solution)/shard_map/ppermute | solution.py:305
  56.1 6.9 %collective-permute-start.18 = (bf16[2,256,128]{2,1,0:T(8,128)(2,1)S(1)}, bf16[2,256,128]{2,1,0:T(8,128)(2,1)S(1)}, u32[]{:S(2)}, u32[]{:S(2)}) collective-permute-start(bf16[2,256,128]{2,1,0:T(8,128)(2,1)S(1)} %get-tuple-element.44), channel_id=1, source_target_pairs={{0,24},{8,16},{16,8},{24,0},{1,25},{9,17},{17,9},{25,1},{2,26},{10... | collective-permute-start | bytes 393224 | tf_op jit(solution)/shard_map/ppermute | solution.py:305
  57.2 5.9 %collective-permute-start.15 = (bf16[2,128,128]{2,1,0:T(8,128)(2,1)S(1)}, bf16[2,128,128]{2,1,0:T(8,128)(2,1)S(1)}, u32[]{:S(2)}, u32[]{:S(2)}) collective-permute-start(bf16[2,128,128]{2,1,0:T(8,128)(2,1)S(1)} %get-tuple-element.40), channel_id=1, source_target_pairs={{0,8},{8,0},{16,24},{24,16},{1,9},{9,1},{17,25},{25,17},{2,10},{10... | collective-permute-start | bytes 196616 | tf_op jit(solution)/shard_map/ppermute | solution.py:305
  63.2 1.5 %collective-permute-start.19 = (bf16[2,384,128]{2,1,0:T(8,128)(2,1)S(1)}, bf16[2,384,128]{2,1,0:T(8,128)(2,1)S(1)}, u32[]{:S(2)}, u32[]{:S(2)}) collective-permute-start(bf16[2,384,128]{2,1,0:T(8,128)(2,1)S(1)} %get-tuple-element.46), channel_id=1, source_target_pairs={{0,1},{1,0},{2,3},{3,2},{4,5},{5,4},{6,7},{7,6},{8,9},{9,8},{10,11... | collective-permute-start | bytes 589832 | tf_op jit(solution)/shard_map/ppermute | solution.py:305

commit v2 on v1

--- a/solution.py
+++ b/solution.py
@@ -19,7 +19,12 @@
 NT = (((1,), (1,)), ((), ()))
 NN = (((1,), (0,)), ((), ()))
 MEDIUM = pltpu.CompilerParams(vmem_limit_bytes=28 * 1024 * 1024)
+PACK = pltpu.CompilerParams(vmem_limit_bytes=int(53.4 * 1024 * 1024))
 SMALL = pltpu.CompilerParams(vmem_limit_bytes=12 * 1024 * 1024)
+def early(gigaflops):
+    return pl.CostEstimate(flops=gigaflops * 10**9, bytes_accessed=0, transcendentals=0)
+
+
 VMEM = pl.BlockSpec(memory_space=pltpu.VMEM)
 HBM = pl.BlockSpec(memory_space=pltpu.HBM)
 
@@ -88,35 +93,64 @@
         packed_ref[entry // 2, span] = words[:4] | lax.shift_left(words[4:], I32(16))
 
 
-def join_kernel(
-    krows, qg_own, qg_pair0, qg_pair1, kv_own, sib_ref, bits_own, bits_sib,
-    qg_out, kv_same, kv_pair, bits_out,
+def key_join_kernel(krows, kv_own, sib_ref, kv_same, kv_pair):
+    core = my_place()[2]
+    for side, ref in enumerate((kv_same, kv_pair)):
+        span = slice(side * 2 * krows, (side + 1) * 2 * krows)
+        ref[core] = kv_own[span]
+        ref[1 - core] = sib_ref[span]
+
+
+def query_join_kernel(
+    krows, tile, qg_own, sib_ref, qg_pair0, qg_pair1, bits_own, bits_pair, lse_own, lse_pair,
+    qg_out, bits_out, lse_out,
 ):
     row, chip, core, quarter = my_place()
+    side = row % 2
     qg_out[quarter] = qg_own[...]
     qg_out[quarter ^ 1] = sib_ref[4 * krows :]
     qg_out[quarter ^ 2] = qg_pair0[...]
     qg_out[quarter ^ 3] = qg_pair1[...]
-    for side, ref in enumerate((kv_same, kv_pair)):
-        span = slice(side * 2 * krows, (side + 1) * 2 * krows)
-        ref[core] = kv_own[span]
-        ref[1 - core] = sib_ref[span]
-    bits_out[core] = bits_own[...]
-    bits_out[1 - core] = bits_sib[...]
+    bits_out[side] = bits_own[...]
+    bits_out[1 - side] = bits_pair[...]
+    for step, ref in enumerate((lse_own, lse_pair)):
+        every = ref[0] * LOG2E
+        own = every[:2]
+        for index in range(1, QUARTERS):
+            own = jnp.where(quarter == index, every[2 * index : 2 * index + 2], own)
+        for u in range(lse_out.shape[1]):
+            lse_out[side ^ step, u] = own[:, u * tile : (u + 1) * tile]
+
+
+def key_place_kernel(head_dim, tile, *refs):
+    kv_refs, (k_out, v_out, k2t_out) = refs[:-3], refs[-3:]
+    krows = kv_refs[0].shape[1] // 2
+    row = my_place()[0]
+    for step, ref in enumerate(kv_refs):
+        start = (row ^ step) * krows
+        inner = pl.multiple_of(start % tile, krows)
+        for block in range(2):
+            k_out[block, start // tile, pl.ds(inner, krows)] = ref[block, :krows]
+            v_out[block, start // tile, pl.ds(inner, krows)] = ref[block, krows:]
+    low_row = lax.broadcasted_iota(I32, (LANES, tile), 0) < head_dim
+    none_t = jnp.zeros((LANES, tile), BF16)
+    for block in range(2):
+        for w in range(k_out.shape[1]):
+            flipped = k_out[block, w].T
+            k2t_out[block, w] = jnp.concatenate(
+                [jnp.where(low_row, flipped, none_t), jnp.where(low_row, none_t, flipped)], axis=1
+            )
 
 
 def pair_kernel(sizes, *refs):
     head_dim, tile, capacity, chips, row_count = sizes
     qg_refs, refs = refs[:chips], refs[chips:]
-    kv_refs, refs = refs[:row_count], refs[row_count:]
-    bits_refs, refs = refs[:2], refs[2:]
-    lse_refs, refs = refs[:2], refs[2:]
-    dq_refs, refs = refs[:chips], refs[chips:]
-    dkv_refs, refs = refs[:row_count], refs[row_count:]
-    (q2_scr, g2_scr, q2t_scr, g2t_scr, k_scr, v_scr, k2t_scr, lse_scr, delta_scr,
-     dqt_scr, dk_scr, dv_scr, dq_scr, info, sems) = refs
+    (k_scr, v_scr, k2t_scr), refs = refs[:3], refs[3:]
+    bits_refs, lse_ref, refs = refs[:2], refs[2], refs[3:]
+    dqt_ref, dkv_refs, refs = refs[0], refs[1 : 1 + row_count], refs[1 + row_count :]
+    q2_scr, g2_scr, delta_scr, dqt_scr, dk_scr, dv_scr, info, sems = refs
     rows = (qg_refs[0].shape[1] - PAD) // 2
-    krows = kv_refs[0].shape[1] // 2
+    krows = dkv_refs[0].shape[1] // 2
     query_tiles = q2_scr.shape[1]
     key_tiles = k_scr.shape[1]
     scaling = float(head_dim) ** -0.5
@@ -125,20 +159,13 @@
 
     copies = [
         pltpu.make_async_copy(
-            bits_refs[i // 2].at[i % 2, capacity // 2], info.at[i], sems.at[i]
+            bits_refs[i % 2].at[i // 2, capacity // 2], info.at[i], sems.at[i]
         )
         for i in range(QUARTERS)
     ]
     for copy in copies:
         copy.start()
 
-    for step, ref in enumerate(lse_refs):
-        every = ref[0] * LOG2E
-        own = every[:2]
-        for index in range(1, QUARTERS):
-            own = jnp.where(quarter == index, every[2 * index : 2 * index + 2], own)
-        for u in range(query_tiles):
-            lse_scr[side ^ step, u] = own[:, u * tile : (u + 1) * tile]
     low = lax.broadcasted_iota(I32, (rows, LANES), 1) < head_dim
     none = jnp.zeros((rows, LANES), BF16)
     for step in range(chips):
@@ -160,26 +187,6 @@
                     @pl.when(source % (tile // rows) == part)
                     def _(part=part, delta=delta, u=u, block=block):
                         delta_scr[block, u, :, part * rows : (part + 1) * rows] = delta
-    for step in range(row_count):
-        start = (row ^ step) * krows
-        inner = pl.multiple_of(start % tile, krows)
-        for block in range(2):
-            k_scr[block, start // tile, pl.ds(inner, krows)] = kv_refs[step][block, :krows]
-            v_scr[block, start // tile, pl.ds(inner, krows)] = kv_refs[step][block, krows:]
-    low_row = lax.broadcasted_iota(I32, (LANES, tile), 0) < head_dim
-    none_t = jnp.zeros((LANES, tile), BF16)
-    for block in range(2):
-        for w in range(key_tiles):
-            flipped = k_scr[block, w].T
-            k2t_scr[block, w] = jnp.concatenate(
-                [jnp.where(low_row, flipped, none_t), jnp.where(low_row, none_t, flipped)], axis=1
-            )
-    for block in range(2):
-        for u in range(query_tiles):
-            for part in range(2):
-                lanes = slice(part * tile, (part + 1) * tile)
-                q2t_scr[block, u, :, lanes] = q2_scr[block, u, part].T
-                g2t_scr[block, u, :, lanes] = g2_scr[block, u, part].T
     dqt_scr[...] = jnp.zeros_like(dqt_scr)
     dk_scr[...] = jnp.zeros_like(dk_scr)
     dv_scr[...] = jnp.zeros_like(dv_scr)
@@ -190,12 +197,12 @@
         copy.wait()
 
     for step in range(QUARTERS):
-        qb = side ^ (step // 2)
-        kb = step % 2
+        qb = step // 2
+        kb = core ^ (step % 2)
         live = info[step, 1, 0]
 
         def two_tiles(index, _, step=step, qb=qb, kb=kb, live=live):
-            both = bits_refs[step // 2][kb, index]
+            both = bits_refs[step % 2][qb, index]
             second = jnp.where(index * 2 + 1 < live, I32(-1), I32(0))
             work = []
             for part in range(2):
@@ -209,16 +216,12 @@
                 edge = (jnp.concatenate([words, words], axis=0) & bit) != 0
                 q2 = q2_scr[qb, u].reshape(2 * tile, LANES)
                 g2 = g2_scr[qb, u].reshape(2 * tile, LANES)
-                scores = lax.dot_general(
-                    k_scr[kb, w], q2t_scr[qb, u], NN, preferred_element_type=F32
-                )
-                grad_prob = lax.dot_general(
-                    v_scr[kb, w], g2t_scr[qb, u], NN, preferred_element_type=F32
-                )
+                scores = lax.dot_general(k_scr[kb, w], q2, NT, preferred_element_type=F32)
+                grad_prob = lax.dot_general(v_scr[kb, w], g2, NT, preferred_element_type=F32)
                 work.append((u, w, edge, q2, g2, scores, grad_prob))
             done = []
             for u, w, edge, q2, g2, scores, grad_prob in work:
-                lse_tile = lse_scr[qb, u]
+                lse_tile = lse_ref[qb, u]
                 delta_tile = delta_scr[qb, u]
                 probs, grads = [], []
                 for h in range(2):
@@ -257,13 +260,20 @@
             dv = dv_scr[block, start // tile, pl.ds(inner, krows)]
             dkv_refs[step][block, :krows] = dk.astype(BF16)
             dkv_refs[step][block, krows:] = dv.astype(BF16)
+    dqt_ref[...] = (dqt_scr[...] * scaling).astype(BF16)
+
+
+def turn_kernel(rows, dqt_ref, *refs):
+    dq_refs, dq_scr = refs[:-1], refs[-1]
+    tile = dqt_ref.shape[3]
+    chip = my_place()[1]
     for block in range(2):
-        for u in range(query_tiles):
-            dq_scr[block, u * tile : (u + 1) * tile] = (dqt_scr[block, u] * scaling).astype(BF16).T
-    for step in range(chips):
+        for u in range(dqt_ref.shape[1]):
+            dq_scr[block, u * tile : (u + 1) * tile] = dqt_ref[block, u].T
+    for step, ref in enumerate(dq_refs):
         for index in range(QUARTERS):
             start = pl.multiple_of(((chip ^ step) * 2 + index % 2) * rows, rows)
-            dq_refs[step][index] = dq_scr[index // 2, pl.ds(start, rows)]
+            ref[index] = dq_scr[index // 2, pl.ds(start, rows)]
 
 
 def query_sum_kernel(chips, *refs):
@@ -279,26 +289,32 @@
 
 
 def key_sum_kernel(row_count, *refs):
-    (dq_same, dq_pair), dkv_refs, (own_ref, sib_ref) = refs[:2], refs[2:-2], refs[-2:]
-    krows2 = dkv_refs[0].shape[1]
+    dkv_refs, (own_ref, sib_ref) = refs[:-2], refs[-2:]
     core = my_place()[2]
     for ref, block in ((own_ref, core), (sib_ref, 1 - core)):
-        for side, dq in enumerate((dq_same, dq_pair)):
+        for side in range(2):
             total = dkv_refs[side][block].astype(F32)
             for other in range(side + 2, row_count, 2):
                 total += dkv_refs[other][block].astype(F32)
-            ref[side, :krows2] = total.astype(BF16)
-            ref[side, krows2:] = dq[block]
-
-
-def finish_kernel(krows, own_ref, sib_ref, dq_out, dk_out, dv_out):
-    quarter = my_place()[3]
-    for core, ref in enumerate((own_ref, sib_ref)):
-        for side in range(2):
-            lanes = lanes_of(quarter ^ (2 * side + core))
+            ref[side] = total.astype(BF16)
+
+
+def bundle_kernel(dkv_ref, dq_same, dq_pair, out):
+    krows2 = dkv_ref.shape[1]
+    sibling = 1 - my_place()[2]
+    out[:, :krows2] = dkv_ref[...]
+    for side, dq in enumerate((dq_same, dq_pair)):
+        out[side, krows2:] = dq[sibling]
+
+
+def finish_kernel(krows, dkv_own, dq_same, dq_pair, sib_ref, dq_out, dk_out, dv_out):
+    row, chip, core, quarter = my_place()
+    for side, dq in enumerate((dq_same, dq_pair)):
+        for step, ref in enumerate((dkv_own, sib_ref)):
+            lanes = lanes_of(quarter ^ (2 * side + step))
             dk_out[0, :, lanes] = ref[side, :krows]
             dv_out[0, :, lanes] = ref[side, krows : 2 * krows]
-            dq_out[0, :, lanes] = ref[side, 2 * krows :]
+            dq_out[0, :, lanes] = ref[side, 2 * krows :] if step else dq[core]
 
 
 def send(block, axes, count, step):
@@ -343,60 +359,84 @@
             pltpu.VMEM((QUARTERS, PAD, rows), BF16),
             pltpu.SemaphoreType.DMA((6,)),
         ],
-        compiler_params=SMALL,
+        compiler_params=PACK,
         name="pack",
     )(queries, grad_out, outputs, keys, values, tile_bits, tile_slot, tile_live)
 
     qg_pair0 = send(qg_pair0, line, places, 2)
     qg_pair1 = send(qg_pair1, line, places, 3)
     from_sibling = send(to_sibling, "core", cores, 1)
-    bits_sibling = send(bits_own, "core", cores, 1)
-    lse_other = send(lse, "row", row_count, 1)
-    qg, kv_same, kv_pair, bits = pl.pallas_call(
-        functools.partial(join_kernel, krows),
-        out_shape=(
-            shape(QUARTERS, 2 * rows + PAD, LANES), kv_shape, kv_shape,
-            shape(2, capacity // 2 + 1, 8, LANES, dtype=I32),
-        ),
-        in_specs=[VMEM] * 7,
-        out_specs=(VMEM,) * 4,
-        compiler_params=SMALL,
-        name="join",
-    )(qg_own, qg_pair0, qg_pair1, kv_own, from_sibling, bits_own, bits_sibling)
+    bits_pair = send(bits_own, "row", row_count, 1)
+    lse_pair = send(lse, "row", row_count, 1)
+    kv_same, kv_pair = pl.pallas_call(
+        functools.partial(key_join_kernel, krows),
+        out_shape=(kv_shape, kv_shape),
+        in_specs=[VMEM] * 2,
+        out_specs=(VMEM,) * 2,
+        compiler_params=SMALL,
+        name="key_join",
+    )(kv_own, from_sibling)
     kv_out = (kv_same, kv_pair)
     kv = [kv_same] + [
         send(kv_out[step % 2], "row", row_count, step) for step in range(1, row_count)
     ]
-    bits_other = send(bits, "row", row_count, 1)
+    qg, bits, lse2 = pl.pallas_call(
+        functools.partial(query_join_kernel, krows, tile),
+        out_shape=(
+            shape(QUARTERS, 2 * rows + PAD, LANES),
+            shape(2, capacity // 2 + 1, 8, LANES, dtype=I32),
+            shape(2, query_tiles, 2, tile, dtype=F32),
+        ),
+        in_specs=[VMEM] * 8,
+        out_specs=(VMEM,) * 3,
+        compiler_params=SMALL,
+        cost_estimate=early(20),
+        name="query_join",
+    )(qg_own, from_sibling, qg_pair0, qg_pair1, bits_own, bits_pair, lse, lse_pair)
     qg = [qg] + [send(qg, "chip", chips, step) for step in range(1, chips)]
-
+    bits_sibling = send(bits, "core", cores, 1)
+
+    placed = pl.pallas_call(
+        functools.partial(key_place_kernel, head_dim, tile),
+        out_shape=(
+            shape(2, key_tiles, tile, LANES), shape(2, key_tiles, tile, LANES),
+            shape(2, key_tiles, LANES, 2 * tile),
+        ),
+        in_specs=[VMEM] * row_count,
+        out_specs=(VMEM,) * 3,
+        compiler_params=SMALL,
+        cost_estimate=early(20),
+        name="key_place",
+    )(*kv)
     parts = pl.pallas_call(
         functools.partial(pair_kernel, (head_dim, tile, capacity, chips, row_count)),
-        out_shape=(shape(QUARTERS, rows, LANES),) * chips + (kv_shape,) * row_count,
-        in_specs=[VMEM] * (chips + row_count + 4),
-        out_specs=(VMEM,) * (chips + row_count),
+        out_shape=(shape(2, query_tiles, LANES, tile),) + (kv_shape,) * row_count,
+        in_specs=[VMEM] * (chips + 6),
+        out_specs=(VMEM,) * (1 + row_count),
         scratch_shapes=[
             pltpu.VMEM((2, query_tiles, 2, tile, LANES), BF16),
             pltpu.VMEM((2, query_tiles, 2, tile, LANES), BF16),
-            pltpu.VMEM((2, query_tiles, LANES, 2 * tile), BF16),
-            pltpu.VMEM((2, query_tiles, LANES, 2 * tile), BF16),
-            pltpu.VMEM((2, key_tiles, tile, LANES), BF16),
-            pltpu.VMEM((2, key_tiles, tile, LANES), BF16),
-            pltpu.VMEM((2, key_tiles, LANES, 2 * tile), BF16),
-            pltpu.VMEM((2, query_tiles, 2, tile), F32),
             pltpu.VMEM((2, query_tiles, PAD, tile), F32),
             pltpu.VMEM((2, query_tiles, LANES, tile), F32),
             pltpu.VMEM((2, key_tiles, tile, LANES), F32),
             pltpu.VMEM((2, key_tiles, tile, LANES), F32),
-            pltpu.VMEM((2, query_tiles * tile, LANES), BF16),
             pltpu.SMEM((QUARTERS, 8, LANES), I32),
             pltpu.SemaphoreType.DMA((QUARTERS,)),
         ],
         compiler_params=MEDIUM,
         name="pair",
-    )(*qg, *kv, bits, bits_other, lse, lse_other)
-
-    dq, dkv = parts[:chips], parts[chips:]
+    )(*qg, *placed, bits, bits_sibling, lse2)
+
+    dkv = parts[1:]
+    dq = pl.pallas_call(
+        functools.partial(turn_kernel, rows),
+        out_shape=(shape(QUARTERS, rows, LANES),) * chips,
+        in_specs=[VMEM],
+        out_specs=(VMEM,) * chips,
+        scratch_shapes=[pltpu.VMEM((2, query_tiles * tile, LANES), BF16)],
+        compiler_params=SMALL,
+        name="turn",
+    )(parts[0])
     dq = [dq[0]] + [send(dq[step], "chip", chips, step) for step in range(1, chips)]
     dkv = [dkv[0]] + [send(dkv[step], "row", row_count, step) for step in range(1, row_count)]
     dq_same, dq_pair = pl.pallas_call(
@@ -408,23 +448,32 @@
         name="query_sum",
     )(*dq)
     dq_pair = send(dq_pair, "row", row_count, 1)
-    own, to_sibling = pl.pallas_call(
+    dkv_own, dkv_sibling = pl.pallas_call(
         functools.partial(key_sum_kernel, row_count),
-        out_shape=(shape(2, 2 * krows + rows, LANES),) * 2,
-        in_specs=[VMEM] * (2 + row_count),
+        out_shape=(kv_shape,) * 2,
+        in_specs=[VMEM] * row_count,
         out_specs=(VMEM,) * 2,
         compiler_params=SMALL,
+        cost_estimate=early(20),
         name="key_sum",
-    )(dq_same, dq_pair, *dkv)
+    )(*dkv)
+    to_sibling = pl.pallas_call(
+        bundle_kernel,
+        out_shape=shape(2, 2 * krows + rows, LANES),
+        in_specs=[VMEM] * 3,
+        out_specs=VMEM,
+        compiler_params=SMALL,
+        name="bundle",
+    )(dkv_sibling, dq_same, dq_pair)
     from_sibling = send(to_sibling, "core", cores, 1)
     return pl.pallas_call(
         functools.partial(finish_kernel, krows),
         out_shape=(shape(1, rows, width), shape(1, krows, width), shape(1, krows, width)),
-        in_specs=[VMEM] * 2,
+        in_specs=[VMEM] * 4,
         out_specs=(VMEM,) * 3,
         compiler_params=SMALL,
         name="finish",
-    )(own, from_sibling)
+    )(dkv_own, dq_same, dq_pair, from_sibling)
 
 
 def solution(mesh):

time: 66.3 us -> 63.6 us (0.959)
  local copies, waits for them, and re-layouts: 5.41 us -> 0.89 us
  Pallas kernels: 10.9 us -> 12.5 us
  starting transfers between devices: 26.6 us -> 27.7 us
  waiting for transfers between devices: 21.2 us -> 20.4 us
    unnamed x16 -> x6, local copies, waits for them, and re-layouts: 5.41 us -> 0.89 us
    ppermute x20, starting transfers between devices: 26.6 us -> 27.7 us  [send(): lax.ppermute(block, axes, [(place, place ^ step) for place in range(count)])]
    pallas_call x1, Pallas kernels: 1.46 us -> 2.35 us  [body(): pl.pallas_call(functools.partial(pack_kernel, heads), out_shape=(qg_shape...]
    ppermute x20, waiting for transfers between devices: 21.2 us -> 20.4 us  [send(): lax.ppermute(block, axes, [(place, place ^ step) for place in range(count)])]
  transfers between devices with their start and end apart: 20 -> 20, of which waited for: 12 -> 8; matrix products, arithmetic and copies ran while one was open for 0% -> 0% of each run, Pallas kernels for 0% -> 1%
where the time goes in v2:
time: 63.6 us; the launch traced here: 63 us
  starting transfers between devices  27.7 us (44%)
  waiting for transfers between devices  20.4 us (32%)
  Pallas kernels  12.5 us (20%)
  between operations  1.42 us (2%)
  local copies, waits for them, and re-layouts  0.89 us (1%)
    ppermute x20, starting transfers between devices, send(): lax.ppermute(block, axes, [(place, place ^ step) for place in range(count)])  27.7 us
    ppermute x20, waiting for transfers between devices, send(): lax.ppermute(block, axes, [(place, place ^ step) for place in range(count)])  20.4 us
    pallas_call x1, Pallas kernels, body(): pl.pallas_call(functools.partial(pair_kernel, (head_dim, tile, capacity,...  8.72 us
    pallas_call x1, Pallas kernels, body(): pl.pallas_call(functools.partial(pack_kernel, heads), out_shape=(qg_shape...  2.35 us
  transfers between devices with their start and end apart: 20, of which 8 were waited for; matrix products, arithmetic and copies ran while one was open for 0% of the time, Pallas kernels for 1%

profile of v2, /device:TPU:0, one launch (start us, length us, event | category | flops | bytes accessed | tf_op | source)
XLA Modules:
  0.0 63.0 jit_solution(6722492253612518480)
XLA Ops:
  0.6 0.0 copy-start.1
  1.3 0.0 copy-done.1
  1.3 0.0 copy-start
  1.3 0.9 %copy-done = s32[1,1,24,8,128]{4,3,2,1,0:T(8,128)S(1)} copy-done((s32[1,1,24,8,128]{4,3,2,1,0:T(8,128)S(1)}, s32[1,1,24,8,128]{4,3,2,1,0:T(8,128)}, u32[]{:S(2)}) %copy-start) | copy-done | bytes 98328
  2.2 0.0 copy-start.2
  2.2 2.4 %pack.1 = (bf16[272,128]{1,0:T(8,128)(2,1)S(1)}, bf16[272,128]{1,0:T(8,128)(2,1)S(1)}, bf16[272,128]{1,0:T(8,128)(2,1)S(1)}, bf16[512,128]{1,0:T(8,128)(2,1)S(1)...) custom-call(bf16[1,128,512]{2,1,0:T(8,128)(2,1)} %q_hbm.1, bf16[1,128,512]{2,1,0:T(8,128)(2,1)} %g_hbm.1, ...), custom_call_target="tpu_custom_call" | custom-call | tf_op jit(solution)/shard_map/pack/pallas_call | solution.py:343
  4.6 0.5 collective-permute-start
  5.1 2.7 %collective-permute-start.1 = (bf16[272,128]{1,0:T(8,128)(2,1)S(1)}, bf16[272,128]{1,0:T(8,128)(2,1)S(1)}, u32[]{:S(2)}, u32[]{:S(2)}) collective-permute-start(bf16[272,128]{1,0:T(8,128)(2,1)S(1)} %get-tuple-element.32), channel_id=1, source_target_pairs={{0,8},{1,9},{8,0},{9,1},{16,24},{17,25},{24,16},{25,17},{2,10},{3,... | collective-permute-start | bytes 208904 | tf_op jit(solution)/shard_map/ppermute | solution.py:321
  7.7 0.1 collective-permute-start.2
  7.8 1.7 %collective-permute-start.3 = (s32[13,8,128]{2,1,0:T(8,128)S(1)}, s32[13,8,128]{2,1,0:T(8,128)S(1)}, u32[]{:S(2)}, u32[]{:S(2)}) collective-permute-start(s32[13,8,128]{2,1,0:T(8,128)S(1)} %get-tuple-element.34.bits_own), channel_id=1, source_target_pairs={{0,8},{8,0},{16,24},{24,16},{1,9},{9,1},{17,25},{25,17},{2,10},{10... | collective-permute-start | bytes 159752 | tf_op jit(solution)/shard_map/ppermute | solution.py:321
  9.5 0.0 copy-done.2
  9.6 0.3 collective-permute-start.4
  9.8 0.0 collective-permute-done.sib_ref
  9.9 3.8 %collective-permute-start.10 = (bf16[2,256,128]{2,1,0:T(8,128)(2,1)S(1)}, bf16[2,256,128]{2,1,0:T(8,128)(2,1)S(1)}, u32[]{:S(2)}, u32[]{:S(2)}) collective-permute-start(bf16[2,256,128]{2,1,0:T(8,128)(2,1)S(1)} %get-tuple-element.38), channel_id=1, source_target_pairs={{0,24},{8,16},{16,8},{24,0},{1,25},{9,17},{17,9},{25,1},{2,26},{10... | collective-permute-start | bytes 393224 | tf_op jit(solution)/shard_map/ppermute | solution.py:321
  13.7 0.4 collective-permute-done.4.lse_pair
  14.1 1.5 %collective-permute-start.8 = (bf16[2,256,128]{2,1,0:T(8,128)(2,1)S(1)}, bf16[2,256,128]{2,1,0:T(8,128)(2,1)S(1)}, u32[]{:S(2)}, u32[]{:S(2)}) collective-permute-start(bf16[2,256,128]{2,1,0:T(8,128)(2,1)S(1)} %get-tuple-element.38), channel_id=1, source_target_pairs={{0,8},{8,0},{16,24},{24,16},{1,9},{9,1},{17,25},{25,17},{2,10},{10... | collective-permute-start | bytes 393224 | tf_op jit(solution)/shard_map/ppermute | solution.py:321
  15.6 0.0 collective-permute-done.3.bits_pair
  15.6 2.6 %collective-permute-start.9 = (bf16[2,256,128]{2,1,0:T(8,128)(2,1)S(1)}, bf16[2,256,128]{2,1,0:T(8,128)(2,1)S(1)}, u32[]{:S(2)}, u32[]{:S(2)}) collective-permute-start(bf16[2,256,128]{2,1,0:T(8,128)(2,1)S(1)} %get-tuple-element.37.refs_0_), channel_id=1, source_target_pairs={{0,16},{8,24},{16,0},{24,8},{1,17},{9,25},{17,1},{25,9},{2,18},{10... | collective-permute-start | bytes 393224 | tf_op jit(solution)/shard_map/ppermute | solution.py:321
  18.2 0.0 collective-permute-done.1.qg_pair0
  18.2 0.0 collective-permute-done.2.qg_pair1
  18.2 0.1 query_join.1
  18.3 2.5 %collective-permute-start.7 = (bf16[4,272,128]{2,1,0:T(8,128)(2,1)S(1)}, bf16[4,272,128]{2,1,0:T(8,128)(2,1)S(1)}, u32[]{:S(2)}, u32[]{:S(2)}) collective-permute-start(bf16[4,272,128]{2,1,0:T(8,128)(2,1)S(1)} %get-tuple-element.35.refs_0_), channel_id=1, source_target_pairs={{0,6},{2,4},{4,2},{6,0},{1,7},{3,5},{5,3},{7,1},{8,14},{10,12},{12... | collective-permute-start | bytes 835592 | tf_op jit(solution)/shard_map/ppermute | solution.py:321
  20.8 0.5 collective-permute-start.6
  21.3 3.4 %collective-permute-done.9.refs_2_ = bf16[2,256,128]{2,1,0:T(8,128)(2,1)S(1)} collective-permute-done((bf16[2,256,128]{2,1,0:T(8,128)(2,1)S(1)}, bf16[2,256,128]{2,1,0:T(8,128)(2,1)S(1)}, u32[]{:S(2)}, u32[]{:S(2)}) %collective-permute-start.9) | collective-permute-done | bytes 131104 | tf_op jit(solution)/shard_map/ppermute | solution.py:321
  24.7 1.5 %collective-permute-start.5 = (bf16[4,272,128]{2,1,0:T(8,128)(2,1)S(1)}, bf16[4,272,128]{2,1,0:T(8,128)(2,1)S(1)}, u32[]{:S(2)}, u32[]{:S(2)}) collective-permute-start(bf16[4,272,128]{2,1,0:T(8,128)(2,1)S(1)} %get-tuple-element.35.refs_0_), channel_id=1, source_target_pairs={{0,2},{2,0},{4,6},{6,4},{1,3},{3,1},{5,7},{7,5},{8,10},{10,8},{12,... | collective-permute-start | bytes 835592 | tf_op jit(solution)/shard_map/ppermute | solution.py:321
  26.2 0.0 collective-permute-done.10.refs_3_
  26.2 0.0 collective-permute-start.11
  26.2 0.0 collective-permute-done.8.refs_1_
  26.2 0.2 key_place.1
  26.4 1.1 %collective-permute-done.11.refs_8_ = s32[2,13,8,128]{3,2,1,0:T(8,128)S(1)} collective-permute-done((s32[2,13,8,128]{3,2,1,0:T(8,128)S(1)}, s32[2,13,8,128]{3,2,1,0:T(8,128)S(1)}, u32[]{:S(2)}, u32[]{:S(2)}) %collective-permute-start.11) | collective-permute-done | bytes 106528 | tf_op jit(solution)/shard_map/ppermute | solution.py:321
  27.5 1.3 %collective-permute-done.7.refs_3_ = bf16[4,272,128]{2,1,0:T(8,128)(2,1)S(1)} collective-permute-done((bf16[4,272,128]{2,1,0:T(8,128)(2,1)S(1)}, bf16[4,272,128]{2,1,0:T(8,128)(2,1)S(1)}, u32[]{:S(2)}, u32[]{:S(2)}) %collective-permute-start.7) | collective-permute-done | bytes 278560 | tf_op jit(solution)/shard_map/ppermute | solution.py:321
  28.9 4.0 %collective-permute-done.6.refs_2_ = bf16[4,272,128]{2,1,0:T(8,128)(2,1)S(1)} collective-permute-done((bf16[4,272,128]{2,1,0:T(8,128)(2,1)S(1)}, bf16[4,272,128]{2,1,0:T(8,128)(2,1)S(1)}, u32[]{:S(2)}, u32[]{:S(2)}) %collective-permute-start.6) | collective-permute-done | bytes 278560 | tf_op jit(solution)/shard_map/ppermute | solution.py:321
  32.9 0.1 collective-permute-done.5.refs_1_
  33.0 8.7 %pair.1 = (bf16[2,8,128,128]{3,2,1,0:T(8,128)(2,1)S(1)}, bf16[2,256,128]{2,1,0:T(8,128)(2,1)S(1)}, bf16[2,256,128]{2,1,0:T(8,128)(2,1)S(1)}, bf16[2,256,128]{2,1,0:T(8,128)(2,1)S(1)}, bf16[2,256,128]{2,1,0:T(8,128)(2,1)S(1)}) custom-call(bf16[4,272,128]{2,1,0:T(8,128)(2,1)S(1)} %get-tuple-element.35.refs_0_, ...), custom_call_target="tpu_custom_call" | custom-call | tf_op jit(solution)/shard_map/pair/pallas_call | solution.py:411
  41.7 0.2 turn.1
  41.9 0.1 collective-permute-start.15
  42.0 1.1 %collective-permute-start.16 = (bf16[4,128,128]{2,1,0:T(8,128)(2,1)S(1)}, bf16[4,128,128]{2,1,0:T(8,128)(2,1)S(1)}, u32[]{:S(2)}, u32[]{:S(2)}) collective-permute-start(bf16[4,128,128]{2,1,0:T(8,128)(2,1)S(1)} %get-tuple-element.52), channel_id=1, source_target_pairs={{0,4},{2,6},{4,0},{6,2},{1,5},{3,7},{5,1},{7,3},{8,12},{10,14},{12... | collective-permute-start | bytes 393224 | tf_op jit(solution)/shard_map/ppermute | solution.py:321
  43.1 2.4 %collective-permute-start.17 = (bf16[4,128,128]{2,1,0:T(8,128)(2,1)S(1)}, bf16[4,128,128]{2,1,0:T(8,128)(2,1)S(1)}, u32[]{:S(2)}, u32[]{:S(2)}) collective-permute-start(bf16[4,128,128]{2,1,0:T(8,128)(2,1)S(1)} %get-tuple-element.53), channel_id=1, source_target_pairs={{0,6},{2,4},{4,2},{6,0},{1,7},{3,5},{5,3},{7,1},{8,14},{10,12},{12... | collective-permute-start | bytes 393224 | tf_op jit(solution)/shard_map/ppermute | solution.py:321
  45.5 0.7 %collective-permute-start.12 = (bf16[2,256,128]{2,1,0:T(8,128)(2,1)S(1)}, bf16[2,256,128]{2,1,0:T(8,128)(2,1)S(1)}, u32[]{:S(2)}, u32[]{:S(2)}) collective-permute-start(bf16[2,256,128]{2,1,0:T(8,128)(2,1)S(1)} %get-tuple-element.45), channel_id=1, source_target_pairs={{0,8},{8,0},{16,24},{24,16},{1,9},{9,1},{17,25},{25,17},{2,10},{10... | collective-permute-start | bytes 393224 | tf_op jit(solution)/shard_map/ppermute | solution.py:321
  46.2 4.7 %collective-permute-start.13 = (bf16[2,256,128]{2,1,0:T(8,128)(2,1)S(1)}, bf16[2,256,128]{2,1,0:T(8,128)(2,1)S(1)}, u32[]{:S(2)}, u32[]{:S(2)}) collective-permute-start(bf16[2,256,128]{2,1,0:T(8,128)(2,1)S(1)} %get-tuple-element.46), channel_id=1, source_target_pairs={{0,16},{8,24},{16,0},{24,8},{1,17},{9,25},{17,1},{25,9},{2,18},{10... | collective-permute-start | bytes 393224 | tf_op jit(solution)/shard_map/ppermute | solution.py:321
  50.9 0.0 collective-permute-done.15.refs_1_
  50.9 0.3 collective-permute-start.14
  51.2 0.0 collective-permute-done.16.refs_2_
  51.2 0.0 collective-permute-done.17.refs_3_
  51.2 0.1 query_sum.1
  51.3 0.7 %collective-permute-start.18 = (bf16[2,128,128]{2,1,0:T(8,128)(2,1)S(1)}, bf16[2,128,128]{2,1,0:T(8,128)(2,1)S(1)}, u32[]{:S(2)}, u32[]{:S(2)}) collective-permute-start(bf16[2,128,128]{2,1,0:T(8,128)(2,1)S(1)} %get-tuple-element.55), channel_id=1, source_target_pairs={{0,8},{8,0},{16,24},{24,16},{1,9},{9,1},{17,25},{25,17},{2,10},{10... | collective-permute-start | bytes 196616 | tf_op jit(solution)/shard_map/ppermute | solution.py:321
  51.9 0.0 collective-permute-done.12.refs_1_
  51.9 8.6 %collective-permute-done.13.refs_2_ = bf16[2,256,128]{2,1,0:T(8,128)(2,1)S(1)} collective-permute-done((bf16[2,256,128]{2,1,0:T(8,128)(2,1)S(1)}, bf16[2,256,128]{2,1,0:T(8,128)(2,1)S(1)}, u32[]{:S(2)}, u32[]{:S(2)}) %collective-permute-start.13) | collective-permute-done | bytes 131104 | tf_op jit(solution)/shard_map/ppermute | solution.py:321
  60.6 0.0 collective-permute-done.14.refs_3_
  60.6 0.1 key_sum.1
  60.6 0.0 collective-permute-done.18.dq_pair
  60.7 0.1 collective-permute-start.19
  60.8 1.4 %collective-permute-done.19.sib_ref = bf16[2,384,128]{2,1,0:T(8,128)(2,1)S(1)} collective-permute-done((bf16[2,384,128]{2,1,0:T(8,128)(2,1)S(1)}, bf16[2,384,128]{2,1,0:T(8,128)(2,1)S(1)}, u32[]{:S(2)}, u32[]{:S(2)}) %collective-permute-start.19) | collective-permute-done | bytes 196640 | tf_op jit(solution)/shard_map/ppermute | solution.py:321
  62.2 0.8 %finish.1 = (bf16[1,128,512]{2,1,0:T(8,128)(2,1)}, bf16[1,128,512]{2,1,0:T(8,128)(2,1)}, bf16[1,128,512]{2,1,0:T(8,128)(2,1)}) custom-call(bf16[2,256,128]{2,1,0:T(8,128)(2,1)S(1)} %get-tuple-element.48.dkv_own, bf16[2,128,128]{2,1,0:T(8,128)(2,1)S(1)} %get-tuple-element.54.dq_same, bf16[2,128,128]{2,1,0:T(8,128)(2,1)S(1)} %collective-permute-done.18.dq_pair, ...), custom_call_target="tpu_custom_call" | custom-call | tf_op jit(solution)/shard_map/finish/pallas_call | solution.py:469
  (2 shorter events, 0.0 us)
Async XLA Ops:
  0.6 0.7 %copy-start.1 = (s32[1,1,24]{2,1,0:T(1,128)S(1)}, s32[1,1,24]{2,1,0:T(1,128)}, u32[]{:S(2)}) copy-start(s32[1,1,24]{2,1,0:T(1,128)} %slot_ref.1) | copy-start | bytes 292
  1.3 0.9 %copy-start = (s32[1,1,24,8,128]{4,3,2,1,0:T(8,128)S(1)}, s32[1,1,24,8,128]{4,3,2,1,0:T(8,128)}, u32[]{:S(2)}) copy-start(s32[1,1,24,8,128]{4,3,2,1,0:T(8,128)} %bits_hbm.1) | copy-start | bytes 294916
  2.2 7.3 %copy-start.2 = (f32[1,8,1024]{2,1,0:T(8,128)S(1)}, f32[1,8,1024]{2,1,0:T(8,128)}, u32[]{:S(2)}) copy-start(f32[1,8,1024]{2,1,0:T(8,128)} %lse_own.1) | copy-start | bytes 98308
  4.6 5.3 %collective-permute-start = (bf16[784,128]{1,0:T(8,128)(2,1)}, bf16[784,128]{1,0:T(8,128)(2,1)S(1)}, u32[]{:S(2)}, u32[]{:S(2)}) collective-permute-start(bf16[784,128]{1,0:T(8,128)(2,1)} %get-tuple-element.31), channel_id=1, source_target_pairs={{0,1},{1,0},{2,3},{3,2},{4,5},{5,4},{6,7},{7,6},{8,9},{9,8},{10,11... | collective-permute-start | bytes 602120 | tf_op jit(solution)/shard_map/ppermute | solution.py:321
  5.1 13.1 %collective-permute-start.1 = (bf16[272,128]{1,0:T(8,128)(2,1)S(1)}, bf16[272,128]{1,0:T(8,128)(2,1)S(1)}, u32[]{:S(2)}, u32[]{:S(2)}) collective-permute-start(bf16[272,128]{1,0:T(8,128)(2,1)S(1)} %get-tuple-element.32), channel_id=1, source_target_pairs={{0,8},{1,9},{8,0},{9,1},{16,24},{17,25},{24,16},{25,17},{2,10},{3,... | collective-permute-start | bytes 208904 | tf_op jit(solution)/shard_map/ppermute | solution.py:321
  7.7 10.5 %collective-permute-start.2 = (bf16[272,128]{1,0:T(8,128)(2,1)S(1)}, bf16[272,128]{1,0:T(8,128)(2,1)S(1)}, u32[]{:S(2)}, u32[]{:S(2)}) collective-permute-start(bf16[272,128]{1,0:T(8,128)(2,1)S(1)} %get-tuple-element.33), channel_id=1, source_target_pairs={{0,9},{1,8},{8,1},{9,0},{16,25},{17,24},{24,17},{25,16},{2,11},{3,... | collective-permute-start | bytes 208904 | tf_op jit(solution)/shard_map/ppermute | solution.py:321
  7.8 7.8 %collective-permute-start.3 = (s32[13,8,128]{2,1,0:T(8,128)S(1)}, s32[13,8,128]{2,1,0:T(8,128)S(1)}, u32[]{:S(2)}, u32[]{:S(2)}) collective-permute-start(s32[13,8,128]{2,1,0:T(8,128)S(1)} %get-tuple-element.34.bits_own), channel_id=1, source_target_pairs={{0,8},{8,0},{16,24},{24,16},{1,9},{9,1},{17,25},{25,17},{2,10},{10... | collective-permute-start | bytes 159752 | tf_op jit(solution)/shard_map/ppermute | solution.py:321
  9.6 4.5 %collective-permute-start.4 = (f32[1,8,1024]{2,1,0:T(8,128)S(1)}, f32[1,8,1024]{2,1,0:T(8,128)S(1)}, u32[]{:S(2)}, u32[]{:S(2)}) collective-permute-start(f32[1,8,1024]{2,1,0:T(8,128)S(1)} %copy-done.2), channel_id=1, source_target_pairs={{0,8},{8,0},{16,24},{24,16},{1,9},{9,1},{17,25},{25,17},{2,10},{10... | collective-permute-start | bytes 98312 | tf_op jit(solution)/shard_map/ppermute | solution.py:321
  9.9 16.3 %collective-permute-start.10 = (bf16[2,256,128]{2,1,0:T(8,128)(2,1)S(1)}, bf16[2,256,128]{2,1,0:T(8,128)(2,1)S(1)}, u32[]{:S(2)}, u32[]{:S(2)}) collective-permute-start(bf16[2,256,128]{2,1,0:T(8,128)(2,1)S(1)} %get-tuple-element.38), channel_id=1, source_target_pairs={{0,24},{8,16},{16,8},{24,0},{1,25},{9,17},{17,9},{25,1},{2,26},{10... | collective-permute-start | bytes 393224 | tf_op jit(solution)/shard_map/ppermute | solution.py:321
  14.1 12.2 %collective-permute-start.8 = (bf16[2,256,128]{2,1,0:T(8,128)(2,1)S(1)}, bf16[2,256,128]{2,1,0:T(8,128)(2,1)S(1)}, u32[]{:S(2)}, u32[]{:S(2)}) collective-permute-start(bf16[2,256,128]{2,1,0:T(8,128)(2,1)S(1)} %get-tuple-element.38), channel_id=1, source_target_pairs={{0,8},{8,0},{16,24},{24,16},{1,9},{9,1},{17,25},{25,17},{2,10},{10... | collective-permute-start | bytes 393224 | tf_op jit(solution)/shard_map/ppermute | solution.py:321
  15.6 9.1 %collective-permute-start.9 = (bf16[2,256,128]{2,1,0:T(8,128)(2,1)S(1)}, bf16[2,256,128]{2,1,0:T(8,128)(2,1)S(1)}, u32[]{:S(2)}, u32[]{:S(2)}) collective-permute-start(bf16[2,256,128]{2,1,0:T(8,128)(2,1)S(1)} %get-tuple-element.37.refs_0_), channel_id=1, source_target_pairs={{0,16},{8,24},{16,0},{24,8},{1,17},{9,25},{17,1},{25,9},{2,18},{10... | collective-permute-start | bytes 393224 | tf_op jit(solution)/shard_map/ppermute | solution.py:321
  18.3 10.6 %collective-permute-start.7 = (bf16[4,272,128]{2,1,0:T(8,128)(2,1)S(1)}, bf16[4,272,128]{2,1,0:T(8,128)(2,1)S(1)}, u32[]{:S(2)}, u32[]{:S(2)}) collective-permute-start(bf16[4,272,128]{2,1,0:T(8,128)(2,1)S(1)} %get-tuple-element.35.refs_0_), channel_id=1, source_target_pairs={{0,6},{2,4},{4,2},{6,0},{1,7},{3,5},{5,3},{7,1},{8,14},{10,12},{12... | collective-permute-start | bytes 835592 | tf_op jit(solution)/shard_map/ppermute | solution.py:321
  20.8 12.1 %collective-permute-start.6 = (bf16[4,272,128]{2,1,0:T(8,128)(2,1)S(1)}, bf16[4,272,128]{2,1,0:T(8,128)(2,1)S(1)}, u32[]{:S(2)}, u32[]{:S(2)}) collective-permute-start(bf16[4,272,128]{2,1,0:T(8,128)(2,1)S(1)} %get-tuple-element.35.refs_0_), channel_id=1, source_target_pairs={{0,4},{2,6},{4,0},{6,2},{1,5},{3,7},{5,1},{7,3},{8,12},{10,14},{12... | collective-permute-start | bytes 835592 | tf_op jit(solution)/shard_map/ppermute | solution.py:321
  24.7 8.2 %collective-permute-start.5 = (bf16[4,272,128]{2,1,0:T(8,128)(2,1)S(1)}, bf16[4,272,128]{2,1,0:T(8,128)(2,1)S(1)}, u32[]{:S(2)}, u32[]{:S(2)}) collective-permute-start(bf16[4,272,128]{2,1,0:T(8,128)(2,1)S(1)} %get-tuple-element.35.refs_0_), channel_id=1, source_target_pairs={{0,2},{2,0},{4,6},{6,4},{1,3},{3,1},{5,7},{7,5},{8,10},{10,8},{12,... | collective-permute-start | bytes 835592 | tf_op jit(solution)/shard_map/ppermute | solution.py:321
  26.2 1.3 %collective-permute-start.11 = (s32[2,13,8,128]{3,2,1,0:T(8,128)S(1)}, s32[2,13,8,128]{3,2,1,0:T(8,128)S(1)}, u32[]{:S(2)}, u32[]{:S(2)}) collective-permute-start(s32[2,13,8,128]{3,2,1,0:T(8,128)S(1)} %get-tuple-element.42.refs_7_), channel_id=1, source_target_pairs={{0,1},{1,0},{2,3},{3,2},{4,5},{5,4},{6,7},{7,6},{8,9},{9,8},{10,11... | collective-permute-start | bytes 319496 | tf_op jit(solution)/shard_map/ppermute | solution.py:321
  41.9 9.0 %collective-permute-start.15 = (bf16[4,128,128]{2,1,0:T(8,128)(2,1)S(1)}, bf16[4,128,128]{2,1,0:T(8,128)(2,1)S(1)}, u32[]{:S(2)}, u32[]{:S(2)}) collective-permute-start(bf16[4,128,128]{2,1,0:T(8,128)(2,1)S(1)} %get-tuple-element.51), channel_id=1, source_target_pairs={{0,2},{2,0},{4,6},{6,4},{1,3},{3,1},{5,7},{7,5},{8,10},{10,8},{12,... | collective-permute-start | bytes 393224 | tf_op jit(solution)/shard_map/ppermute | solution.py:321
  42.0 9.2 %collective-permute-start.16 = (bf16[4,128,128]{2,1,0:T(8,128)(2,1)S(1)}, bf16[4,128,128]{2,1,0:T(8,128)(2,1)S(1)}, u32[]{:S(2)}, u32[]{:S(2)}) collective-permute-start(bf16[4,128,128]{2,1,0:T(8,128)(2,1)S(1)} %get-tuple-element.52), channel_id=1, source_target_pairs={{0,4},{2,6},{4,0},{6,2},{1,5},{3,7},{5,1},{7,3},{8,12},{10,14},{12... | collective-permute-start | bytes 393224 | tf_op jit(solution)/shard_map/ppermute | solution.py:321
  43.1 8.1 %collective-permute-start.17 = (bf16[4,128,128]{2,1,0:T(8,128)(2,1)S(1)}, bf16[4,128,128]{2,1,0:T(8,128)(2,1)S(1)}, u32[]{:S(2)}, u32[]{:S(2)}) collective-permute-start(bf16[4,128,128]{2,1,0:T(8,128)(2,1)S(1)} %get-tuple-element.53), channel_id=1, source_target_pairs={{0,6},{2,4},{4,2},{6,0},{1,7},{3,5},{5,3},{7,1},{8,14},{10,12},{12... | collective-permute-start | bytes 393224 | tf_op jit(solution)/shard_map/ppermute | solution.py:321
  45.5 6.5 %collective-permute-start.12 = (bf16[2,256,128]{2,1,0:T(8,128)(2,1)S(1)}, bf16[2,256,128]{2,1,0:T(8,128)(2,1)S(1)}, u32[]{:S(2)}, u32[]{:S(2)}) collective-permute-start(bf16[2,256,128]{2,1,0:T(8,128)(2,1)S(1)} %get-tuple-element.45), channel_id=1, source_target_pairs={{0,8},{8,0},{16,24},{24,16},{1,9},{9,1},{17,25},{25,17},{2,10},{10... | collective-permute-start | bytes 393224 | tf_op jit(solution)/shard_map/ppermute | solution.py:321
  46.2 14.4 %collective-permute-start.13 = (bf16[2,256,128]{2,1,0:T(8,128)(2,1)S(1)}, bf16[2,256,128]{2,1,0:T(8,128)(2,1)S(1)}, u32[]{:S(2)}, u32[]{:S(2)}) collective-permute-start(bf16[2,256,128]{2,1,0:T(8,128)(2,1)S(1)} %get-tuple-element.46), channel_id=1, source_target_pairs={{0,16},{8,24},{16,0},{24,8},{1,17},{9,25},{17,1},{25,9},{2,18},{10... | collective-permute-start | bytes 393224 | tf_op jit(solution)/shard_map/ppermute | solution.py:321
  50.9 9.7 %collective-permute-start.14 = (bf16[2,256,128]{2,1,0:T(8,128)(2,1)S(1)}, bf16[2,256,128]{2,1,0:T(8,128)(2,1)S(1)}, u32[]{:S(2)}, u32[]{:S(2)}) collective-permute-start(bf16[2,256,128]{2,1,0:T(8,128)(2,1)S(1)} %get-tuple-element.47), channel_id=1, source_target_pairs={{0,24},{8,16},{16,8},{24,0},{1,25},{9,17},{17,9},{25,1},{2,26},{10... | collective-permute-start | bytes 393224 | tf_op jit(solution)/shard_map/ppermute | solution.py:321
  51.3 9.4 %collective-permute-start.18 = (bf16[2,128,128]{2,1,0:T(8,128)(2,1)S(1)}, bf16[2,128,128]{2,1,0:T(8,128)(2,1)S(1)}, u32[]{:S(2)}, u32[]{:S(2)}) collective-permute-start(bf16[2,128,128]{2,1,0:T(8,128)(2,1)S(1)} %get-tuple-element.55), channel_id=1, source_target_pairs={{0,8},{8,0},{16,24},{24,16},{1,9},{9,1},{17,25},{25,17},{2,10},{10... | collective-permute-start | bytes 196616 | tf_op jit(solution)/shard_map/ppermute | solution.py:321
  60.7 1.5 %collective-permute-start.19 = (bf16[2,384,128]{2,1,0:T(8,128)(2,1)S(1)}, bf16[2,384,128]{2,1,0:T(8,128)(2,1)S(1)}, u32[]{:S(2)}, u32[]{:S(2)}) collective-permute-start(bf16[2,384,128]{2,1,0:T(8,128)(2,1)S(1)} %bundle.1), channel_id=1, source_target_pairs={{0,1},{1,0},{2,3},{3,2},{4,5},{5,4},{6,7},{7,6},{8,9},{9,8},{10,11... | collective-permute-start | bytes 589832 | tf_op jit(solution)/shard_map/ppermute | solution.py:321

commit v3 on v2

--- a/solution.py
+++ b/solution.py
@@ -16,10 +16,11 @@
 PAD = 16
 QUARTERS = 4
 LOG2E = 1.4426950408889634
+LSE_UNIT = 2.0**21
 NT = (((1,), (1,)), ((), ()))
 NN = (((1,), (0,)), ((), ()))
 MEDIUM = pltpu.CompilerParams(vmem_limit_bytes=28 * 1024 * 1024)
-PACK = pltpu.CompilerParams(vmem_limit_bytes=int(53.4 * 1024 * 1024))
+PACK = pltpu.CompilerParams(vmem_limit_bytes=int(53.5 * 1024 * 1024))
 SMALL = pltpu.CompilerParams(vmem_limit_bytes=12 * 1024 * 1024)
 def early(gigaflops):
     return pl.CostEstimate(flops=gigaflops * 10**9, bytes_accessed=0, transcendentals=0)
@@ -39,13 +40,13 @@
 
 
 def pack_kernel(
-    heads, q_hbm, g_hbm, o_hbm, k_hbm, v_hbm, bits_hbm, slot_ref, live_ref,
-    qg_own, qg_pair0, qg_pair1, kv_own, sib_ref, packed_ref,
-    q_ref, g_ref, o_ref, k_ref, v_ref, bits_ref, delta_ref, sems,
+    heads, q_hbm, g_hbm, o_hbm, k_hbm, v_hbm, bits_hbm, lse_hbm, slot_ref, live_ref,
+    qg_own, pair0_ref, pair1_ref, kv_own, sib_ref, packed_ref, lse_own,
+    q_ref, g_ref, o_ref, k_ref, v_ref, bits_ref, lse_ref, delta_ref, sems,
 ):
     arrays = (
-        (q_hbm, q_ref), (g_hbm, g_ref), (o_hbm, o_ref),
-        (k_hbm, k_ref), (v_hbm, v_ref), (bits_hbm, bits_ref),
+        (q_hbm, q_ref), (g_hbm, g_ref), (o_hbm, o_ref), (k_hbm, k_ref),
+        (v_hbm, v_ref), (bits_hbm, bits_ref), (lse_hbm, lse_ref),
     )
     copies = [pltpu.make_async_copy(a, b, sems.at[i]) for i, (a, b) in enumerate(arrays)]
     for copy in copies:
@@ -71,9 +72,8 @@
     ).astype(BF16)
     for index in range(QUARTERS):
         delta_ref[index] = delta[index * PAD : (index + 1) * PAD]
-    base = 4 * krows
     for step, (ref, start) in enumerate(
-        ((qg_own, 0), (sib_ref, base), (qg_pair0, 0), (qg_pair1, 0))
+        ((qg_own, 0), (sib_ref, 4 * krows), (pair0_ref, 2 * krows), (pair1_ref, 2 * krows))
     ):
         lanes = lanes_of(quarter ^ step)
         ref[start : start + rows] = q_ref[0, :, lanes]
@@ -81,12 +81,30 @@
         if rows < LANES:
             ref[start + 2 * rows : start + 2 * rows + PAD] = jnp.zeros((PAD, LANES), BF16)
         ref[start + 2 * rows : start + 2 * rows + PAD, :rows] = delta_ref[quarter ^ step]
-    for side in range(2):
-        for ref, step in ((kv_own, 2 * side), (sib_ref, 2 * side + 1)):
-            lanes = lanes_of(quarter ^ step)
-            start = side * 2 * krows
+    for step, targets in enumerate((
+        ((kv_own, 0),), ((sib_ref, 0),),
+        ((kv_own, 2 * krows), (pair0_ref, 0)), ((sib_ref, 2 * krows), (pair1_ref, 0)),
+    )):
+        lanes = lanes_of(quarter ^ step)
+        for ref, start in targets:
             ref[start : start + krows] = k_ref[0, :, lanes]
             ref[start + krows : start + 2 * krows] = v_ref[0, :, lanes]
+    every = lse_ref[0]
+
+    def lse_of(wanted_quarter):
+        own = every[:local]
+        for index in range(1, QUARTERS):
+            own = jnp.where(
+                wanted_quarter == index, every[local * index : local * (index + 1)], own
+            )
+        return own
+
+    mine = lse_of(quarter) * LOG2E
+    other = (lse_of(quarter ^ 2) * LSE_UNIT).astype(I32)
+    for u in range(lse_own.shape[0]):
+        lanes = slice(u * LANES, (u + 1) * LANES)
+        lse_own[u] = mine[:, lanes]
+        packed_ref[capacity // 2 + 1 + u // 4, u % 4 * 2 : u % 4 * 2 + 2] = other[:, lanes]
     for entry in range(capacity):
         words = bits_ref[0, 0, entry]
         span = slice(entry % 2 * 4, entry % 2 * 4 + 4)
@@ -102,36 +120,36 @@
 
 
 def query_join_kernel(
-    krows, tile, qg_own, sib_ref, qg_pair0, qg_pair1, bits_own, bits_pair, lse_own, lse_pair,
+    krows, slabs, qg_own, sib_ref, pair0_ref, pair1_ref, bits_own, bits_pair, lse_own,
     qg_out, bits_out, lse_out,
 ):
     row, chip, core, quarter = my_place()
     side = row % 2
     qg_out[quarter] = qg_own[...]
     qg_out[quarter ^ 1] = sib_ref[4 * krows :]
-    qg_out[quarter ^ 2] = qg_pair0[...]
-    qg_out[quarter ^ 3] = qg_pair1[...]
-    bits_out[side] = bits_own[...]
-    bits_out[1 - side] = bits_pair[...]
-    for step, ref in enumerate((lse_own, lse_pair)):
-        every = ref[0] * LOG2E
-        own = every[:2]
-        for index in range(1, QUARTERS):
-            own = jnp.where(quarter == index, every[2 * index : 2 * index + 2], own)
-        for u in range(lse_out.shape[1]):
-            lse_out[side ^ step, u] = own[:, u * tile : (u + 1) * tile]
-
-
-def key_place_kernel(head_dim, tile, *refs):
+    qg_out[quarter ^ 2] = pair0_ref[2 * krows :]
+    qg_out[quarter ^ 3] = pair1_ref[2 * krows :]
+    bits_out[side] = bits_own[:slabs]
+    bits_out[1 - side] = bits_pair[:slabs]
+    lse_out[side] = lse_own[...]
+    for u in range(lse_out.shape[1]):
+        fixed = bits_pair[slabs + u // 4, u % 4 * 2 : u % 4 * 2 + 2]
+        lse_out[1 - side, u] = fixed.astype(F32) * (LOG2E / LSE_UNIT)
+
+
+def key_place_kernel(head_dim, tile, pair0_ref, pair1_ref, *refs):
     kv_refs, (k_out, v_out, k2t_out) = refs[:-3], refs[-3:]
     krows = kv_refs[0].shape[1] // 2
-    row = my_place()[0]
-    for step, ref in enumerate(kv_refs):
+    row, chip, core, quarter = my_place()
+    blocks = [(0, 0, kv_refs[0].at[0]), (0, 1, kv_refs[0].at[1])]
+    blocks += [(1, core, pair0_ref), (1, 1 - core, pair1_ref)]
+    for index, ref in enumerate(kv_refs[1:]):
+        blocks += [(index + 2, 0, ref.at[0]), (index + 2, 1, ref.at[1])]
+    for step, block, ref in blocks:
         start = (row ^ step) * krows
         inner = pl.multiple_of(start % tile, krows)
-        for block in range(2):
-            k_out[block, start // tile, pl.ds(inner, krows)] = ref[block, :krows]
-            v_out[block, start // tile, pl.ds(inner, krows)] = ref[block, krows:]
+        k_out[block, start // tile, pl.ds(inner, krows)] = ref[:krows]
+        v_out[block, start // tile, pl.ds(inner, krows)] = ref[krows : 2 * krows]
     low_row = lax.broadcasted_iota(I32, (LANES, tile), 0) < head_dim
     none_t = jnp.zeros((LANES, tile), BF16)
     for block in range(2):
@@ -277,15 +295,13 @@
 
 
 def query_sum_kernel(chips, *refs):
-    parts, (same_ref, pair_ref) = refs[:chips], refs[chips:]
-    side = my_place()[0] % 2
-    for step, ref in enumerate((same_ref, pair_ref)):
-        for core in range(2):
-            index = (side ^ step) * 2 + core
-            total = parts[0][index].astype(F32)
-            for part in parts[1:]:
-                total += part[index].astype(F32)
-            ref[core] = total.astype(BF16)
+    parts, outs = refs[:chips], refs[chips:]
+    quarter = my_place()[3]
+    for step, out in enumerate(outs):
+        total = parts[0][quarter ^ step].astype(F32)
+        for part in parts[1:]:
+            total += part[quarter ^ step].astype(F32)
+        out[...] = total.astype(BF16)
 
 
 def key_sum_kernel(row_count, *refs):
@@ -299,22 +315,16 @@
             ref[side] = total.astype(BF16)
 
 
-def bundle_kernel(dkv_ref, dq_same, dq_pair, out):
-    krows2 = dkv_ref.shape[1]
-    sibling = 1 - my_place()[2]
-    out[:, :krows2] = dkv_ref[...]
-    for side, dq in enumerate((dq_same, dq_pair)):
-        out[side, krows2:] = dq[sibling]
-
-
-def finish_kernel(krows, dkv_own, dq_same, dq_pair, sib_ref, dq_out, dk_out, dv_out):
-    row, chip, core, quarter = my_place()
-    for side, dq in enumerate((dq_same, dq_pair)):
-        for step, ref in enumerate((dkv_own, sib_ref)):
-            lanes = lanes_of(quarter ^ (2 * side + step))
-            dk_out[0, :, lanes] = ref[side, :krows]
-            dv_out[0, :, lanes] = ref[side, krows : 2 * krows]
-            dq_out[0, :, lanes] = ref[side, 2 * krows :] if step else dq[core]
+def finish_kernel(own_ref, sib_ref, *refs):
+    dq_refs, (dq_out, dk_out, dv_out) = refs[:QUARTERS], refs[QUARTERS:]
+    krows = dk_out.shape[1]
+    quarter = my_place()[3]
+    for step, dq in enumerate(dq_refs):
+        lanes = lanes_of(quarter ^ step)
+        dkv = (own_ref, sib_ref)[step % 2]
+        dk_out[0, :, lanes] = dkv[step // 2, :krows]
+        dv_out[0, :, lanes] = dkv[step // 2, krows:]
+        dq_out[0, :, lanes] = dq[...]
 
 
 def send(block, axes, count, step):
@@ -340,15 +350,18 @@
 
     qg_shape = shape(2 * rows + PAD, LANES)
     kv_shape = shape(2, 2 * krows, LANES)
-    qg_own, qg_pair0, qg_pair1, kv_own, to_sibling, bits_own = pl.pallas_call(
+    slabs = capacity // 2 + 1
+    pair_shape = shape(2 * krows + 2 * rows + PAD, LANES)
+    qg_own, pair0, pair1, kv_own, to_sibling, bits_own, lse_own = pl.pallas_call(
         functools.partial(pack_kernel, heads),
         out_shape=(
-            qg_shape, qg_shape, qg_shape, shape(4 * krows, LANES),
+            qg_shape, pair_shape, pair_shape, shape(4 * krows, LANES),
             shape(4 * krows + 2 * rows + PAD, LANES),
-            shape(capacity // 2 + 1, 8, LANES, dtype=I32),
+            shape(slabs + query_tiles // 4, 8, LANES, dtype=I32),
+            shape(query_tiles, 2, tile, dtype=F32),
         ),
-        in_specs=[HBM] * 6 + [VMEM] * 2,
-        out_specs=(VMEM,) * 6,
+        in_specs=[HBM] * 7 + [VMEM] * 2,
+        out_specs=(VMEM,) * 7,
         scratch_shapes=[
             pltpu.VMEM(queries.shape, BF16),
             pltpu.VMEM(queries.shape, BF16),
@@ -356,18 +369,18 @@
             pltpu.VMEM(keys.shape, BF16),
             pltpu.VMEM(keys.shape, BF16),
             pltpu.VMEM(tile_bits.shape, I32),
+            pltpu.VMEM(lse.shape, F32),
             pltpu.VMEM((QUARTERS, PAD, rows), BF16),
-            pltpu.SemaphoreType.DMA((6,)),
+            pltpu.SemaphoreType.DMA((7,)),
         ],
         compiler_params=PACK,
         name="pack",
-    )(queries, grad_out, outputs, keys, values, tile_bits, tile_slot, tile_live)
-
-    qg_pair0 = send(qg_pair0, line, places, 2)
-    qg_pair1 = send(qg_pair1, line, places, 3)
+    )(queries, grad_out, outputs, keys, values, tile_bits, lse, tile_slot, tile_live)
+
+    pair0 = send(pair0, line, places, 2)
+    pair1 = send(pair1, line, places, 3)
     from_sibling = send(to_sibling, "core", cores, 1)
     bits_pair = send(bits_own, "row", row_count, 1)
-    lse_pair = send(lse, "row", row_count, 1)
     kv_same, kv_pair = pl.pallas_call(
         functools.partial(key_join_kernel, krows),
         out_shape=(kv_shape, kv_shape),
@@ -378,21 +391,21 @@
     )(kv_own, from_sibling)
     kv_out = (kv_same, kv_pair)
     kv = [kv_same] + [
-        send(kv_out[step % 2], "row", row_count, step) for step in range(1, row_count)
+        send(kv_out[step % 2], "row", row_count, step) for step in range(2, row_count)
     ]
     qg, bits, lse2 = pl.pallas_call(
-        functools.partial(query_join_kernel, krows, tile),
+        functools.partial(query_join_kernel, krows, slabs),
         out_shape=(
             shape(QUARTERS, 2 * rows + PAD, LANES),
-            shape(2, capacity // 2 + 1, 8, LANES, dtype=I32),
+            shape(2, slabs, 8, LANES, dtype=I32),
             shape(2, query_tiles, 2, tile, dtype=F32),
         ),
-        in_specs=[VMEM] * 8,
+        in_specs=[VMEM] * 7,
         out_specs=(VMEM,) * 3,
         compiler_params=SMALL,
         cost_estimate=early(20),
         name="query_join",
-    )(qg_own, from_sibling, qg_pair0, qg_pair1, bits_own, bits_pair, lse, lse_pair)
+    )(qg_own, from_sibling, pair0, pair1, bits_own, bits_pair, lse_own)
     qg = [qg] + [send(qg, "chip", chips, step) for step in range(1, chips)]
     bits_sibling = send(bits, "core", cores, 1)
 
@@ -402,12 +415,12 @@
             shape(2, key_tiles, tile, LANES), shape(2, key_tiles, tile, LANES),
             shape(2, key_tiles, LANES, 2 * tile),
         ),
-        in_specs=[VMEM] * row_count,
+        in_specs=[VMEM] * (row_count + 1),
         out_specs=(VMEM,) * 3,
         compiler_params=SMALL,
         cost_estimate=early(20),
         name="key_place",
-    )(*kv)
+    )(pair0, pair1, *kv)
     parts = pl.pallas_call(
         functools.partial(pair_kernel, (head_dim, tile, capacity, chips, row_count)),
         out_shape=(shape(2, query_tiles, LANES, tile),) + (kv_shape,) * row_count,
@@ -439,41 +452,32 @@
     )(parts[0])
     dq = [dq[0]] + [send(dq[step], "chip", chips, step) for step in range(1, chips)]
     dkv = [dkv[0]] + [send(dkv[step], "row", row_count, step) for step in range(1, row_count)]
-    dq_same, dq_pair = pl.pallas_call(
+    dq = pl.pallas_call(
         functools.partial(query_sum_kernel, chips),
-        out_shape=(shape(2, rows, LANES),) * 2,
+        out_shape=(shape(rows, LANES),) * QUARTERS,
         in_specs=[VMEM] * chips,
-        out_specs=(VMEM,) * 2,
+        out_specs=(VMEM,) * QUARTERS,
         compiler_params=SMALL,
         name="query_sum",
     )(*dq)
-    dq_pair = send(dq_pair, "row", row_count, 1)
+    dq = [dq[0]] + [send(dq[step], line, places, step) for step in range(1, QUARTERS)]
     dkv_own, dkv_sibling = pl.pallas_call(
         functools.partial(key_sum_kernel, row_count),
         out_shape=(kv_shape,) * 2,
         in_specs=[VMEM] * row_count,
         out_specs=(VMEM,) * 2,
         compiler_params=SMALL,
-        cost_estimate=early(20),
         name="key_sum",
     )(*dkv)
-    to_sibling = pl.pallas_call(
-        bundle_kernel,
-        out_shape=shape(2, 2 * krows + rows, LANES),
-        in_specs=[VMEM] * 3,
-        out_specs=VMEM,
-        compiler_params=SMALL,
-        name="bundle",
-    )(dkv_sibling, dq_same, dq_pair)
-    from_sibling = send(to_sibling, "core", cores, 1)
+    dkv_sibling = send(dkv_sibling, "core", cores, 1)
     return pl.pallas_call(
-        functools.partial(finish_kernel, krows),
+        finish_kernel,
         out_shape=(shape(1, rows, width), shape(1, krows, width), shape(1, krows, width)),
-        in_specs=[VMEM] * 4,
+        in_specs=[VMEM] * (2 + QUARTERS),
         out_specs=(VMEM,) * 3,
         compiler_params=SMALL,
         name="finish",
-    )(dkv_own, dq_same, dq_pair, from_sibling)
+    )(dkv_own, dkv_sibling, *dq)
 
 
 def solution(mesh):

time: 63.6 us -> 73.9 us (1.16); the launches traced: 63 us -> 74.8 us
  waiting for transfers between devices: 20.4 us -> 28.4 us
  Pallas kernels: 12.5 us -> 15.5 us
  local copies, waits for them, and re-layouts: 0.89 us -> 1.65 us
    ppermute x20, waiting for transfers between devices: 20.4 us -> 28.4 us  [send(): lax.ppermute(block, axes, [(place, place ^ step) for place in range(count)])]
    pallas_call x1, Pallas kernels: 8.72 us -> 11.6 us  [body(): pl.pallas_call(functools.partial(pair_kernel, (head_dim, tile, capacity,...]
    unnamed x6, local copies, waits for them, and re-layouts: 0.89 us -> 1.65 us
where the time goes in v3:
time: 73.9 us; the launch traced here: 74.8 us
  waiting for transfers between devices  28.4 us (38%)
  starting transfers between devices  27.8 us (38%)
  Pallas kernels  15.5 us (21%)
  local copies, waits for them, and re-layouts  1.65 us (2%)
  between operations  1.42 us (2%)
    ppermute x20, waiting for transfers between devices, send(): lax.ppermute(block, axes, [(place, place ^ step) for place in range(count)])  28.4 us
    ppermute x20, starting transfers between devices, send(): lax.ppermute(block, axes, [(place, place ^ step) for place in range(count)])  27.8 us
    pallas_call x1, Pallas kernels, body(): pl.pallas_call(functools.partial(pair_kernel, (head_dim, tile, capacity,...  11.6 us
    pallas_call x1, Pallas kernels, body(): pl.pallas_call(functools.partial(pack_kernel, heads), out_shape=(qg_shape...  2.47 us
    unnamed x6, local copies, waits for them, and re-layouts  1.65 us
  transfers between devices with their start and end apart: 20, of which 8 were waited for; matrix products, arithmetic and copies ran while one was open for 0% of the time, Pallas kernels for 1%

profile of v3, /device:TPU:0, one launch (start us, length us, event | category | flops | bytes accessed | tf_op | source)
XLA Modules:
  0.0 74.8 jit_solution(3277623854598757695)
XLA Ops:
  0.6 0.0 copy-start.2
  1.3 0.0 copy-done.2
  1.3 0.0 copy-start
  1.3 0.9 %copy-done = s32[1,1,24,8,128]{4,3,2,1,0:T(8,128)S(1)} copy-done((s32[1,1,24,8,128]{4,3,2,1,0:T(8,128)S(1)}, s32[1,1,24,8,128]{4,3,2,1,0:T(8,128)}, u32[]{:S(2)}) %copy-start) | copy-done | bytes 98328
  2.2 0.0 copy-start.1
  2.2 0.8 %copy-done.1 = f32[1,8,1024]{2,1,0:T(8,128)S(1)} copy-done((f32[1,8,1024]{2,1,0:T(8,128)S(1)}, f32[1,8,1024]{2,1,0:T(8,128)}, u32[]{:S(2)}) %copy-start.1) | copy-done | bytes 32792
  3.0 2.5 %pack.1 = (bf16[272,128]{1,0:T(8,128)(2,1)S(1)}, bf16[528,128]{1,0:T(8,128)(2,1)}, bf16[528,128]{1,0:T(8,128)(2,1)}, bf16[512,128]{1,0:T(8,128)(2,1)S(1)}, bf16[...) custom-call(bf16[1,128,512]{2,1,0:T(8,128)(2,1)} %q_hbm.1, bf16[1,128,512]{2,1,0:T(8,128)(2,1)} %g_hbm.1, ...), custom_call_target="tpu_custom_call" | custom-call | tf_op jit(solution)/shard_map/pack/pallas_call | solution.py:355
  5.4 0.5 collective-permute-start
  6.0 2.7 %collective-permute-start.1 = (bf16[528,128]{1,0:T(8,128)(2,1)}, bf16[528,128]{1,0:T(8,128)(2,1)S(1)}, u32[]{:S(2)}, u32[]{:S(2)}) collective-permute-start(bf16[528,128]{1,0:T(8,128)(2,1)} %get-tuple-element.35), channel_id=1, source_target_pairs={{0,8},{1,9},{8,0},{9,1},{16,24},{17,25},{24,16},{25,17},{2,10},{3,... | collective-permute-start | bytes 405512 | tf_op jit(solution)/shard_map/ppermute | solution.py:331
  8.6 0.1 collective-permute-start.2
  8.7 1.7 %collective-permute-start.3 = (s32[15,8,128]{2,1,0:T(8,128)S(1)}, s32[15,8,128]{2,1,0:T(8,128)S(1)}, u32[]{:S(2)}, u32[]{:S(2)}) collective-permute-start(s32[15,8,128]{2,1,0:T(8,128)S(1)} %get-tuple-element.37.bits_own), channel_id=1, source_target_pairs={{0,8},{8,0},{16,24},{24,16},{1,9},{9,1},{17,25},{25,17},{2,10},{10... | collective-permute-start | bytes 184328 | tf_op jit(solution)/shard_map/ppermute | solution.py:331
  10.4 0.0 collective-permute-done.sib_ref
  10.4 2.5 %collective-permute-start.8 = (bf16[2,256,128]{2,1,0:T(8,128)(2,1)S(1)}, bf16[2,256,128]{2,1,0:T(8,128)(2,1)S(1)}, u32[]{:S(2)}, u32[]{:S(2)}) collective-permute-start(bf16[2,256,128]{2,1,0:T(8,128)(2,1)S(1)} %get-tuple-element.42), channel_id=1, source_target_pairs={{0,24},{8,16},{16,8},{24,0},{1,25},{9,17},{17,9},{25,1},{2,26},{10... | collective-permute-start | bytes 393224 | tf_op jit(solution)/shard_map/ppermute | solution.py:331
  13.0 0.2 collective-permute-start.7
  13.2 9.4 %collective-permute-done.3.bits_pair = s32[15,8,128]{2,1,0:T(8,128)S(1)} collective-permute-done((s32[15,8,128]{2,1,0:T(8,128)S(1)}, s32[15,8,128]{2,1,0:T(8,128)S(1)}, u32[]{:S(2)}, u32[]{:S(2)}) %collective-permute-start.3) | collective-permute-done | bytes 61472 | tf_op jit(solution)/shard_map/ppermute | solution.py:331
  22.6 0.0 collective-permute-done.1.pair0_ref
  22.6 0.0 collective-permute-done.2.pair1_ref
  22.6 2.8 %collective-permute-start.6 = (bf16[4,272,128]{2,1,0:T(8,128)(2,1)S(1)}, bf16[4,272,128]{2,1,0:T(8,128)(2,1)S(1)}, u32[]{:S(2)}, u32[]{:S(2)}) collective-permute-start(bf16[4,272,128]{2,1,0:T(8,128)(2,1)S(1)} %get-tuple-element.39.refs_0_), channel_id=1, source_target_pairs={{0,6},{2,4},{4,2},{6,0},{1,7},{3,5},{5,3},{7,1},{8,14},{10,12},{12... | collective-permute-start | bytes 835592 | tf_op jit(solution)/shard_map/ppermute | solution.py:331
  25.4 0.5 collective-permute-start.5
  25.9 0.2 collective-permute-start.4
  26.2 0.0 collective-permute-done.8.refs_2_
  26.2 0.0 collective-permute-start.9
  26.2 0.0 collective-permute-done.7.refs_1_
  26.2 0.2 key_place.1
  26.4 1.1 %collective-permute-done.9.refs_8_ = s32[2,13,8,128]{3,2,1,0:T(8,128)S(1)} collective-permute-done((s32[2,13,8,128]{3,2,1,0:T(8,128)S(1)}, s32[2,13,8,128]{3,2,1,0:T(8,128)S(1)}, u32[]{:S(2)}, u32[]{:S(2)}) %collective-permute-start.9) | collective-permute-done | bytes 106528 | tf_op jit(solution)/shard_map/ppermute | solution.py:331
  27.5 5.7 %collective-permute-done.6.refs_3_ = bf16[4,272,128]{2,1,0:T(8,128)(2,1)S(1)} collective-permute-done((bf16[4,272,128]{2,1,0:T(8,128)(2,1)S(1)}, bf16[4,272,128]{2,1,0:T(8,128)(2,1)S(1)}, u32[]{:S(2)}, u32[]{:S(2)}) %collective-permute-start.6) | collective-permute-done | bytes 278560 | tf_op jit(solution)/shard_map/ppermute | solution.py:331
  33.2 4.5 %collective-permute-done.5.refs_2_ = bf16[4,272,128]{2,1,0:T(8,128)(2,1)S(1)} collective-permute-done((bf16[4,272,128]{2,1,0:T(8,128)(2,1)S(1)}, bf16[4,272,128]{2,1,0:T(8,128)(2,1)S(1)}, u32[]{:S(2)}, u32[]{:S(2)}) %collective-permute-start.5) | collective-permute-done | bytes 278560 | tf_op jit(solution)/shard_map/ppermute | solution.py:331
  37.7 0.1 collective-permute-done.4.refs_1_
  37.8 11.6 %pair.1 = (bf16[2,8,128,128]{3,2,1,0:T(8,128)(2,1)S(1)}, bf16[2,256,128]{2,1,0:T(8,128)(2,1)S(1)}, bf16[2,256,128]{2,1,0:T(8,128)(2,1)S(1)}, bf16[2,256,128]{2,1,0:T(8,128)(2,1)S(1)}, bf16[2,256,128]{2,1,0:T(8,128)(2,1)S(1)}) custom-call(bf16[4,272,128]{2,1,0:T(8,128)(2,1)S(1)} %get-tuple-element.39.refs_0_, ...), custom_call_target="tpu_custom_call" | custom-call | tf_op jit(solution)/shard_map/pair/pallas_call | solution.py:424
  49.4 0.1 collective-permute-start.10
  49.5 1.2 %collective-permute-start.11 = (bf16[2,256,128]{2,1,0:T(8,128)(2,1)S(1)}, bf16[2,256,128]{2,1,0:T(8,128)(2,1)S(1)}, u32[]{:S(2)}, u32[]{:S(2)}) collective-permute-start(bf16[2,256,128]{2,1,0:T(8,128)(2,1)S(1)} %get-tuple-element.50), channel_id=1, source_target_pairs={{0,16},{8,24},{16,0},{24,8},{1,17},{9,25},{17,1},{25,9},{2,18},{10... | collective-permute-start | bytes 393224 | tf_op jit(solution)/shard_map/ppermute | solution.py:331
  50.7 3.1 %collective-permute-start.12 = (bf16[2,256,128]{2,1,0:T(8,128)(2,1)S(1)}, bf16[2,256,128]{2,1,0:T(8,128)(2,1)S(1)}, u32[]{:S(2)}, u32[]{:S(2)}) collective-permute-start(bf16[2,256,128]{2,1,0:T(8,128)(2,1)S(1)} %get-tuple-element.51), channel_id=1, source_target_pairs={{0,24},{8,16},{16,8},{24,0},{1,25},{9,17},{17,9},{25,1},{2,26},{10... | collective-permute-start | bytes 393224 | tf_op jit(solution)/shard_map/ppermute | solution.py:331
  53.8 0.2 turn.1
  54.1 8.6 %collective-permute-start.14 = (bf16[4,128,128]{2,1,0:T(8,128)(2,1)S(1)}, bf16[4,128,128]{2,1,0:T(8,128)(2,1)S(1)}, u32[]{:S(2)}, u32[]{:S(2)}) collective-permute-start(bf16[4,128,128]{2,1,0:T(8,128)(2,1)S(1)} %get-tuple-element.56), channel_id=1, source_target_pairs={{0,2},{2,0},{4,6},{6,4},{1,3},{3,1},{5,7},{7,5},{8,10},{10,8},{12,... | collective-permute-start | bytes 393224 | tf_op jit(solution)/shard_map/ppermute | solution.py:331
  62.6 0.0 collective-permute-start.15
  62.6 0.0 collective-permute-done.10.refs_1_
  62.7 1.5 %collective-permute-start.16 = (bf16[4,128,128]{2,1,0:T(8,128)(2,1)S(1)}, bf16[4,128,128]{2,1,0:T(8,128)(2,1)S(1)}, u32[]{:S(2)}, u32[]{:S(2)}) collective-permute-start(bf16[4,128,128]{2,1,0:T(8,128)(2,1)S(1)} %get-tuple-element.58), channel_id=1, source_target_pairs={{0,6},{2,4},{4,2},{6,0},{1,7},{3,5},{5,3},{7,1},{8,14},{10,12},{12... | collective-permute-start | bytes 393224 | tf_op jit(solution)/shard_map/ppermute | solution.py:331
  64.2 0.0 collective-permute-done.11.refs_2_
  64.2 0.0 collective-permute-done.12.refs_3_
  64.2 0.1 key_sum.1
  64.3 0.1 collective-permute-start.13
  64.3 1.7 %collective-permute-done.14.refs_1_ = bf16[4,128,128]{2,1,0:T(8,128)(2,1)S(1)} collective-permute-done((bf16[4,128,128]{2,1,0:T(8,128)(2,1)S(1)}, bf16[4,128,128]{2,1,0:T(8,128)(2,1)S(1)}, u32[]{:S(2)}, u32[]{:S(2)}) %collective-permute-start.14) | collective-permute-done | bytes 131104 | tf_op jit(solution)/shard_map/ppermute | solution.py:331
  66.0 3.6 %collective-permute-done.15.refs_2_ = bf16[4,128,128]{2,1,0:T(8,128)(2,1)S(1)} collective-permute-done((bf16[4,128,128]{2,1,0:T(8,128)(2,1)S(1)}, bf16[4,128,128]{2,1,0:T(8,128)(2,1)S(1)}, u32[]{:S(2)}, u32[]{:S(2)}) %collective-permute-start.15) | collective-permute-done | bytes 131104 | tf_op jit(solution)/shard_map/ppermute | solution.py:331
  69.7 0.0 collective-permute-done.16.refs_3_
  69.7 0.1 query_sum.1
  69.7 0.1 collective-permute-start.17
  69.8 0.1 collective-permute-start.18
  69.9 1.8 %collective-permute-start.19 = (bf16[128,128]{1,0:T(8,128)(2,1)S(1)}, bf16[128,128]{1,0:T(8,128)(2,1)S(1)}, u32[]{:S(2)}, u32[]{:S(2)}) collective-permute-start(bf16[128,128]{1,0:T(8,128)(2,1)S(1)} %get-tuple-element.62), channel_id=1, source_target_pairs={{0,9},{1,8},{8,1},{9,0},{16,25},{17,24},{24,17},{25,16},{2,11},{3,... | collective-permute-start | bytes 98312 | tf_op jit(solution)/shard_map/ppermute | solution.py:331
  71.7 0.0 collective-permute-done.17.refs_1_
  71.7 2.3 %collective-permute-done.18.refs_2_ = bf16[128,128]{1,0:T(8,128)(2,1)S(1)} collective-permute-done((bf16[128,128]{1,0:T(8,128)(2,1)S(1)}, bf16[128,128]{1,0:T(8,128)(2,1)S(1)}, u32[]{:S(2)}, u32[]{:S(2)}) %collective-permute-start.18) | collective-permute-done | bytes 32800 | tf_op jit(solution)/shard_map/ppermute | solution.py:331
  74.0 0.0 collective-permute-done.19.refs_3_
  74.0 0.0 collective-permute-done.13.sib_ref
  74.0 0.8 %finish.1 = (bf16[1,128,512]{2,1,0:T(8,128)(2,1)}, bf16[1,128,512]{2,1,0:T(8,128)(2,1)}, bf16[1,128,512]{2,1,0:T(8,128)(2,1)}) custom-call(bf16[2,256,128]{2,1,0:T(8,128)(2,1)S(1)} %get-tuple-element.52.own_ref, bf16[2,256,128]{2,1,0:T(8,128)(2,1)S(1)} %collective-permute-done.13.sib_ref, bf16[128,128]{1,0:T(8,128)(2,1)S(1)} %get-tuple-element.59.refs_0_, ...), custom_call_target="tpu_custom_call" | custom-call | tf_op jit(solution)/shard_map/finish/pallas_call | solution.py:473
  (2 shorter events, 0.1 us)
Async XLA Ops:
  0.6 0.7 copy-start.2
  1.3 0.9 %copy-start = (s32[1,1,24,8,128]{4,3,2,1,0:T(8,128)S(1)}, s32[1,1,24,8,128]{4,3,2,1,0:T(8,128)}, u32[]{:S(2)}) copy-start(s32[1,1,24,8,128]{4,3,2,1,0:T(8,128)} %bits_hbm.1) | copy-start | bytes 294916
  2.2 0.8 %copy-start.1 = (f32[1,8,1024]{2,1,0:T(8,128)S(1)}, f32[1,8,1024]{2,1,0:T(8,128)}, u32[]{:S(2)}) copy-start(f32[1,8,1024]{2,1,0:T(8,128)} %lse_hbm.1) | copy-start | bytes 98308
  5.4 5.0 %collective-permute-start = (bf16[784,128]{1,0:T(8,128)(2,1)}, bf16[784,128]{1,0:T(8,128)(2,1)S(1)}, u32[]{:S(2)}, u32[]{:S(2)}) collective-permute-start(bf16[784,128]{1,0:T(8,128)(2,1)} %get-tuple-element.34), channel_id=1, source_target_pairs={{0,1},{1,0},{2,3},{3,2},{4,5},{5,4},{6,7},{7,6},{8,9},{9,8},{10,11... | collective-permute-start | bytes 602120 | tf_op jit(solution)/shard_map/ppermute | solution.py:331
  6.0 16.6 %collective-permute-start.1 = (bf16[528,128]{1,0:T(8,128)(2,1)}, bf16[528,128]{1,0:T(8,128)(2,1)S(1)}, u32[]{:S(2)}, u32[]{:S(2)}) collective-permute-start(bf16[528,128]{1,0:T(8,128)(2,1)} %get-tuple-element.35), channel_id=1, source_target_pairs={{0,8},{1,9},{8,0},{9,1},{16,24},{17,25},{24,16},{25,17},{2,10},{3,... | collective-permute-start | bytes 405512 | tf_op jit(solution)/shard_map/ppermute | solution.py:331
  8.6 14.0 %collective-permute-start.2 = (bf16[528,128]{1,0:T(8,128)(2,1)}, bf16[528,128]{1,0:T(8,128)(2,1)S(1)}, u32[]{:S(2)}, u32[]{:S(2)}) collective-permute-start(bf16[528,128]{1,0:T(8,128)(2,1)} %get-tuple-element.36), channel_id=1, source_target_pairs={{0,9},{1,8},{8,1},{9,0},{16,25},{17,24},{24,17},{25,16},{2,11},{3,... | collective-permute-start | bytes 405512 | tf_op jit(solution)/shard_map/ppermute | solution.py:331
  8.7 13.9 %collective-permute-start.3 = (s32[15,8,128]{2,1,0:T(8,128)S(1)}, s32[15,8,128]{2,1,0:T(8,128)S(1)}, u32[]{:S(2)}, u32[]{:S(2)}) collective-permute-start(s32[15,8,128]{2,1,0:T(8,128)S(1)} %get-tuple-element.37.bits_own), channel_id=1, source_target_pairs={{0,8},{8,0},{16,24},{24,16},{1,9},{9,1},{17,25},{25,17},{2,10},{10... | collective-permute-start | bytes 184328 | tf_op jit(solution)/shard_map/ppermute | solution.py:331
  10.4 15.7 %collective-permute-start.8 = (bf16[2,256,128]{2,1,0:T(8,128)(2,1)S(1)}, bf16[2,256,128]{2,1,0:T(8,128)(2,1)S(1)}, u32[]{:S(2)}, u32[]{:S(2)}) collective-permute-start(bf16[2,256,128]{2,1,0:T(8,128)(2,1)S(1)} %get-tuple-element.42), channel_id=1, source_target_pairs={{0,24},{8,16},{16,8},{24,0},{1,25},{9,17},{17,9},{25,1},{2,26},{10... | collective-permute-start | bytes 393224 | tf_op jit(solution)/shard_map/ppermute | solution.py:331
  13.0 13.2 %collective-permute-start.7 = (bf16[2,256,128]{2,1,0:T(8,128)(2,1)S(1)}, bf16[2,256,128]{2,1,0:T(8,128)(2,1)S(1)}, u32[]{:S(2)}, u32[]{:S(2)}) collective-permute-start(bf16[2,256,128]{2,1,0:T(8,128)(2,1)S(1)} %get-tuple-element.41.refs_0_), channel_id=1, source_target_pairs={{0,16},{8,24},{16,0},{24,8},{1,17},{9,25},{17,1},{25,9},{2,18},{10... | collective-permute-start | bytes 393224 | tf_op jit(solution)/shard_map/ppermute | solution.py:331
  22.6 10.6 %collective-permute-start.6 = (bf16[4,272,128]{2,1,0:T(8,128)(2,1)S(1)}, bf16[4,272,128]{2,1,0:T(8,128)(2,1)S(1)}, u32[]{:S(2)}, u32[]{:S(2)}) collective-permute-start(bf16[4,272,128]{2,1,0:T(8,128)(2,1)S(1)} %get-tuple-element.39.refs_0_), channel_id=1, source_target_pairs={{0,6},{2,4},{4,2},{6,0},{1,7},{3,5},{5,3},{7,1},{8,14},{10,12},{12... | collective-permute-start | bytes 835592 | tf_op jit(solution)/shard_map/ppermute | solution.py:331
  25.4 12.3 %collective-permute-start.5 = (bf16[4,272,128]{2,1,0:T(8,128)(2,1)S(1)}, bf16[4,272,128]{2,1,0:T(8,128)(2,1)S(1)}, u32[]{:S(2)}, u32[]{:S(2)}) collective-permute-start(bf16[4,272,128]{2,1,0:T(8,128)(2,1)S(1)} %get-tuple-element.39.refs_0_), channel_id=1, source_target_pairs={{0,4},{2,6},{4,0},{6,2},{1,5},{3,7},{5,1},{7,3},{8,12},{10,14},{12... | collective-permute-start | bytes 835592 | tf_op jit(solution)/shard_map/ppermute | solution.py:331
  25.9 11.9 %collective-permute-start.4 = (bf16[4,272,128]{2,1,0:T(8,128)(2,1)S(1)}, bf16[4,272,128]{2,1,0:T(8,128)(2,1)S(1)}, u32[]{:S(2)}, u32[]{:S(2)}) collective-permute-start(bf16[4,272,128]{2,1,0:T(8,128)(2,1)S(1)} %get-tuple-element.39.refs_0_), channel_id=1, source_target_pairs={{0,2},{2,0},{4,6},{6,4},{1,3},{3,1},{5,7},{7,5},{8,10},{10,8},{12,... | collective-permute-start | bytes 835592 | tf_op jit(solution)/shard_map/ppermute | solution.py:331
  26.2 1.3 %collective-permute-start.9 = (s32[2,13,8,128]{3,2,1,0:T(8,128)S(1)}, s32[2,13,8,128]{3,2,1,0:T(8,128)S(1)}, u32[]{:S(2)}, u32[]{:S(2)}) collective-permute-start(s32[2,13,8,128]{3,2,1,0:T(8,128)S(1)} %get-tuple-element.46.refs_7_), channel_id=1, source_target_pairs={{0,1},{1,0},{2,3},{3,2},{4,5},{5,4},{6,7},{7,6},{8,9},{9,8},{10,11... | collective-permute-start | bytes 319496 | tf_op jit(solution)/shard_map/ppermute | solution.py:331
  49.4 13.3 %collective-permute-start.10 = (bf16[2,256,128]{2,1,0:T(8,128)(2,1)S(1)}, bf16[2,256,128]{2,1,0:T(8,128)(2,1)S(1)}, u32[]{:S(2)}, u32[]{:S(2)}) collective-permute-start(bf16[2,256,128]{2,1,0:T(8,128)(2,1)S(1)} %get-tuple-element.49), channel_id=1, source_target_pairs={{0,8},{8,0},{16,24},{24,16},{1,9},{9,1},{17,25},{25,17},{2,10},{10... | collective-permute-start | bytes 393224 | tf_op jit(solution)/shard_map/ppermute | solution.py:331
  49.5 14.7 %collective-permute-start.11 = (bf16[2,256,128]{2,1,0:T(8,128)(2,1)S(1)}, bf16[2,256,128]{2,1,0:T(8,128)(2,1)S(1)}, u32[]{:S(2)}, u32[]{:S(2)}) collective-permute-start(bf16[2,256,128]{2,1,0:T(8,128)(2,1)S(1)} %get-tuple-element.50), channel_id=1, source_target_pairs={{0,16},{8,24},{16,0},{24,8},{1,17},{9,25},{17,1},{25,9},{2,18},{10... | collective-permute-start | bytes 393224 | tf_op jit(solution)/shard_map/ppermute | solution.py:331
  50.7 13.5 %collective-permute-start.12 = (bf16[2,256,128]{2,1,0:T(8,128)(2,1)S(1)}, bf16[2,256,128]{2,1,0:T(8,128)(2,1)S(1)}, u32[]{:S(2)}, u32[]{:S(2)}) collective-permute-start(bf16[2,256,128]{2,1,0:T(8,128)(2,1)S(1)} %get-tuple-element.51), channel_id=1, source_target_pairs={{0,24},{8,16},{16,8},{24,0},{1,25},{9,17},{17,9},{25,1},{2,26},{10... | collective-permute-start | bytes 393224 | tf_op jit(solution)/shard_map/ppermute | solution.py:331
  54.1 12.0 %collective-permute-start.14 = (bf16[4,128,128]{2,1,0:T(8,128)(2,1)S(1)}, bf16[4,128,128]{2,1,0:T(8,128)(2,1)S(1)}, u32[]{:S(2)}, u32[]{:S(2)}) collective-permute-start(bf16[4,128,128]{2,1,0:T(8,128)(2,1)S(1)} %get-tuple-element.56), channel_id=1, source_target_pairs={{0,2},{2,0},{4,6},{6,4},{1,3},{3,1},{5,7},{7,5},{8,10},{10,8},{12,... | collective-permute-start | bytes 393224 | tf_op jit(solution)/shard_map/ppermute | solution.py:331
  62.6 7.0 %collective-permute-start.15 = (bf16[4,128,128]{2,1,0:T(8,128)(2,1)S(1)}, bf16[4,128,128]{2,1,0:T(8,128)(2,1)S(1)}, u32[]{:S(2)}, u32[]{:S(2)}) collective-permute-start(bf16[4,128,128]{2,1,0:T(8,128)(2,1)S(1)} %get-tuple-element.57), channel_id=1, source_target_pairs={{0,4},{2,6},{4,0},{6,2},{1,5},{3,7},{5,1},{7,3},{8,12},{10,14},{12... | collective-permute-start | bytes 393224 | tf_op jit(solution)/shard_map/ppermute | solution.py:331
  62.7 7.0 %collective-permute-start.16 = (bf16[4,128,128]{2,1,0:T(8,128)(2,1)S(1)}, bf16[4,128,128]{2,1,0:T(8,128)(2,1)S(1)}, u32[]{:S(2)}, u32[]{:S(2)}) collective-permute-start(bf16[4,128,128]{2,1,0:T(8,128)(2,1)S(1)} %get-tuple-element.58), channel_id=1, source_target_pairs={{0,6},{2,4},{4,2},{6,0},{1,7},{3,5},{5,3},{7,1},{8,14},{10,12},{12... | collective-permute-start | bytes 393224 | tf_op jit(solution)/shard_map/ppermute | solution.py:331
  64.3 9.7 %collective-permute-start.13 = (bf16[2,256,128]{2,1,0:T(8,128)(2,1)S(1)}, bf16[2,256,128]{2,1,0:T(8,128)(2,1)S(1)}, u32[]{:S(2)}, u32[]{:S(2)}) collective-permute-start(bf16[2,256,128]{2,1,0:T(8,128)(2,1)S(1)} %get-tuple-element.53), channel_id=1, source_target_pairs={{0,1},{1,0},{2,3},{3,2},{4,5},{5,4},{6,7},{7,6},{8,9},{9,8},{10,11... | collective-permute-start | bytes 393224 | tf_op jit(solution)/shard_map/ppermute | solution.py:331
  69.7 1.9 %collective-permute-start.17 = (bf16[128,128]{1,0:T(8,128)(2,1)S(1)}, bf16[128,128]{1,0:T(8,128)(2,1)S(1)}, u32[]{:S(2)}, u32[]{:S(2)}) collective-permute-start(bf16[128,128]{1,0:T(8,128)(2,1)S(1)} %get-tuple-element.60), channel_id=1, source_target_pairs={{0,1},{1,0},{8,9},{9,8},{16,17},{17,16},{24,25},{25,24},{2,3},{3,2... | collective-permute-start | bytes 98312 | tf_op jit(solution)/shard_map/ppermute | solution.py:331
  69.8 4.2 %collective-permute-start.18 = (bf16[128,128]{1,0:T(8,128)(2,1)S(1)}, bf16[128,128]{1,0:T(8,128)(2,1)S(1)}, u32[]{:S(2)}, u32[]{:S(2)}) collective-permute-start(bf16[128,128]{1,0:T(8,128)(2,1)S(1)} %get-tuple-element.61), channel_id=1, source_target_pairs={{0,8},{1,9},{8,0},{9,1},{16,24},{17,25},{24,16},{25,17},{2,10},{3,... | collective-permute-start | bytes 98312 | tf_op jit(solution)/shard_map/ppermute | solution.py:331
  69.9 4.1 %collective-permute-start.19 = (bf16[128,128]{1,0:T(8,128)(2,1)S(1)}, bf16[128,128]{1,0:T(8,128)(2,1)S(1)}, u32[]{:S(2)}, u32[]{:S(2)}) collective-permute-start(bf16[128,128]{1,0:T(8,128)(2,1)S(1)} %get-tuple-element.62), channel_id=1, source_target_pairs={{0,9},{1,8},{8,1},{9,0},{16,25},{17,24},{24,17},{25,16},{2,11},{3,... | collective-permute-start | bytes 98312 | tf_op jit(solution)/shard_map/ppermute | solution.py:331

commit v4 on v2

--- a/solution.py
+++ b/solution.py
@@ -16,10 +16,11 @@
 PAD = 16
 QUARTERS = 4
 LOG2E = 1.4426950408889634
+LSE_UNIT = 2.0**21
 NT = (((1,), (1,)), ((), ()))
 NN = (((1,), (0,)), ((), ()))
 MEDIUM = pltpu.CompilerParams(vmem_limit_bytes=28 * 1024 * 1024)
-PACK = pltpu.CompilerParams(vmem_limit_bytes=int(53.4 * 1024 * 1024))
+PACK = pltpu.CompilerParams(vmem_limit_bytes=int(53.6 * 1024 * 1024))
 SMALL = pltpu.CompilerParams(vmem_limit_bytes=12 * 1024 * 1024)
 def early(gigaflops):
     return pl.CostEstimate(flops=gigaflops * 10**9, bytes_accessed=0, transcendentals=0)
@@ -38,31 +39,22 @@
     return row, chip, core, row % 2 * 2 + core
 
 
-def pack_kernel(
-    heads, q_hbm, g_hbm, o_hbm, k_hbm, v_hbm, bits_hbm, slot_ref, live_ref,
-    qg_own, qg_pair0, qg_pair1, kv_own, sib_ref, packed_ref,
-    q_ref, g_ref, o_ref, k_ref, v_ref, bits_ref, delta_ref, sems,
+def pack_query_kernel(
+    heads, q_hbm, g_hbm, o_hbm, own_ref, sib_ref, pair0_ref, pair1_ref,
+    q_ref, g_ref, o_ref, delta_ref, sems,
 ):
-    arrays = (
-        (q_hbm, q_ref), (g_hbm, g_ref), (o_hbm, o_ref),
-        (k_hbm, k_ref), (v_hbm, v_ref), (bits_hbm, bits_ref),
-    )
+    arrays = ((q_hbm, q_ref), (g_hbm, g_ref), (o_hbm, o_ref))
     copies = [pltpu.make_async_copy(a, b, sems.at[i]) for i, (a, b) in enumerate(arrays)]
     for copy in copies:
         copy.start()
     rows, width = q_ref.shape[1:]
-    krows = k_ref.shape[1]
     head_dim = width // heads
     local = heads // QUARTERS
-    capacity = bits_ref.shape[2]
     quarter = my_place()[3]
     feature = lax.broadcasted_iota(I32, (QUARTERS * PAD, width), 1)
     line = lax.broadcasted_iota(I32, (QUARTERS * PAD, width), 0)
     wanted = jnp.where(line % PAD < local, line // PAD * local + line % PAD, -1)
     pick = (feature // head_dim == wanted).astype(F32)
-    packed_ref[capacity // 2] = jnp.zeros((8, LANES), I32)
-    packed_ref[capacity // 2, 0:1, 0:capacity] = slot_ref[0]
-    packed_ref[capacity // 2, 1:2, 0:1] = live_ref[...]
     for copy in copies:
         copy.wait()
     product = g_ref[0].astype(F32) * o_ref[0].astype(F32)
@@ -71,22 +63,53 @@
     ).astype(BF16)
     for index in range(QUARTERS):
         delta_ref[index] = delta[index * PAD : (index + 1) * PAD]
-    base = 4 * krows
-    for step, (ref, start) in enumerate(
-        ((qg_own, 0), (sib_ref, base), (qg_pair0, 0), (qg_pair1, 0))
-    ):
+    for step, ref in enumerate((own_ref, sib_ref, pair0_ref, pair1_ref)):
         lanes = lanes_of(quarter ^ step)
-        ref[start : start + rows] = q_ref[0, :, lanes]
-        ref[start + rows : start + 2 * rows] = g_ref[0, :, lanes]
+        ref[:rows] = q_ref[0, :, lanes]
+        ref[rows : 2 * rows] = g_ref[0, :, lanes]
         if rows < LANES:
-            ref[start + 2 * rows : start + 2 * rows + PAD] = jnp.zeros((PAD, LANES), BF16)
-        ref[start + 2 * rows : start + 2 * rows + PAD, :rows] = delta_ref[quarter ^ step]
-    for side in range(2):
-        for ref, step in ((kv_own, 2 * side), (sib_ref, 2 * side + 1)):
-            lanes = lanes_of(quarter ^ step)
-            start = side * 2 * krows
-            ref[start : start + krows] = k_ref[0, :, lanes]
-            ref[start + krows : start + 2 * krows] = v_ref[0, :, lanes]
+            ref[2 * rows :] = jnp.zeros((PAD, LANES), BF16)
+        ref[2 * rows :, :rows] = delta_ref[quarter ^ step]
+
+
+def pack_key_kernel(
+    local, k_hbm, v_hbm, bits_hbm, lse_hbm, slot_ref, live_ref, _after0, _after1, _after2,
+    own_ref, sib_ref, packed_ref, lse_own, k_ref, v_ref, bits_ref, lse_ref, sems,
+):
+    arrays = ((k_hbm, k_ref), (v_hbm, v_ref), (bits_hbm, bits_ref), (lse_hbm, lse_ref))
+    copies = [pltpu.make_async_copy(a, b, sems.at[i]) for i, (a, b) in enumerate(arrays)]
+    for copy in copies:
+        copy.start()
+    krows = k_ref.shape[1]
+    capacity = bits_ref.shape[2]
+    quarter = my_place()[3]
+    packed_ref[capacity // 2] = jnp.zeros((8, LANES), I32)
+    packed_ref[capacity // 2, 0:1, 0:capacity] = slot_ref[0]
+    packed_ref[capacity // 2, 1:2, 0:1] = live_ref[...]
+    for copy in copies:
+        copy.wait()
+    for step in range(QUARTERS):
+        ref = (own_ref, sib_ref)[step % 2]
+        lanes = lanes_of(quarter ^ step)
+        start = step // 2 * 2 * krows
+        ref[start : start + krows] = k_ref[0, :, lanes]
+        ref[start + krows : start + 2 * krows] = v_ref[0, :, lanes]
+    every = lse_ref[0]
+
+    def lse_of(wanted_quarter):
+        own = every[:local]
+        for index in range(1, QUARTERS):
+            own = jnp.where(
+                wanted_quarter == index, every[local * index : local * (index + 1)], own
+            )
+        return own
+
+    mine = lse_of(quarter) * LOG2E
+    other = (lse_of(quarter ^ 2) * LSE_UNIT).astype(I32)
+    for u in range(lse_own.shape[0]):
+        lanes = slice(u * LANES, (u + 1) * LANES)
+        lse_own[u] = mine[:, lanes]
+        packed_ref[capacity // 2 + 1 + u // 4, u % 4 * 2 : u % 4 * 2 + 2] = other[:, lanes]
     for entry in range(capacity):
         words = bits_ref[0, 0, entry]
         span = slice(entry % 2 * 4, entry % 2 * 4 + 4)
@@ -101,54 +124,25 @@
         ref[1 - core] = sib_ref[span]
 
 
-def query_join_kernel(
-    krows, tile, qg_own, sib_ref, qg_pair0, qg_pair1, bits_own, bits_pair, lse_own, lse_pair,
-    qg_out, bits_out, lse_out,
-):
-    row, chip, core, quarter = my_place()
-    side = row % 2
-    qg_out[quarter] = qg_own[...]
-    qg_out[quarter ^ 1] = sib_ref[4 * krows :]
-    qg_out[quarter ^ 2] = qg_pair0[...]
-    qg_out[quarter ^ 3] = qg_pair1[...]
-    bits_out[side] = bits_own[...]
-    bits_out[1 - side] = bits_pair[...]
-    for step, ref in enumerate((lse_own, lse_pair)):
-        every = ref[0] * LOG2E
-        own = every[:2]
-        for index in range(1, QUARTERS):
-            own = jnp.where(quarter == index, every[2 * index : 2 * index + 2], own)
-        for u in range(lse_out.shape[1]):
-            lse_out[side ^ step, u] = own[:, u * tile : (u + 1) * tile]
-
-
-def key_place_kernel(head_dim, tile, *refs):
-    kv_refs, (k_out, v_out, k2t_out) = refs[:-3], refs[-3:]
-    krows = kv_refs[0].shape[1] // 2
-    row = my_place()[0]
-    for step, ref in enumerate(kv_refs):
-        start = (row ^ step) * krows
-        inner = pl.multiple_of(start % tile, krows)
-        for block in range(2):
-            k_out[block, start // tile, pl.ds(inner, krows)] = ref[block, :krows]
-            v_out[block, start // tile, pl.ds(inner, krows)] = ref[block, krows:]
-    low_row = lax.broadcasted_iota(I32, (LANES, tile), 0) < head_dim
-    none_t = jnp.zeros((LANES, tile), BF16)
-    for block in range(2):
-        for w in range(k_out.shape[1]):
-            flipped = k_out[block, w].T
-            k2t_out[block, w] = jnp.concatenate(
-                [jnp.where(low_row, flipped, none_t), jnp.where(low_row, none_t, flipped)], axis=1
-            )
+def query_join_kernel(own_ref, sib_ref, pair0_ref, pair1_ref, out):
+    quarter = my_place()[3]
+    for step, ref in enumerate((own_ref, sib_ref, pair0_ref, pair1_ref)):
+        out[quarter ^ step] = ref[...]
+
+
+def far_join_kernel(*refs):
+    for index, ref in enumerate(refs[:-1]):
+        refs[-1][index] = ref[...]
 
 
 def pair_kernel(sizes, *refs):
     head_dim, tile, capacity, chips, row_count = sizes
     qg_refs, refs = refs[:chips], refs[chips:]
-    (k_scr, v_scr, k2t_scr), refs = refs[:3], refs[3:]
-    bits_refs, lse_ref, refs = refs[:2], refs[2], refs[3:]
+    (same_ref, pair_ref, far_ref), refs = refs[:3], refs[3:]
+    bits_refs, lse_own, refs = refs[:QUARTERS], refs[QUARTERS], refs[QUARTERS + 1 :]
     dqt_ref, dkv_refs, refs = refs[0], refs[1 : 1 + row_count], refs[1 + row_count :]
-    q2_scr, g2_scr, delta_scr, dqt_scr, dk_scr, dv_scr, info, sems = refs
+    (q2_scr, g2_scr, k_scr, v_scr, k2t_scr, lse_scr, delta_scr, dqt_scr, dk_scr, dv_scr,
+     info, sems) = refs
     rows = (qg_refs[0].shape[1] - PAD) // 2
     krows = dkv_refs[0].shape[1] // 2
     query_tiles = q2_scr.shape[1]
@@ -156,16 +150,18 @@
     scaling = float(head_dim) ** -0.5
     row, chip, core, quarter = my_place()
     side = row % 2
+    slabs = capacity // 2 + 1
 
     copies = [
-        pltpu.make_async_copy(
-            bits_refs[i % 2].at[i // 2, capacity // 2], info.at[i], sems.at[i]
-        )
-        for i in range(QUARTERS)
+        pltpu.make_async_copy(ref.at[slabs - 1], info.at[i], sems.at[i])
+        for i, ref in enumerate(bits_refs)
     ]
     for copy in copies:
         copy.start()
-
+    lse_scr[side] = lse_own[...]
+    for u in range(query_tiles):
+        fixed = bits_refs[2][slabs + u // 4, u % 4 * 2 : u % 4 * 2 + 2]
+        lse_scr[1 - side, u] = fixed.astype(F32) * (LOG2E / LSE_UNIT)
     low = lax.broadcasted_iota(I32, (rows, LANES), 1) < head_dim
     none = jnp.zeros((rows, LANES), BF16)
     for step in range(chips):
@@ -187,6 +183,21 @@
                     @pl.when(source % (tile // rows) == part)
                     def _(part=part, delta=delta, u=u, block=block):
                         delta_scr[block, u, :, part * rows : (part + 1) * rows] = delta
+    sources = [same_ref, pair_ref] + [far_ref.at[index] for index in range(row_count - 2)]
+    for step, ref in enumerate(sources):
+        start = (row ^ step) * krows
+        inner = pl.multiple_of(start % tile, krows)
+        for block in range(2):
+            k_scr[block, start // tile, pl.ds(inner, krows)] = ref[block, :krows]
+            v_scr[block, start // tile, pl.ds(inner, krows)] = ref[block, krows:]
+    low_row = lax.broadcasted_iota(I32, (LANES, tile), 0) < head_dim
+    none_t = jnp.zeros((LANES, tile), BF16)
+    for block in range(2):
+        for w in range(key_tiles):
+            flipped = k_scr[block, w].T
+            k2t_scr[block, w] = jnp.concatenate(
+                [jnp.where(low_row, flipped, none_t), jnp.where(low_row, none_t, flipped)], axis=1
+            )
     dqt_scr[...] = jnp.zeros_like(dqt_scr)
     dk_scr[...] = jnp.zeros_like(dk_scr)
     dv_scr[...] = jnp.zeros_like(dv_scr)
@@ -197,12 +208,12 @@
         copy.wait()
 
     for step in range(QUARTERS):
-        qb = step // 2
+        qb = side ^ (step // 2)
         kb = core ^ (step % 2)
         live = info[step, 1, 0]
 
         def two_tiles(index, _, step=step, qb=qb, kb=kb, live=live):
-            both = bits_refs[step % 2][qb, index]
+            both = bits_refs[step][index]
             second = jnp.where(index * 2 + 1 < live, I32(-1), I32(0))
             work = []
             for part in range(2):
@@ -221,7 +232,7 @@
                 work.append((u, w, edge, q2, g2, scores, grad_prob))
             done = []
             for u, w, edge, q2, g2, scores, grad_prob in work:
-                lse_tile = lse_ref[qb, u]
+                lse_tile = lse_scr[qb, u]
                 delta_tile = delta_scr[qb, u]
                 probs, grads = [], []
                 for h in range(2):
@@ -340,34 +351,47 @@
 
     qg_shape = shape(2 * rows + PAD, LANES)
     kv_shape = shape(2, 2 * krows, LANES)
-    qg_own, qg_pair0, qg_pair1, kv_own, to_sibling, bits_own = pl.pallas_call(
-        functools.partial(pack_kernel, heads),
-        out_shape=(
-            qg_shape, qg_shape, qg_shape, shape(4 * krows, LANES),
-            shape(4 * krows + 2 * rows + PAD, LANES),
-            shape(capacity // 2 + 1, 8, LANES, dtype=I32),
-        ),
-        in_specs=[HBM] * 6 + [VMEM] * 2,
-        out_specs=(VMEM,) * 6,
+    slabs = capacity // 2 + 1
+    qg_own, qg_sibling, pair0, pair1 = pl.pallas_call(
+        functools.partial(pack_query_kernel, heads),
+        out_shape=(qg_shape,) * QUARTERS,
+        in_specs=[HBM] * 3,
+        out_specs=(VMEM,) * QUARTERS,
         scratch_shapes=[
             pltpu.VMEM(queries.shape, BF16),
             pltpu.VMEM(queries.shape, BF16),
             pltpu.VMEM(queries.shape, BF16),
+            pltpu.VMEM((QUARTERS, PAD, rows), BF16),
+            pltpu.SemaphoreType.DMA((3,)),
+        ],
+        compiler_params=PACK,
+        name="pack_query",
+    )(queries, grad_out, outputs)
+    pair0 = send(pair0, line, places, 2)
+    pair1 = send(pair1, line, places, 3)
+    qg_sibling = send(qg_sibling, "core", cores, 1)
+    kv_own, kv_sibling, bits_own, lse_own = pl.pallas_call(
+        functools.partial(pack_key_kernel, heads // QUARTERS),
+        out_shape=(
+            shape(4 * krows, LANES), shape(4 * krows, LANES),
+            shape(slabs + query_tiles // 4, 8, LANES, dtype=I32),
+            shape(query_tiles, 2, tile, dtype=F32),
+        ),
+        in_specs=[HBM] * 4 + [VMEM] * 2 + [HBM] * 3,
+        out_specs=(VMEM,) * 4,
+        scratch_shapes=[
             pltpu.VMEM(keys.shape, BF16),
             pltpu.VMEM(keys.shape, BF16),
             pltpu.VMEM(tile_bits.shape, I32),
-            pltpu.VMEM((QUARTERS, PAD, rows), BF16),
-            pltpu.SemaphoreType.DMA((6,)),
+            pltpu.VMEM(lse.shape, F32),
+            pltpu.SemaphoreType.DMA((4,)),
         ],
         compiler_params=PACK,
-        name="pack",
-    )(queries, grad_out, outputs, keys, values, tile_bits, tile_slot, tile_live)
-
-    qg_pair0 = send(qg_pair0, line, places, 2)
-    qg_pair1 = send(qg_pair1, line, places, 3)
-    from_sibling = send(to_sibling, "core", cores, 1)
+        name="pack_key",
+    )(keys, values, tile_bits, lse, tile_slot, tile_live, qg_sibling, pair0, pair1)
+    kv_sibling = send(kv_sibling, "core", cores, 1)
     bits_pair = send(bits_own, "row", row_count, 1)
-    lse_pair = send(lse, "row", row_count, 1)
+    bits = [bits_own, send(bits_own, "core", cores, 1), bits_pair, send(bits_pair, "core", cores, 1)]
     kv_same, kv_pair = pl.pallas_call(
         functools.partial(key_join_kernel, krows),
         out_shape=(kv_shape, kv_shape),
@@ -375,47 +399,40 @@
         out_specs=(VMEM,) * 2,
         compiler_params=SMALL,
         name="key_join",
-    )(kv_own, from_sibling)
+    )(kv_own, kv_sibling)
     kv_out = (kv_same, kv_pair)
-    kv = [kv_same] + [
-        send(kv_out[step % 2], "row", row_count, step) for step in range(1, row_count)
-    ]
-    qg, bits, lse2 = pl.pallas_call(
-        functools.partial(query_join_kernel, krows, tile),
-        out_shape=(
-            shape(QUARTERS, 2 * rows + PAD, LANES),
-            shape(2, capacity // 2 + 1, 8, LANES, dtype=I32),
-            shape(2, query_tiles, 2, tile, dtype=F32),
-        ),
-        in_specs=[VMEM] * 8,
-        out_specs=(VMEM,) * 3,
-        compiler_params=SMALL,
-        cost_estimate=early(20),
+    kv_far = pl.pallas_call(
+        far_join_kernel,
+        out_shape=shape(row_count - 2, 2, 2 * krows, LANES),
+        in_specs=[VMEM] * (row_count - 2),
+        out_specs=VMEM,
+        compiler_params=SMALL,
+        name="far_join",
+    )(*[send(kv_out[step % 2], "row", row_count, step) for step in range(2, row_count)])
+    kv_pair = send(kv_pair, "row", row_count, 1)
+    qg = pl.pallas_call(
+        query_join_kernel,
+        out_shape=shape(QUARTERS, 2 * rows + PAD, LANES),
+        in_specs=[VMEM] * QUARTERS,
+        out_specs=VMEM,
+        compiler_params=SMALL,
+        cost_estimate=early(60),
         name="query_join",
-    )(qg_own, from_sibling, qg_pair0, qg_pair1, bits_own, bits_pair, lse, lse_pair)
+    )(qg_own, qg_sibling, pair0, pair1)
     qg = [qg] + [send(qg, "chip", chips, step) for step in range(1, chips)]
-    bits_sibling = send(bits, "core", cores, 1)
-
-    placed = pl.pallas_call(
-        functools.partial(key_place_kernel, head_dim, tile),
-        out_shape=(
-            shape(2, key_tiles, tile, LANES), shape(2, key_tiles, tile, LANES),
-            shape(2, key_tiles, LANES, 2 * tile),
-        ),
-        in_specs=[VMEM] * row_count,
-        out_specs=(VMEM,) * 3,
-        compiler_params=SMALL,
-        cost_estimate=early(20),
-        name="key_place",
-    )(*kv)
+
     parts = pl.pallas_call(
         functools.partial(pair_kernel, (head_dim, tile, capacity, chips, row_count)),
         out_shape=(shape(2, query_tiles, LANES, tile),) + (kv_shape,) * row_count,
-        in_specs=[VMEM] * (chips + 6),
+        in_specs=[VMEM] * (chips + 4 + QUARTERS),
         out_specs=(VMEM,) * (1 + row_count),
         scratch_shapes=[
             pltpu.VMEM((2, query_tiles, 2, tile, LANES), BF16),
             pltpu.VMEM((2, query_tiles, 2, tile, LANES), BF16),
+            pltpu.VMEM((2, key_tiles, tile, LANES), BF16),
+            pltpu.VMEM((2, key_tiles, tile, LANES), BF16),
+            pltpu.VMEM((2, key_tiles, LANES, 2 * tile), BF16),
+            pltpu.VMEM((2, query_tiles, 2, tile), F32),
             pltpu.VMEM((2, query_tiles, PAD, tile), F32),
             pltpu.VMEM((2, query_tiles, LANES, tile), F32),
             pltpu.VMEM((2, key_tiles, tile, LANES), F32),
@@ -425,7 +442,7 @@
         ],
         compiler_params=MEDIUM,
         name="pair",
-    )(*qg, *placed, bits, bits_sibling, lse2)
+    )(*qg, kv_same, kv_pair, kv_far, *bits, lse_own)
 
     dkv = parts[1:]
     dq = pl.pallas_call(

time: 63.6 us -> 64.5 us (1.014)
  waiting for transfers between devices: 20.4 us -> 24.9 us
  Pallas kernels: 12.5 us -> 9.93 us
  local copies, waits for them, and re-layouts: 0.89 us -> 0.01 us
    ppermute x20 -> x21, waiting for transfers between devices: 20.4 us -> 24.9 us  [send(): lax.ppermute(block, axes, [(place, place ^ step) for place in range(count)])]
    pallas_call x1, Pallas kernels: 8.72 us -> 5.37 us  [body(): pl.pallas_call(functools.partial(pair_kernel, (head_dim, tile, capacity,...]
    unnamed x6, local copies, waits for them, and re-layouts: 0.89 us -> 0.01 us
    pallas_call x3 -> x4, Pallas kernels: 2.58 us -> 3.34 us  [the longest x1 1.81 us: body(): pl.pallas_call(functools.partial(pack_key_kernel, heads // QUARTERS), out...]
    ppermute x20 -> x21, starting transfers between devices: 27.7 us -> 27.8 us  [send(): lax.ppermute(block, axes, [(place, place ^ step) for place in range(count)])]
  transfers between devices with their start and end apart: 20 -> 21, of which waited for: 8 -> 10; matrix products, arithmetic and copies ran while one was open for 0% -> 0% of each run, Pallas kernels for 1% -> 0%
where the time goes in v4:
time: 64.5 us; the launch traced here: 64.1 us
  starting transfers between devices  27.8 us (43%)
  waiting for transfers between devices  24.9 us (39%)
  Pallas kernels  9.93 us (15%)
  between operations  1.4 us (2%)
    ppermute x21, starting transfers between devices, send(): lax.ppermute(block, axes, [(place, place ^ step) for place in range(count)])  27.8 us
    ppermute x21, waiting for transfers between devices, send(): lax.ppermute(block, axes, [(place, place ^ step) for place in range(count)])  24.9 us
    pallas_call x1, Pallas kernels, body(): pl.pallas_call(functools.partial(pair_kernel, (head_dim, tile, capacity,...  5.37 us
    pallas_call x1, Pallas kernels, body(): pl.pallas_call(functools.partial(pack_key_kernel, heads // QUARTERS), out...  1.81 us
    pallas_call x1, Pallas kernels, body(): pl.pallas_call(functools.partial(pack_query_kernel, heads), out_shape=(qg...  1.49 us
  transfers between devices with their start and end apart: 21, of which 10 were waited for; matrix products, arithmetic and copies ran while one was open for 0% of the time, Pallas kernels for 0%

profile of v4, /device:TPU:0, one launch (start us, length us, event | category | flops | bytes accessed | tf_op | source)
XLA Modules:
  0.0 64.1 jit_solution(16493083463940776008)
XLA Ops:
  0.6 0.0 copy-start.1
  0.6 1.5 %pack_query.1 = (bf16[272,128]{1,0:T(8,128)(2,1)S(1)}, bf16[272,128]{1,0:T(8,128)(2,1)S(1)}, bf16[272,128]{1,0:T(8,128)(2,1)S(1)}, bf16[272,128]{1,0:T(8,128)(2,1)S(1)}) custom-call(bf16[1,128,512]{2,1,0:T(8,128)(2,1)} %q_hbm.1, bf16[1,128,512]{2,1,0:T(8,128)(2,1)} %g_hbm.1, bf16[1,128,512]{2,1,0:T(8,128)(2,1)} %o_hbm.1), custom_call_target="tpu_custom_call" | custom-call | tf_op jit(solution)/shard_map/pack_query/pallas_call | solution.py:355
  2.1 0.5 collective-permute-start
  2.7 2.7 %collective-permute-start.1 = (bf16[272,128]{1,0:T(8,128)(2,1)S(1)}, bf16[272,128]{1,0:T(8,128)(2,1)S(1)}, u32[]{:S(2)}, u32[]{:S(2)}) collective-permute-start(bf16[272,128]{1,0:T(8,128)(2,1)S(1)} %get-tuple-element.28), channel_id=1, source_target_pairs={{0,8},{1,9},{8,0},{9,1},{16,24},{17,25},{24,16},{25,17},{2,10},{3,... | collective-permute-start | bytes 208904 | tf_op jit(solution)/shard_map/ppermute | solution.py:332
  5.3 0.0 copy-start.2
  5.3 0.1 collective-permute-start.2
  6.0 0.0 collective-permute-done.sib_ref._after0
  6.0 2.0 %collective-permute-done.1.pair0_ref._after1 = bf16[272,128]{1,0:T(8,128)(2,1)S(1)} collective-permute-done((bf16[272,128]{1,0:T(8,128)(2,1)S(1)}, bf16[272,128]{1,0:T(8,128)(2,1)S(1)}, u32[]{:S(2)}, u32[]{:S(2)}) %collective-permute-start.1) | collective-permute-done | bytes 69664 | tf_op jit(solution)/shard_map/ppermute | solution.py:332
  8.1 1.4 %collective-permute-done.2.pair1_ref._after2 = bf16[272,128]{1,0:T(8,128)(2,1)S(1)} collective-permute-done((bf16[272,128]{1,0:T(8,128)(2,1)S(1)}, bf16[272,128]{1,0:T(8,128)(2,1)S(1)}, u32[]{:S(2)}, u32[]{:S(2)}) %collective-permute-start.2) | collective-permute-done | bytes 69664 | tf_op jit(solution)/shard_map/ppermute | solution.py:332
  9.4 0.0 copy-done.1
  9.4 0.0 copy-done.2
  9.4 1.8 %pack_key.1 = (bf16[512,128]{1,0:T(8,128)(2,1)}, bf16[512,128]{1,0:T(8,128)(2,1)}, s32[15,8,128]{2,1,0:T(8,128)S(1)}, f32[8,2,128]{2,1,0:T(2,128)S(1)}) custom-call(bf16[1,128,512]{2,1,0:T(8,128)(2,1)} %k_hbm.1, bf16[1,128,512]{2,1,0:T(8,128)(2,1)} %v_hbm.1, s32[1,1,24,8,128]{4,3,2,1,0:T(8,128)} %bits_hbm.1, f32[1,8,1024]{2,1,0:T(8,128)S(1)} %copy-done.1, ...), custom_call_target="tpu_custom_call" | custom-call | tf_op jit(solution)/shard_map/pack_key/pallas_call | solution.py:373
  11.3 1.5 %collective-permute-start.11 = (s32[15,8,128]{2,1,0:T(8,128)S(1)}, s32[15,8,128]{2,1,0:T(8,128)S(1)}, u32[]{:S(2)}, u32[]{:S(2)}) collective-permute-start(s32[15,8,128]{2,1,0:T(8,128)S(1)} %get-tuple-element.34.refs_7_), channel_id=1, source_target_pairs={{0,8},{8,0},{16,24},{24,16},{1,9},{9,1},{17,25},{25,17},{2,10},{10... | collective-permute-start | bytes 184328 | tf_op jit(solution)/shard_map/ppermute | solution.py:332
  12.8 0.0 collective-permute-start.6
  12.8 0.0 copy-start
  12.8 2.5 %collective-permute-start.5 = (bf16[4,272,128]{2,1,0:T(8,128)(2,1)S(1)}, bf16[4,272,128]{2,1,0:T(8,128)(2,1)S(1)}, u32[]{:S(2)}, u32[]{:S(2)}) collective-permute-start(bf16[4,272,128]{2,1,0:T(8,128)(2,1)S(1)} %query_join.1.refs_0_), channel_id=1, source_target_pairs={{0,6},{2,4},{4,2},{6,0},{1,7},{3,5},{5,3},{7,1},{8,14},{10,12},{12... | collective-permute-start | bytes 835592 | tf_op jit(solution)/shard_map/ppermute | solution.py:332
  15.3 0.5 collective-permute-start.4
  15.8 0.5 collective-permute-start.3
  16.4 0.0 collective-permute-done.6.sib_ref
  16.4 0.0 copy-done
  16.4 2.7 %collective-permute-start.8 = (bf16[2,256,128]{2,1,0:T(8,128)(2,1)S(1)}, bf16[2,256,128]{2,1,0:T(8,128)(2,1)S(1)}, u32[]{:S(2)}, u32[]{:S(2)}) collective-permute-start(bf16[2,256,128]{2,1,0:T(8,128)(2,1)S(1)} %get-tuple-element.32.refs_4_), channel_id=1, source_target_pairs={{0,16},{8,24},{16,0},{24,8},{1,17},{9,25},{17,1},{25,9},{2,18},{10... | collective-permute-start | bytes 393224 | tf_op jit(solution)/shard_map/ppermute | solution.py:332
  19.0 0.0 collective-permute-done.11.refs_9_
  19.1 0.0 collective-permute-start.10
  19.1 1.2 %collective-permute-done.10.refs_8_ = s32[15,8,128]{2,1,0:T(8,128)S(1)} collective-permute-done((s32[15,8,128]{2,1,0:T(8,128)S(1)}, s32[15,8,128]{2,1,0:T(8,128)S(1)}, u32[]{:S(2)}, u32[]{:S(2)}) %collective-permute-start.10) | collective-permute-done | bytes 61472 | tf_op jit(solution)/shard_map/ppermute | solution.py:332
  20.3 0.4 collective-permute-start.9
  20.7 7.5 %collective-permute-done.8.refs_0_ = bf16[2,256,128]{2,1,0:T(8,128)(2,1)S(1)} collective-permute-done((bf16[2,256,128]{2,1,0:T(8,128)(2,1)S(1)}, bf16[2,256,128]{2,1,0:T(8,128)(2,1)S(1)}, u32[]{:S(2)}, u32[]{:S(2)}) %collective-permute-start.8) | collective-permute-done | bytes 131104 | tf_op jit(solution)/shard_map/ppermute | solution.py:332
  28.2 0.7 %collective-permute-start.7 = (bf16[2,256,128]{2,1,0:T(8,128)(2,1)S(1)}, bf16[2,256,128]{2,1,0:T(8,128)(2,1)S(1)}, u32[]{:S(2)}, u32[]{:S(2)}) collective-permute-start(bf16[2,256,128]{2,1,0:T(8,128)(2,1)S(1)} %get-tuple-element.33), channel_id=1, source_target_pairs={{0,8},{8,0},{16,24},{24,16},{1,9},{9,1},{17,25},{25,17},{2,10},{10... | collective-permute-start | bytes 393224 | tf_op jit(solution)/shard_map/ppermute | solution.py:332
  28.9 0.0 collective-permute-done.9.refs_1_
  28.9 0.0 collective-permute-start.12
  28.9 1.2 %collective-permute-done.12.refs_10_ = s32[15,8,128]{2,1,0:T(8,128)S(1)} collective-permute-done((s32[15,8,128]{2,1,0:T(8,128)S(1)}, s32[15,8,128]{2,1,0:T(8,128)S(1)}, u32[]{:S(2)}, u32[]{:S(2)}) %collective-permute-start.12) | collective-permute-done | bytes 61472 | tf_op jit(solution)/shard_map/ppermute | solution.py:332
  30.1 3.3 %collective-permute-done.7.refs_5_ = bf16[2,256,128]{2,1,0:T(8,128)(2,1)S(1)} collective-permute-done((bf16[2,256,128]{2,1,0:T(8,128)(2,1)S(1)}, bf16[2,256,128]{2,1,0:T(8,128)(2,1)S(1)}, u32[]{:S(2)}, u32[]{:S(2)}) %collective-permute-start.7) | collective-permute-done | bytes 131104 | tf_op jit(solution)/shard_map/ppermute | solution.py:332
  33.4 0.0 collective-permute-done.5.refs_3_
  33.4 0.0 collective-permute-done.4.refs_2_
  33.4 0.0 collective-permute-done.3.refs_1_
  33.4 5.4 %pair.1 = (bf16[2,8,128,128]{3,2,1,0:T(8,128)(2,1)S(1)}, bf16[2,256,128]{2,1,0:T(8,128)(2,1)S(1)}, bf16[2,256,128]{2,1,0:T(8,128)(2,1)S(1)}, bf16[2,256,128]{2,1,0:T(8,128)(2,1)S(1)}, bf16[2,256,128]{2,1,0:T(8,128)(2,1)S(1)}) custom-call(bf16[4,272,128]{2,1,0:T(8,128)(2,1)S(1)} %query_join.1.refs_0_, ...), custom_call_target="tpu_custom_call" | custom-call | tf_op jit(solution)/shard_map/pair/pallas_call | solution.py:424
  38.8 0.2 turn.1
  39.1 2.0 %collective-permute-start.16 = (bf16[4,128,128]{2,1,0:T(8,128)(2,1)S(1)}, bf16[4,128,128]{2,1,0:T(8,128)(2,1)S(1)}, u32[]{:S(2)}, u32[]{:S(2)}) collective-permute-start(bf16[4,128,128]{2,1,0:T(8,128)(2,1)S(1)} %get-tuple-element.43), channel_id=1, source_target_pairs={{0,2},{2,0},{4,6},{6,4},{1,3},{3,1},{5,7},{7,5},{8,10},{10,8},{12,... | collective-permute-start | bytes 393224 | tf_op jit(solution)/shard_map/ppermute | solution.py:332
  41.0 8.9 %collective-permute-start.17 = (bf16[4,128,128]{2,1,0:T(8,128)(2,1)S(1)}, bf16[4,128,128]{2,1,0:T(8,128)(2,1)S(1)}, u32[]{:S(2)}, u32[]{:S(2)}) collective-permute-start(bf16[4,128,128]{2,1,0:T(8,128)(2,1)S(1)} %get-tuple-element.44), channel_id=1, source_target_pairs={{0,4},{2,6},{4,0},{6,2},{1,5},{3,7},{5,1},{7,3},{8,12},{10,14},{12... | collective-permute-start | bytes 393224 | tf_op jit(solution)/shard_map/ppermute | solution.py:332
  50.0 0.0 collective-permute-start.18
  50.0 0.4 collective-permute-start.13
  50.4 0.0 collective-permute-start.14
  50.4 0.0 collective-permute-done.16.refs_1_
  50.4 4.0 %collective-permute-start.15 = (bf16[2,256,128]{2,1,0:T(8,128)(2,1)S(1)}, bf16[2,256,128]{2,1,0:T(8,128)(2,1)S(1)}, u32[]{:S(2)}, u32[]{:S(2)}) collective-permute-start(bf16[2,256,128]{2,1,0:T(8,128)(2,1)S(1)} %get-tuple-element.39), channel_id=1, source_target_pairs={{0,24},{8,16},{16,8},{24,0},{1,25},{9,17},{17,9},{25,1},{2,26},{10... | collective-permute-start | bytes 393224 | tf_op jit(solution)/shard_map/ppermute | solution.py:332
  54.4 0.0 collective-permute-done.17.refs_2_
  54.4 1.5 %collective-permute-done.18.refs_3_ = bf16[4,128,128]{2,1,0:T(8,128)(2,1)S(1)} collective-permute-done((bf16[4,128,128]{2,1,0:T(8,128)(2,1)S(1)}, bf16[4,128,128]{2,1,0:T(8,128)(2,1)S(1)}, u32[]{:S(2)}, u32[]{:S(2)}) %collective-permute-start.18) | collective-permute-done | bytes 131104 | tf_op jit(solution)/shard_map/ppermute | solution.py:332
  55.8 0.1 query_sum.1
  55.9 0.5 collective-permute-start.19
  56.4 0.4 collective-permute-done.13.refs_1_
  56.8 4.9 %collective-permute-done.14.refs_2_ = bf16[2,256,128]{2,1,0:T(8,128)(2,1)S(1)} collective-permute-done((bf16[2,256,128]{2,1,0:T(8,128)(2,1)S(1)}, bf16[2,256,128]{2,1,0:T(8,128)(2,1)S(1)}, u32[]{:S(2)}, u32[]{:S(2)}) %collective-permute-start.14) | collective-permute-done | bytes 131104 | tf_op jit(solution)/shard_map/ppermute | solution.py:332
  61.7 0.0 collective-permute-done.15.refs_3_
  61.7 0.1 key_sum.1
  61.7 0.0 collective-permute-done.19.dq_pair
  61.8 0.1 collective-permute-start.20
  61.9 1.4 %collective-permute-done.20.sib_ref = bf16[2,384,128]{2,1,0:T(8,128)(2,1)S(1)} collective-permute-done((bf16[2,384,128]{2,1,0:T(8,128)(2,1)S(1)}, bf16[2,384,128]{2,1,0:T(8,128)(2,1)S(1)}, u32[]{:S(2)}, u32[]{:S(2)}) %collective-permute-start.20) | collective-permute-done | bytes 196640 | tf_op jit(solution)/shard_map/ppermute | solution.py:332
  63.3 0.8 %finish.1 = (bf16[1,128,512]{2,1,0:T(8,128)(2,1)}, bf16[1,128,512]{2,1,0:T(8,128)(2,1)}, bf16[1,128,512]{2,1,0:T(8,128)(2,1)}) custom-call(bf16[2,256,128]{2,1,0:T(8,128)(2,1)S(1)} %get-tuple-element.40.dkv_own, bf16[2,128,128]{2,1,0:T(8,128)(2,1)S(1)} %get-tuple-element.46.dq_same, bf16[2,128,128]{2,1,0:T(8,128)(2,1)S(1)} %collective-permute-done.19.dq_pair, ...), custom_call_target="tpu_custom_call" | custom-call | tf_op jit(solution)/shard_map/finish/pallas_call | solution.py:486
  (4 shorter events, 0.1 us)
Async XLA Ops:
  0.6 8.8 %copy-start.1 = (f32[1,8,1024]{2,1,0:T(8,128)S(1)}, f32[1,8,1024]{2,1,0:T(8,128)}, u32[]{:S(2)}) copy-start(f32[1,8,1024]{2,1,0:T(8,128)} %lse_hbm.1) | copy-start | bytes 98308
  2.1 3.9 %collective-permute-start = (bf16[272,128]{1,0:T(8,128)(2,1)S(1)}, bf16[272,128]{1,0:T(8,128)(2,1)S(1)}, u32[]{:S(2)}, u32[]{:S(2)}) collective-permute-start(bf16[272,128]{1,0:T(8,128)(2,1)S(1)} %get-tuple-element.27), channel_id=1, source_target_pairs={{0,1},{1,0},{2,3},{3,2},{4,5},{5,4},{6,7},{7,6},{8,9},{9,8},{10,11... | collective-permute-start | bytes 208904 | tf_op jit(solution)/shard_map/ppermute | solution.py:332
  2.7 5.4 %collective-permute-start.1 = (bf16[272,128]{1,0:T(8,128)(2,1)S(1)}, bf16[272,128]{1,0:T(8,128)(2,1)S(1)}, u32[]{:S(2)}, u32[]{:S(2)}) collective-permute-start(bf16[272,128]{1,0:T(8,128)(2,1)S(1)} %get-tuple-element.28), channel_id=1, source_target_pairs={{0,8},{1,9},{8,0},{9,1},{16,24},{17,25},{24,16},{25,17},{2,10},{3,... | collective-permute-start | bytes 208904 | tf_op jit(solution)/shard_map/ppermute | solution.py:332
  5.3 4.1 %copy-start.2 = (s32[1,1,24]{2,1,0:T(1,128)S(1)}, s32[1,1,24]{2,1,0:T(1,128)}, u32[]{:S(2)}) copy-start(s32[1,1,24]{2,1,0:T(1,128)} %slot_ref.1) | copy-start | bytes 292
  5.3 4.1 %collective-permute-start.2 = (bf16[272,128]{1,0:T(8,128)(2,1)S(1)}, bf16[272,128]{1,0:T(8,128)(2,1)S(1)}, u32[]{:S(2)}, u32[]{:S(2)}) collective-permute-start(bf16[272,128]{1,0:T(8,128)(2,1)S(1)} %get-tuple-element.29), channel_id=1, source_target_pairs={{0,9},{1,8},{8,1},{9,0},{16,25},{17,24},{24,17},{25,16},{2,11},{3,... | collective-permute-start | bytes 208904 | tf_op jit(solution)/shard_map/ppermute | solution.py:332
  11.3 7.8 %collective-permute-start.11 = (s32[15,8,128]{2,1,0:T(8,128)S(1)}, s32[15,8,128]{2,1,0:T(8,128)S(1)}, u32[]{:S(2)}, u32[]{:S(2)}) collective-permute-start(s32[15,8,128]{2,1,0:T(8,128)S(1)} %get-tuple-element.34.refs_7_), channel_id=1, source_target_pairs={{0,8},{8,0},{16,24},{24,16},{1,9},{9,1},{17,25},{25,17},{2,10},{10... | collective-permute-start | bytes 184328 | tf_op jit(solution)/shard_map/ppermute | solution.py:332
  12.8 3.6 %collective-permute-start.6 = (bf16[512,128]{1,0:T(8,128)(2,1)}, bf16[512,128]{1,0:T(8,128)(2,1)S(1)}, u32[]{:S(2)}, u32[]{:S(2)}) collective-permute-start(bf16[512,128]{1,0:T(8,128)(2,1)} %get-tuple-element.31), channel_id=1, source_target_pairs={{0,1},{1,0},{2,3},{3,2},{4,5},{5,4},{6,7},{7,6},{8,9},{9,8},{10,11... | collective-permute-start | bytes 393224 | tf_op jit(solution)/shard_map/ppermute | solution.py:332
  12.8 3.6 %copy-start = (bf16[512,128]{1,0:T(8,128)(2,1)S(1)}, bf16[512,128]{1,0:T(8,128)(2,1)}, u32[]{:S(2)}) copy-start(bf16[512,128]{1,0:T(8,128)(2,1)} %get-tuple-element.30.kv_own) | copy-start | bytes 393220
  12.8 20.6 %collective-permute-start.5 = (bf16[4,272,128]{2,1,0:T(8,128)(2,1)S(1)}, bf16[4,272,128]{2,1,0:T(8,128)(2,1)S(1)}, u32[]{:S(2)}, u32[]{:S(2)}) collective-permute-start(bf16[4,272,128]{2,1,0:T(8,128)(2,1)S(1)} %query_join.1.refs_0_), channel_id=1, source_target_pairs={{0,6},{2,4},{4,2},{6,0},{1,7},{3,5},{5,3},{7,1},{8,14},{10,12},{12... | collective-permute-start | bytes 835592 | tf_op jit(solution)/shard_map/ppermute | solution.py:332
  15.3 18.1 %collective-permute-start.4 = (bf16[4,272,128]{2,1,0:T(8,128)(2,1)S(1)}, bf16[4,272,128]{2,1,0:T(8,128)(2,1)S(1)}, u32[]{:S(2)}, u32[]{:S(2)}) collective-permute-start(bf16[4,272,128]{2,1,0:T(8,128)(2,1)S(1)} %query_join.1.refs_0_), channel_id=1, source_target_pairs={{0,4},{2,6},{4,0},{6,2},{1,5},{3,7},{5,1},{7,3},{8,12},{10,14},{12... | collective-permute-start | bytes 835592 | tf_op jit(solution)/shard_map/ppermute | solution.py:332
  15.8 17.6 %collective-permute-start.3 = (bf16[4,272,128]{2,1,0:T(8,128)(2,1)S(1)}, bf16[4,272,128]{2,1,0:T(8,128)(2,1)S(1)}, u32[]{:S(2)}, u32[]{:S(2)}) collective-permute-start(bf16[4,272,128]{2,1,0:T(8,128)(2,1)S(1)} %query_join.1.refs_0_), channel_id=1, source_target_pairs={{0,2},{2,0},{4,6},{6,4},{1,3},{3,1},{5,7},{7,5},{8,10},{10,8},{12,... | collective-permute-start | bytes 835592 | tf_op jit(solution)/shard_map/ppermute | solution.py:332
  16.4 11.8 %collective-permute-start.8 = (bf16[2,256,128]{2,1,0:T(8,128)(2,1)S(1)}, bf16[2,256,128]{2,1,0:T(8,128)(2,1)S(1)}, u32[]{:S(2)}, u32[]{:S(2)}) collective-permute-start(bf16[2,256,128]{2,1,0:T(8,128)(2,1)S(1)} %get-tuple-element.32.refs_4_), channel_id=1, source_target_pairs={{0,16},{8,24},{16,0},{24,8},{1,17},{9,25},{17,1},{25,9},{2,18},{10... | collective-permute-start | bytes 393224 | tf_op jit(solution)/shard_map/ppermute | solution.py:332
  19.1 1.2 %collective-permute-start.10 = (s32[15,8,128]{2,1,0:T(8,128)S(1)}, s32[15,8,128]{2,1,0:T(8,128)S(1)}, u32[]{:S(2)}, u32[]{:S(2)}) collective-permute-start(s32[15,8,128]{2,1,0:T(8,128)S(1)} %get-tuple-element.34.refs_7_), channel_id=1, source_target_pairs={{0,1},{1,0},{2,3},{3,2},{4,5},{5,4},{6,7},{7,6},{8,9},{9,8},{10,11... | collective-permute-start | bytes 184328 | tf_op jit(solution)/shard_map/ppermute | solution.py:332
  20.3 8.6 %collective-permute-start.9 = (bf16[2,256,128]{2,1,0:T(8,128)(2,1)S(1)}, bf16[2,256,128]{2,1,0:T(8,128)(2,1)S(1)}, u32[]{:S(2)}, u32[]{:S(2)}) collective-permute-start(bf16[2,256,128]{2,1,0:T(8,128)(2,1)S(1)} %get-tuple-element.33), channel_id=1, source_target_pairs={{0,24},{8,16},{16,8},{24,0},{1,25},{9,17},{17,9},{25,1},{2,26},{10... | collective-permute-start | bytes 393224 | tf_op jit(solution)/shard_map/ppermute | solution.py:332
  28.2 5.3 %collective-permute-start.7 = (bf16[2,256,128]{2,1,0:T(8,128)(2,1)S(1)}, bf16[2,256,128]{2,1,0:T(8,128)(2,1)S(1)}, u32[]{:S(2)}, u32[]{:S(2)}) collective-permute-start(bf16[2,256,128]{2,1,0:T(8,128)(2,1)S(1)} %get-tuple-element.33), channel_id=1, source_target_pairs={{0,8},{8,0},{16,24},{24,16},{1,9},{9,1},{17,25},{25,17},{2,10},{10... | collective-permute-start | bytes 393224 | tf_op jit(solution)/shard_map/ppermute | solution.py:332
  28.9 1.2 %collective-permute-start.12 = (s32[15,8,128]{2,1,0:T(8,128)S(1)}, s32[15,8,128]{2,1,0:T(8,128)S(1)}, u32[]{:S(2)}, u32[]{:S(2)}) collective-permute-start(s32[15,8,128]{2,1,0:T(8,128)S(1)} %collective-permute-done.11.refs_9_), channel_id=1, source_target_pairs={{0,1},{1,0},{2,3},{3,2},{4,5},{5,4},{6,7},{7,6},{8,9},{9,8},{10,11... | collective-permute-start | bytes 184328 | tf_op jit(solution)/shard_map/ppermute | solution.py:332
  39.1 11.3 %collective-permute-start.16 = (bf16[4,128,128]{2,1,0:T(8,128)(2,1)S(1)}, bf16[4,128,128]{2,1,0:T(8,128)(2,1)S(1)}, u32[]{:S(2)}, u32[]{:S(2)}) collective-permute-start(bf16[4,128,128]{2,1,0:T(8,128)(2,1)S(1)} %get-tuple-element.43), channel_id=1, source_target_pairs={{0,2},{2,0},{4,6},{6,4},{1,3},{3,1},{5,7},{7,5},{8,10},{10,8},{12,... | collective-permute-start | bytes 393224 | tf_op jit(solution)/shard_map/ppermute | solution.py:332
  41.0 13.3 %collective-permute-start.17 = (bf16[4,128,128]{2,1,0:T(8,128)(2,1)S(1)}, bf16[4,128,128]{2,1,0:T(8,128)(2,1)S(1)}, u32[]{:S(2)}, u32[]{:S(2)}) collective-permute-start(bf16[4,128,128]{2,1,0:T(8,128)(2,1)S(1)} %get-tuple-element.44), channel_id=1, source_target_pairs={{0,4},{2,6},{4,0},{6,2},{1,5},{3,7},{5,1},{7,3},{8,12},{10,14},{12... | collective-permute-start | bytes 393224 | tf_op jit(solution)/shard_map/ppermute | solution.py:332
  50.0 5.9 %collective-permute-start.18 = (bf16[4,128,128]{2,1,0:T(8,128)(2,1)S(1)}, bf16[4,128,128]{2,1,0:T(8,128)(2,1)S(1)}, u32[]{:S(2)}, u32[]{:S(2)}) collective-permute-start(bf16[4,128,128]{2,1,0:T(8,128)(2,1)S(1)} %get-tuple-element.45), channel_id=1, source_target_pairs={{0,6},{2,4},{4,2},{6,0},{1,7},{3,5},{5,3},{7,1},{8,14},{10,12},{12... | collective-permute-start | bytes 393224 | tf_op jit(solution)/shard_map/ppermute | solution.py:332
  50.0 6.8 %collective-permute-start.13 = (bf16[2,256,128]{2,1,0:T(8,128)(2,1)S(1)}, bf16[2,256,128]{2,1,0:T(8,128)(2,1)S(1)}, u32[]{:S(2)}, u32[]{:S(2)}) collective-permute-start(bf16[2,256,128]{2,1,0:T(8,128)(2,1)S(1)} %get-tuple-element.37), channel_id=1, source_target_pairs={{0,8},{8,0},{16,24},{24,16},{1,9},{9,1},{17,25},{25,17},{2,10},{10... | collective-permute-start | bytes 393224 | tf_op jit(solution)/shard_map/ppermute | solution.py:332
  50.4 11.3 %collective-permute-start.14 = (bf16[2,256,128]{2,1,0:T(8,128)(2,1)S(1)}, bf16[2,256,128]{2,1,0:T(8,128)(2,1)S(1)}, u32[]{:S(2)}, u32[]{:S(2)}) collective-permute-start(bf16[2,256,128]{2,1,0:T(8,128)(2,1)S(1)} %get-tuple-element.38), channel_id=1, source_target_pairs={{0,16},{8,24},{16,0},{24,8},{1,17},{9,25},{17,1},{25,9},{2,18},{10... | collective-permute-start | bytes 393224 | tf_op jit(solution)/shard_map/ppermute | solution.py:332
  50.4 11.3 %collective-permute-start.15 = (bf16[2,256,128]{2,1,0:T(8,128)(2,1)S(1)}, bf16[2,256,128]{2,1,0:T(8,128)(2,1)S(1)}, u32[]{:S(2)}, u32[]{:S(2)}) collective-permute-start(bf16[2,256,128]{2,1,0:T(8,128)(2,1)S(1)} %get-tuple-element.39), channel_id=1, source_target_pairs={{0,24},{8,16},{16,8},{24,0},{1,25},{9,17},{17,9},{25,1},{2,26},{10... | collective-permute-start | bytes 393224 | tf_op jit(solution)/shard_map/ppermute | solution.py:332
  55.9 5.8 %collective-permute-start.19 = (bf16[2,128,128]{2,1,0:T(8,128)(2,1)S(1)}, bf16[2,128,128]{2,1,0:T(8,128)(2,1)S(1)}, u32[]{:S(2)}, u32[]{:S(2)}) collective-permute-start(bf16[2,128,128]{2,1,0:T(8,128)(2,1)S(1)} %get-tuple-element.47), channel_id=1, source_target_pairs={{0,8},{8,0},{16,24},{24,16},{1,9},{9,1},{17,25},{25,17},{2,10},{10... | collective-permute-start | bytes 196616 | tf_op jit(solution)/shard_map/ppermute | solution.py:332
  61.8 1.5 %collective-permute-start.20 = (bf16[2,384,128]{2,1,0:T(8,128)(2,1)S(1)}, bf16[2,384,128]{2,1,0:T(8,128)(2,1)S(1)}, u32[]{:S(2)}, u32[]{:S(2)}) collective-permute-start(bf16[2,384,128]{2,1,0:T(8,128)(2,1)S(1)} %bundle.1), channel_id=1, source_target_pairs={{0,1},{1,0},{2,3},{3,2},{4,5},{5,4},{6,7},{7,6},{8,9},{9,8},{10,11... | collective-permute-start | bytes 589832 | tf_op jit(solution)/shard_map/ppermute | solution.py:332
